TPU v7x, 128 devices: a whole 4x4x4 slice. The times are simulated.
128 devices in a mesh: expert: 8 (over y, core), shard: 16 (over z, x).
Axes of the slice: x: 4, y: 4, z: 4, core: 2. Of those that a mesh axis runs over, the one named last changes fastest.
Arguments:
- slot_inputs: bfloat16 [32768, 4096], P(('expert', 'shard')), may hold values from -6 to 6
- slot_grads: bfloat16 [32768, 8192], P(('expert', 'shard')), may hold values from -6 to 6
- slot_expert: int32 [32768, 1], P(('expert', 'shard')), may hold values from 0 to 7; in each aligned block of 256 rows (0 to 255, 256 to 511, ...) at most 64 rows name the same one
- weight_grad: bfloat16 [8, 4096, 8192], P('expert', None, 'shard'), may hold values from -6 to 6
Outputs:
- preconditioned: bfloat16 [8, 4096, 8192], P('expert', None, 'shard')
Inputs may be any that keep to these rules, and one draw needn't show every extreme that they name: `slot_expert`: among the slots of one device no expert appears more than 64 times, and some expert appears exactly 64 times on some device; every expert appears somewhere.
All inputs are finite; a program needn't handle non-finite values.
Results may differ from a plain program's by a relative error of at most 0.01.
Values may be sent and summed in bfloat16 or wider, within the bound.
No kernel may reach another device: no remote copies, remote signals or barrier semaphores. Data moves between devices by JAX's collectives and lax.ppermute only.
A program may use at most 128 MiB of HBM per device.

v0:
```python
import jax
import jax.numpy as jnp
from jax import lax
from jax.sharding import PartitionSpec as P

D = 4096
FF = 8192
BLK = 512
NS_STEPS = 8


DAMPING = 0.1
PRECISE = lax.Precision.HIGHEST


def partner_2(block, axis, distance):
    count = lax.axis_size(axis)
    route = []
    for low in range(count):
        high = low | 1 << distance
        if high != low and high < count:
            route += [(low, high), (high, low)]
    return lax.ppermute(block, axis, route)


def slot_sources(route_ids, experts, capacity, slot_count):
    labels = jnp.arange(experts, dtype=jnp.int32)
    onehot = (route_ids[:, None] == labels[None, :]).astype(jnp.int32)
    before = jnp.cumsum(onehot, axis=0) - onehot
    placed = route_ids * capacity + jnp.sum(before * onehot, axis=1)
    target = jnp.arange(experts * capacity, dtype=jnp.int32)
    matched = (placed[None, :] == target[:, None]).astype(jnp.int32)
    source = jnp.sum(matched * jnp.arange(slot_count, dtype=jnp.int32)[None, :], axis=1)
    return (source, jnp.sum(matched, axis=1), jnp.sum(onehot, axis=0))


def newton_whole(matrix):
    extent = matrix.shape[-1]
    norm_value = jnp.sqrt(jnp.sum(matrix * matrix, axis=(-2, -1), keepdims=True))
    iterate = jnp.eye(extent, dtype=jnp.float32) / norm_value
    for step_index in range(NS_STEPS):
        product = jnp.matmul(
            jnp.matmul(iterate, matrix, precision=PRECISE), iterate, precision=PRECISE
        )
        iterate = 2.0 * iterate - product
    return iterate


def per_device(slot_inputs, slot_grads, slot_expert, weight_grad):
    experts = lax.axis_size("expert")
    shards = lax.axis_size("shard")
    shard_pos = lax.axis_index("shard")
    group_pos = lax.axis_index("expert")
    slot_count = slot_inputs.shape[0]
    capacity = 2 * slot_count // experts
    source, filled, local_counts = slot_sources(slot_expert[:, 0], experts, capacity, slot_count)
    keep_mask = filled.astype(jnp.bfloat16)[:, None]
    sent_inputs = (jnp.take(slot_inputs, source, axis=0) * keep_mask).reshape(experts, capacity, D)
    sent_grads = (jnp.take(slot_grads, source, axis=0) * keep_mask).reshape(experts, capacity, FF)
    totals = lax.psum(local_counts.astype(jnp.float32), ("expert", "shard"))
    routed = jnp.sum(jnp.where(jnp.arange(experts, dtype=jnp.int32) == group_pos, totals, 0.0))
    got_inputs, got_grads = (
        lax.all_to_all(sent_inputs, "expert", split_axis=0, concat_axis=0, tiled=True),
        lax.all_to_all(sent_grads, "expert", split_axis=0, concat_axis=0, tiled=True),
    )
    rows_total = experts * capacity
    got_inputs = got_inputs.reshape(rows_total, D)
    got_grads = got_grads.reshape(rows_total, FF)
    slab_rows = D // shards
    spread = BLK // slab_rows
    own_blocks = FF // (BLK * shards)
    split_in = got_inputs.reshape(rows_total, D // BLK, BLK)
    part_act = jnp.einsum(
        "rbi,rbj->bij", split_in, split_in, preferred_element_type=jnp.float32
    ).reshape(D, BLK)
    split_grad = got_grads.reshape(rows_total, FF // BLK, BLK)
    part_out = jnp.einsum(
        "rbi,rbj->bij", split_grad, split_grad, preferred_element_type=jnp.float32
    ).reshape(FF, BLK)
    act_gram, out_rows = (
        lax.psum_scatter(part_act, "shard", scatter_dimension=0, tiled=True),
        lax.psum_scatter(part_out, "shard", scatter_dimension=0, tiled=True),
    )
    partner = partner_2(act_gram.astype(jnp.bfloat16), "shard", 0).astype(act_gram.dtype)
    lower_half = shard_pos >> 0 & 1 == 0
    act_gram = jnp.where(
        lower_half, jnp.concatenate([act_gram, partner], 0), jnp.concatenate([partner, act_gram], 0)
    )
    out_gram = out_rows.reshape(own_blocks, BLK, BLK)
    identity = jnp.eye(BLK, dtype=jnp.float32)
    act_matrix = act_gram / routed + DAMPING * identity
    out_matrix = out_gram / routed + DAMPING * identity
    out_inverse = newton_whole(out_matrix).astype(jnp.bfloat16)
    offset = shard_pos % spread * slab_rows
    full_inverse = newton_whole(act_matrix)
    act_rows_inv = lax.dynamic_slice_in_dim(full_inverse, offset, slab_rows, 0)
    act_inverse = lax.all_gather(act_rows_inv.astype(jnp.bfloat16), "shard", axis=0, tiled=True)
    local_grad = weight_grad[0].reshape(D, own_blocks, BLK)
    halfway = jnp.einsum(
        "dgi,gij->dgj", local_grad, out_inverse, preferred_element_type=jnp.float32
    ).astype(jnp.bfloat16)
    halfway = halfway.reshape(D // BLK, BLK, own_blocks * BLK)
    result = jnp.einsum(
        "bij,bjc->bic",
        act_inverse.reshape(D // BLK, BLK, BLK),
        halfway,
        preferred_element_type=jnp.float32,
    )
    return result.reshape(1, D, own_blocks * BLK).astype(jnp.bfloat16)


def solution(mesh):
    in_specs = (
        P(("expert", "shard"), None),
        P(("expert", "shard"), None),
        P(("expert", "shard"), None),
        P("expert", None, "shard"),
    )
    out_specs = P("expert", None, "shard")
    return jax.shard_map(
        per_device, mesh=mesh, in_specs=in_specs, out_specs=out_specs, check_vma=False
    )
```

profile of v0, /device:TPU:24, one launch (start us, length us, event | category | flops | bytes accessed | tf_op | source)
XLA Modules:
  0.0 483.4 jit_solution(3390052568376372741)
XLA Ops:
  10.2 4.4 gather_fusion
  14.6 2.7 select_multiply_fusion.1
  17.3 52.7 %all_to_all.10 = bf16[8,64,4096]{2,1,0:T(8,128)(2,1)S(1)} all-to-all(bf16[8,64,4096]{2,1,0:T(8,128)(2,1)S(1)} %select_multiply_fusion.1), channel_id=1, replica_groups=mesh['expert'=8,'shard'=16] {'expert'}, dimensions={0} | all-to-all | bytes 8388608 | tf_op jit(solution)/shard_map/all_to_all | solution.py:63
  72.2 9.0 %fusion.4 = f32[8,512,512]{2,1,0:T(8,128)} fusion(bf16[512,8,512]{2,1,0:T(8,128)(2,1)S(1)} %bitcast.80), kind=kOutput, calls=%fused_computation.8 | convolution fusion | flops 2147483648 | bytes 12582912 | tf_op jit(solution)/shard_map/rbi,rbj->bij/dot_general | solution.py:73
  81.8 18.2 %gather_fusion.1 = bf16[512,8192]{1,0:T(8,128)(2,1)} fusion(bf16[256,8192]{1,0:T(8,128)(2,1)} %param.5, s32[1024]{0:T(1024)S(1)} %pad_clamp_fusion), kind=kCustom, calls=%fused_computation.1 | custom fusion | bytes 16779264 | tf_op jit(solution)/shard_map/jit(_take)/gather | solution.py:59
  100.0 7.5 %select_multiply_fusion = bf16[8,64,8192]{2,1,0:T(8,128)(2,1)} fusion(bf16[8,64,8192]{2,1,0:T(8,128)(2,1)} %bitcast.79, pred[8,64]{1,0:T(8,128)(4,1)S(1)} %compare_and_fusion, bf16[8,64]{1,0:T(8,128)(2,1)S(1)} %convert_element_type.68), kind=kLoop, calls=%fused_computation.4 | loop fusion | flops 8388608 | bytes 16778752 | tf_op jit(solution)/shard_map/mul | solution.py:59
  107.4 101.9 %all_to_all.11 = bf16[8,64,8192]{2,1,0:T(8,128)(2,1)} all-to-all(bf16[8,64,8192]{2,1,0:T(8,128)(2,1)} %select_multiply_fusion), channel_id=1, replica_groups=mesh['expert'=8,'shard'=16] {'expert'}, dimensions={0} | all-to-all | bytes 16777216 | tf_op jit(solution)/shard_map/all_to_all | solution.py:64
  209.3 11.0 %copy.20 = bf16[64,8,16,512]{3,2,1,0:T(8,128)(2,1)} copy(bf16[64,8,16,512]{3,1,2,0:T(8,128)(2,1)} %bitcast.78) | data formatting | bytes 16777216
  220.3 40.6 %fusion = f32[16,512,512]{2,1,0:T(8,128)} fusion(bf16[512,16,512]{2,1,0:T(8,128)(2,1)} %bitcast.77), kind=kOutput, calls=%fused_computation.2 | convolution fusion | flops 4294967296 | bytes 25165824 | tf_op jit(solution)/shard_map/rbi,rbj->bij/dot_general | solution.py:77
  263.7 69.4 %psum.7 = f32[8]{0:T(128)S(1)} all-reduce(f32[8]{0:T(128)S(1)} %convert_element_type.71), channel_id=1, replica_groups=mesh['expert'=8,'shard'=16] {'expert','shard'}, use_global_device_ids=true, to_apply=%region_7.8 | all-reduce | flops 8 | bytes 64 | tf_op jit(solution)/shard_map/psum | solution.py:60
  333.8 41.7 %reduce-scatter.5.cloned.1.call-done = f32[512,512]{1,0:T(8,128)} async-done(((f32[8192,512]{1,0:T(8,128)}), f32[512,512]{1,0:T(8,128)}) %reduce-scatter.5.cloned.1.call-update) | async-done | bytes 1048592 | tf_op jit(solution)/shard_map/reduce_scatter | solution.py:82
  375.5 3.1 multiply_reduce_fusion
  379.3 3.8 fusion.12
  385.0 2.6 fusion.52
  389.4 2.6 fusion.51
  393.9 2.8 fusion.50
  398.5 2.6 fusion.49
  412.2 2.6 fusion.46
  426.8 3.0 fusion.44
  449.5 2.7 fusion.39
  454.1 4.4 fusion.2
  458.5 6.5 %copy.18 = bf16[4096,1,512]{2,0,1:T(8,128)(2,1)} copy(bf16[4096,1,512]{0,2,1:T(8,128)(2,1)} %fusion.2) | data formatting | bytes 8388608 | tf_op jit(solution)/shard_map/reshape | solution.py:102
  465.0 3.6 all-gather.2.cloned.1.call-done
  468.7 8.0 %convolution_convert_fusion.1 = bf16[8,512,512]{2,1,0:T(8,128)(2,1)} fusion(bf16[8,512,512]{2,1,0:T(8,128)(2,1)} %bitcast.89, bf16[8,512,512]{2,1,0:T(8,128)(2,1)} %bitcast.83), kind=kOutput, calls=%fused_computation.11 | convolution fusion | flops 2149580800 | bytes 12582912 | tf_op jit(solution)/shard_map/bij,bjc->bic/dot_general | solution.py:103
  (63 shorter events, 60.9 us)
Async XLA Ops:
  6.5 3.7 copy-start
  6.5 254.5 %reduce-scatter.3.cloned.1.call-start = ((), (), s32[]{:S(2)}) async-start(), calls=%async_computation.4 | async-start | bytes 8912896 | tf_op jit(solution)/shard_map/reduce_scatter | solution.py:81
  81.2 294.2 %reduce-scatter.5.cloned.1.call-start = ((), (), s32[]{:S(2)}) async-start(), calls=%async_computation.6 | async-start | bytes 17825792 | tf_op jit(solution)/shard_map/reduce_scatter | solution.py:82
  261.0 207.7 %all-gather.2.cloned.1.call-start = ((), (), s32[]{:S(2)}) async-start(), calls=%async_computation.5 | async-start | bytes 4456448 | tf_op jit(solution)/shard_map/all_gather | solution.py:97
  262.1 71.6 %collective-permute-start = (bf16[256,512]{1,0:T(8,128)(2,1)S(1)}, bf16[256,512]{1,0:T(8,128)(2,1)S(1)}, u32[]{:S(2)}, u32[]{:S(2)}) collective-permute-start(bf16[256,512]{1,0:T(8,128)(2,1)S(1)} %convert_element_type.69), channel_id=1, source_target_pairs={{0,1},{1,0},{2,3},{3,2},{4,5},{5,4},{6,7},{7,6},{8,9},{9,8},{10,11... | collective-permute-start | bytes 786440 | tf_op jit(solution)/shard_map/ppermute | solution.py:23
  379.3 5.6 %copy-start.2 = (f32[256,512]{1,0:T(8,128)S(1)}, f32[256,512]{1,0:T(8,128)}, u32[]{:S(2)}) copy-start(f32[256,512]{1,0:T(8,128)} %reduce-scatter.3.cloned.1.call-done) | copy-start | bytes 1572868
  414.8 3.4 copy-start.3
  449.5 4.6 copy-start.4
  468.7 8.0 %copy-start.1 = (bf16[256,4096]{1,0:T(8,128)(2,1)S(1)}, bf16[256,4096]{1,0:T(8,128)(2,1)}, u32[]{:S(2)}) copy-start(bf16[256,4096]{1,0:T(8,128)(2,1)} %param.4) | copy-start | bytes 6291460
Sparse Core Ops, SparseCore 0:
  81.4 86.9 reduce-scatter.2
  261.1 114.2 reduce-scatter.4
  417.6 51.0 all-gather.1
where the time goes:
time: 493 us; the launch traced here: 483 us
  blocking collectives  224 us (45%)
  matrix products  135 us (27%)
  waiting for transfers between devices  45.4 us (9%)
  local copies, waits for them, and re-layouts  42.8 us (9%)
  other arithmetic  19.1 us (4%)
  between operations  15.1 us (3%)
    all_to_all x1, blocking collectives, per_device(): lax.all_to_all(sent_grads, 'expert', split_axis=0, concat_axis=0, tiled=T...  102 us
    psum x1, blocking collectives, per_device(): totals = lax.psum(local_counts.astype(jnp.float32), ('expert', 'shard'))  69.4 us
    all_to_all x1, blocking collectives, per_device(): lax.all_to_all(sent_inputs, 'expert', split_axis=0, concat_axis=0, tiled=...  52.7 us
    dot_general x16, matrix products, newton_whole(): jnp.matmul(iterate, matrix, precision=PRECISE)  43 us
    reduce_scatter x1, waiting for transfers between devices, per_device(): lax.psum_scatter(part_out, 'shard', scatter_dimension=0, tiled=True)  41.7 us
    dot_general x1, matrix products, per_device(): jnp.einsum('rbi,rbj->bij', split_grad, split_grad, preferred_element_type...  40.6 us
    dot_general x16, matrix products, newton_whole(): jnp.matmul(jnp.matmul(iterate, matrix, precision=PRECISE), iterate, preci...  29.9 us
    gather x1, local copies, waits for them, and re-layouts, per_device(): jnp.take(slot_grads, source, axis=0) * keep_mask  18.2 us
  transfers between devices with their start and end apart: 4, of which 2 were waited for; matrix products, arithmetic and copies ran while one was open for 26% of the time, Pallas kernels for 0%

commit v1 on v0

v1 whole, which is shorter than its diff:
```python
import jax
import jax.numpy as jnp
from jax import lax
from jax.experimental import pallas as pl
from jax.experimental.pallas import tpu as pltpu
from jax.sharding import PartitionSpec as P

D = 4096
FF = 8192
BLK = 512
HALF = 256
TILE = 128
EXPERTS = 8
SLOT_DEV = 256
NS_STEPS = 8
DAMPING = 0.1
VMEM_LIMIT = 40 * 1024 * 1024

TILES = [(i, j) for i in range(4) for j in range(i, 4)]
PACKED = len(TILES) * TILE


def params():
    return pltpu.CompilerParams(vmem_limit_bytes=VMEM_LIMIT)


def route_kernel(interleave, col_ref, row_ref, x_ref, o_ref, perm):
    @pl.when(pl.program_id(0) == 0)
    def _():
        n = SLOT_DEV
        sub = lax.broadcasted_iota(jnp.int32, (n, n), 0)
        lane = lax.broadcasted_iota(jnp.int32, (n, n), 1)
        earlier = col_ref[...] * n + sub < row_ref[...] * n + lane
        place = jnp.sum(earlier.astype(jnp.float32), axis=0, keepdims=True)
        place = place.astype(jnp.int32)
        if interleave:
            place = (place >> 1) + (place & 1) * (n // 2)
        perm[...] = (sub == place).astype(jnp.float32).astype(jnp.bfloat16)

    moved = jnp.dot(perm[...], x_ref[...], preferred_element_type=jnp.float32)
    o_ref[...] = moved.astype(jnp.bfloat16).reshape(o_ref.shape)


def route(x, ids_col, ids_row, interleave):
    blocks = x.shape[1] // BLK
    parts = 2 if interleave else 1
    rows = SLOT_DEV // parts
    return pl.pallas_call(
        lambda *refs: route_kernel(interleave, *refs),
        grid=(blocks,),
        in_specs=[
            pl.BlockSpec((SLOT_DEV, 1), lambda b: (0, 0)),
            pl.BlockSpec((1, SLOT_DEV), lambda b: (0, 0)),
            pl.BlockSpec((SLOT_DEV, BLK), lambda b: (0, b)),
        ],
        out_specs=pl.BlockSpec((parts, rows, BLK), lambda b: (b, 0, 0)),
        out_shape=jax.ShapeDtypeStruct((blocks * parts, rows, BLK), jnp.bfloat16),
        scratch_shapes=[pltpu.VMEM((SLOT_DEV, SLOT_DEV), jnp.bfloat16)],
        compiler_params=params(),
        cost_estimate=pl.CostEstimate(
            flops=2 * SLOT_DEV * SLOT_DEV * x.shape[1],
            bytes_accessed=4 * SLOT_DEV * x.shape[1],
            transcendentals=0,
        ),
    )(ids_col, ids_row, x)


def gram_kernel(window, start_ref, end_ref, x_ref, o_ref, picked):
    e = pl.program_id(0)
    sources, rows = x_ref.shape[0], x_ref.shape[1]
    place = lax.broadcasted_iota(jnp.int32, (window, BLK), 0)
    for j in range(sources):
        start = start_ref[j, e]
        end = end_ref[j, e]
        base = pl.multiple_of(jnp.minimum(start // 16 * 16, rows - window), 16)
        part = x_ref[j, pl.ds(base, window), :]
        keep = (place >= start - base) & (place < end - base)
        picked[pl.ds(j * window, window), :] = jnp.where(keep, part, jnp.zeros_like(part))
    left = picked[:, :HALF]
    right = picked[:, HALF:]

    def product(a, b):
        return lax.dot_general(a, b, (((0,), (0,)), ((), ())), preferred_element_type=jnp.float32)

    quarters = {(0, 0): product(left, left), (0, 1): product(left, right), (1, 1): product(right, right)}
    for n, (i, j) in enumerate(TILES):
        block = quarters[(i // 2, j // 2)]
        r, c = i % 2 * TILE, j % 2 * TILE
        o_ref[0, pl.ds(n * TILE, TILE), :] = block[r : r + TILE, c : c + TILE]


def gram(x, start, end, window):
    sources, rows, _ = x.shape
    return pl.pallas_call(
        lambda *refs: gram_kernel(window, *refs),
        grid_spec=pltpu.PrefetchScalarGridSpec(
            num_scalar_prefetch=2,
            grid=(EXPERTS,),
            in_specs=[pl.BlockSpec((sources, rows, BLK), lambda e, s, t: (0, 0, 0))],
            out_specs=pl.BlockSpec((1, PACKED, TILE), lambda e, s, t: (e, 0, 0)),
            scratch_shapes=[pltpu.VMEM((sources * window, BLK), jnp.bfloat16)],
        ),
        out_shape=jax.ShapeDtypeStruct((EXPERTS, PACKED, TILE), jnp.float32),
        compiler_params=params(),
        cost_estimate=pl.CostEstimate(
            flops=2 * EXPERTS * sources * window * BLK * BLK,
            bytes_accessed=2 * x.size + 4 * EXPERTS * PACKED * TILE,
            transcendentals=0,
        ),
    )(start, end, x)


def split(x):
    high = x.astype(jnp.bfloat16)
    return high, (x - high.astype(jnp.float32)).astype(jnp.bfloat16)


def dot3(a, b):
    def one(p, q):
        return jnp.dot(p, q, preferred_element_type=jnp.float32)

    return one(a[0], b[0]) + (one(a[0], b[1]) + one(a[1], b[0]))


def newton_kernel(count_ref, *refs):
    grams, o_ref, e_ref, y_ref = refs[:-3], refs[-3], refs[-2], refs[-1]
    scale = 1.0 / count_ref[0]
    for n, (i, j) in enumerate(TILES):
        tile = grams[0][pl.ds(n * TILE, TILE), :]
        for more in grams[1:]:
            tile = tile + more[pl.ds(n * TILE, TILE), :]
        tile = tile * scale
        e_ref[pl.ds(i * TILE, TILE), pl.ds(j * TILE, TILE)] = tile
        if i != j:
            e_ref[pl.ds(j * TILE, TILE), pl.ds(i * TILE, TILE)] = tile.T
    sub = lax.broadcasted_iota(jnp.int32, (BLK, BLK), 0)
    lane = lax.broadcasted_iota(jnp.int32, (BLK, BLK), 1)
    diagonal = sub == lane
    matrix = e_ref[...] + jnp.where(diagonal, DAMPING, 0.0)
    norm = jnp.sqrt(jnp.sum(matrix * matrix, keepdims=True))
    e = matrix / norm
    e_ref[...] = e
    y_ref[...] = (jnp.where(diagonal, 2.0, 0.0) - e) / norm
    es = split(e)
    e_ref[...] = 2.0 * e_ref[...] - dot3(es, es)

    def step(_, carry):
        es = split(e_ref[...])
        ys = split(y_ref[...])
        y_ref[...] = 2.0 * y_ref[...] - dot3(ys, es)
        e_ref[...] = 2.0 * e_ref[...] - dot3(es, es)
        return carry

    lax.fori_loop(0, NS_STEPS - 2, step, 0)
    y = y_ref[...]
    o_ref[...] = (2.0 * y - dot3(split(y), split(e_ref[...]))).astype(jnp.bfloat16)


def newton(count, *grams):
    return pl.pallas_call(
        newton_kernel,
        in_specs=[pl.BlockSpec(memory_space=pltpu.SMEM)]
        + [pl.BlockSpec(memory_space=pltpu.VMEM)] * len(grams),
        out_specs=pl.BlockSpec(memory_space=pltpu.VMEM),
        out_shape=jax.ShapeDtypeStruct((BLK, BLK), jnp.bfloat16),
        scratch_shapes=[pltpu.VMEM((BLK, BLK), jnp.float32)] * 2,
        compiler_params=params(),
        cost_estimate=pl.CostEstimate(
            flops=2 * 14 * 3 * BLK**3, bytes_accessed=4 * BLK * BLK, transcendentals=0
        ),
    )(count, *grams)


def block_dot_kernel(a_ref, b_ref, o_ref):
    o_ref[...] = jnp.dot(
        a_ref[...], b_ref[...], preferred_element_type=jnp.float32
    ).astype(jnp.bfloat16)


def block_dot(a, b):
    blocks = a.shape[0] // BLK
    single = b.shape[0] == BLK
    return pl.pallas_call(
        block_dot_kernel,
        grid=(blocks,),
        in_specs=[
            pl.BlockSpec((BLK, BLK), lambda n: (n, 0)),
            pl.BlockSpec((BLK, BLK), lambda n: (0, 0) if single else (n, 0)),
        ],
        out_specs=pl.BlockSpec((BLK, BLK), lambda n: (n, 0)),
        out_shape=jax.ShapeDtypeStruct((blocks * BLK, BLK), jnp.bfloat16),
        compiler_params=params(),
        cost_estimate=pl.CostEstimate(
            flops=2 * blocks * BLK**3, bytes_accessed=6 * blocks * BLK * BLK, transcendentals=0
        ),
    )(a, b)


def per_device(slot_inputs, slot_grads, slot_expert, weight_grad):
    group_pos = lax.axis_index("expert")
    shard_pos = lax.axis_index("shard")
    labels = jnp.arange(EXPERTS, dtype=jnp.int32)
    ids_row = slot_expert.reshape(1, SLOT_DEV)
    sent_act = route(slot_inputs, slot_expert, ids_row, True)
    sent_out = route(slot_grads, slot_expert, ids_row, False)

    own_counts = jnp.sum((slot_expert == labels[None, :]).astype(jnp.int32), axis=0)
    counts = lax.all_gather(own_counts[None], ("expert", "shard"), axis=0, tiled=True)
    routed = jnp.sum(jnp.where(labels[None, :] == group_pos, counts, 0)).astype(jnp.float32)
    routed = routed.reshape(1)
    shards = lax.axis_size("shard")
    plane = lax.dynamic_slice_in_dim(counts, group_pos * shards, shards, 0)
    end = jnp.cumsum(plane, axis=1)
    start = end - plane
    odd = shard_pos & 1

    got_act = lax.all_to_all(sent_act, "shard", 0, 0, tiled=True)
    act = gram(got_act, (start + 1 - odd) >> 1, (end + 1 - odd) >> 1, 48)
    act = lax.psum_scatter(act, "expert", scatter_dimension=0, tiled=True)[0]
    got_out = lax.all_to_all(sent_out, "shard", 0, 0, tiled=True)
    out = gram(got_out, start, end, 80)
    out = lax.psum_scatter(out, "expert", scatter_dimension=0, tiled=True)[0]

    other = lax.ppermute(act, "shard", [(i, i ^ 1) for i in range(shards)])
    act_inverse = newton(routed, act, other)
    rows = lax.dynamic_slice_in_dim(act_inverse, odd * HALF, HALF, 0)
    act_inverse = lax.all_gather(rows, "shard", axis=0, tiled=True)
    out_inverse = newton(routed, out)

    left = block_dot(act_inverse, weight_grad[0])
    return block_dot(left, out_inverse)[None]


def solution(mesh):
    in_specs = (
        P(("expert", "shard"), None),
        P(("expert", "shard"), None),
        P(("expert", "shard"), None),
        P("expert", None, "shard"),
    )
    out_specs = P("expert", None, "shard")
    return jax.shard_map(
        per_device, mesh=mesh, in_specs=in_specs, out_specs=out_specs, check_vma=False
    )
```

time: 493 us -> 298 us (0.60); the launches traced: 483 us -> 296 us
  matrix products: 135 us -> 0 us
  blocking collectives: 224 us -> 138 us
  Pallas kernels: 0 us -> 57.2 us
  local copies, waits for them, and re-layouts: 42.8 us -> 17.5 us
  other arithmetic: 19.1 us -> 0.95 us
  waiting for transfers between devices: 45.4 us -> 59.5 us
  starting transfers between devices: 2.1 us -> 8.65 us
    dot_general x36 -> x0, matrix products: 135 us -> none  [the longest x16 43 us: newton_whole(): jnp.matmul(iterate, matrix, precision=PRECISE)]
    all_to_all x2 -> x1, blocking collectives: 155 us -> 54.9 us  [per_device(): got_out = lax.all_to_all(sent_out, 'shard', 0, 0, tiled=True)]
    unnamed x0 -> x1, blocking collectives: none -> 83.2 us
    psum x1 -> x0, blocking collectives: 69.4 us -> none  [per_device(): totals = lax.psum(local_counts.astype(jnp.float32), ('expert', 'shard'))]
    pallas_call x0 -> x8, Pallas kernels: none -> 57.2 us  [the longest x2 26.8 us: newton(): pl.pallas_call(newton_kernel, in_specs=[pl.BlockSpec(memory_space=pltpu.S...]
    all_gather x1, waiting for transfers between devices: 3.65 us -> 42.5 us  [per_device(): act_inverse = lax.all_gather(rows, 'shard', axis=0, tiled=True)]
    reduce_scatter x2, waiting for transfers between devices: 41.7 us -> 3.37 us  [the longest x1 3.35 us: per_device(): out = lax.psum_scatter(out, 'expert', scatter_dimension=0, tiled=True)[0]]
    gather x2 -> x0, local copies, waits for them, and re-layouts: 22.6 us -> none  [the longest x1 18.2 us: per_device(): jnp.take(slot_grads, source, axis=0) * keep_mask]
  transfers between devices with their start and end apart: 4 -> 5, of which waited for: 2 -> 3; matrix products, arithmetic and copies ran while one was open for 26% -> 1% of each run, Pallas kernels for 0% -> 13%
where the time goes in v1:
time: 298 us; the launch traced here: 296 us
  blocking collectives  138 us (46%)
  waiting for transfers between devices  59.5 us (20%)
  Pallas kernels  57.2 us (19%)
  local copies, waits for them, and re-layouts  17.5 us (6%)
  between operations  13.9 us (5%)
  starting transfers between devices  8.65 us (3%)
    unnamed x1, blocking collectives  83.2 us
    all_to_all x1, blocking collectives, per_device(): got_out = lax.all_to_all(sent_out, 'shard', 0, 0, tiled=True)  54.9 us
    all_gather x1, waiting for transfers between devices, per_device(): act_inverse = lax.all_gather(rows, 'shard', axis=0, tiled=True)  42.5 us
    pallas_call x2, Pallas kernels, newton(): pl.pallas_call(newton_kernel, in_specs=[pl.BlockSpec(memory_space=pltpu.S...  26.8 us
    unnamed x23, local copies, waits for them, and re-layouts  16.7 us
    ppermute x1, waiting for transfers between devices, per_device(): other = lax.ppermute(act, 'shard', [(i, i ^ 1) for i in range(shards)])  13.6 us
    pallas_call x2, Pallas kernels, gram(): pl.pallas_call(lambda *refs: gram_kernel(window, *refs), grid_spec=pltpu....  13 us
    pallas_call x2, Pallas kernels, block_dot(): pl.pallas_call(block_dot_kernel, grid=(blocks,), in_specs=[pl.BlockSpec((...  8.93 us
  transfers between devices with their start and end apart: 5, of which 3 were waited for; matrix products, arithmetic and copies ran while one was open for 1% of the time, Pallas kernels for 13%

profile of v1, /device:TPU:24, one launch (start us, length us, event | category | flops | bytes accessed | tf_op | source)
XLA Modules:
  0.0 295.9 jit_solution(4282317499323009615)
XLA Ops:
  6.5 0.8 copy.9.refs_0_
  7.4 1.6 copy-done.5
  9.6 4.2 %shard_map.46 = bf16[16,128,512]{2,1,0:T(8,128)(2,1)} custom-call(s32[256,1]{1,0:T(8,128)S(1)} %copy.9.refs_0_, s32[1,256]{1,0:T(1,128)S(1)} %bitcast.8, bf16[256,4096]{1,0:T(8,128)(2,1)S(1)} %copy-done.5), custom_call_target="tpu_custom_call" | custom-call | flops 536870912 | bytes 4194304 | tf_op jit(solution)/shard_map/pallas_call | solution.py:48
  13.9 7.9 %all-to-all-start = ((bf16[16,128,512]{2,1,0:T(8,128)(2,1)}), bf16[16,128,512]{2,1,0:T(8,128)(2,1)S(1)}, u32[]{:S(2)}, u32[]{:S(2)}) async-start(bf16[16,128,512]{2,1,0:T(8,128)(2,1)} %shard_map.46), calls=%async_computation | async-start | bytes 4194304 | tf_op jit(solution)/shard_map/all_to_all | solution.py:217
  22.2 83.2 %all-reduce = s32[1024]{0:T(1024)S(1)} all-reduce(s32[1024]{0:T(1024)S(1)} %dynamic-update-slice), channel_id=2, replica_groups=mesh['expert'=8,'shard'=16] {'expert','shard'}, use_global_device_ids=true, to_apply=%add | all-reduce | flops 1024 | bytes 8192
  105.7 5.7 %shard_map.47 = f32[8,1280,128]{2,1,0:T(8,128)S(1)} custom-call(s32[16,8]{1,0:T(8,128)S(1)} %get-tuple-element.5.refs_0_, s32[16,8]{1,0:T(8,128)S(1)} %get-tuple-element.7.refs_1_, bf16[16,128,512]{2,1,0:T(8,128)(2,1)S(1)} %all-to-all-done.refs_2_), custom_call_target="tpu_custom_call" | custom-call | flops 3221225472 | bytes 7340032 | tf_op jit(solution)/shard_map/pallas_call | solution.py:94
  111.4 2.3 copy-done.1
  113.8 2.2 copy-done.4
  116.0 4.3 %shard_map.50 = bf16[16,256,512]{2,1,0:T(8,128)(2,1)S(1)} custom-call(s32[256,1]{1,0:T(8,128)S(1)} %copy.9.refs_0_, s32[1,256]{1,0:T(1,128)S(1)} %bitcast.10, bf16[256,8192]{1,0:T(8,128)(2,1)S(1)} %copy-done.4), custom_call_target="tpu_custom_call" | custom-call | flops 1073741824 | bytes 8388608 | tf_op jit(solution)/shard_map/pallas_call | solution.py:48
  120.3 54.9 %all_to_all.10.refs_2_ = bf16[16,256,512]{2,1,0:T(8,128)(2,1)S(1)} all-to-all(bf16[16,256,512]{2,1,0:T(8,128)(2,1)S(1)} %shard_map.50), channel_id=1, replica_groups=mesh['expert'=8,'shard'=16] {'shard'}, dimensions={0} | all-to-all | bytes 8388608 | tf_op jit(solution)/shard_map/all_to_all | solution.py:220
  175.2 7.3 %shard_map.51 = f32[8,1280,128]{2,1,0:T(8,128)S(1)} custom-call(s32[16,8]{1,0:T(8,128)S(1)} %get-tuple-element.6.refs_0_, s32[16,8]{1,0:T(8,128)S(1)} %reduce_window_sum.11.refs_1_, bf16[16,256,512]{2,1,0:T(8,128)(2,1)S(1)} %all_to_all.10.refs_2_), custom_call_target="tpu_custom_call" | custom-call | flops 5368709120 | bytes 9437184 | tf_op jit(solution)/shard_map/pallas_call | solution.py:94
  182.5 2.3 copy-done
  186.9 13.6 %collective-permute-done.refs_1_ = f32[1280,128]{1,0:T(8,128)S(1)} collective-permute-done((f32[1280,128]{1,0:T(8,128)}, f32[1280,128]{1,0:T(8,128)S(1)}, u32[]{:S(2)}, u32[]{:S(2)}) %collective-permute-start) | collective-permute-done | bytes 655392 | tf_op jit(solution)/shard_map/ppermute | solution.py:224
  200.4 1.1 copy-done.8
  201.5 13.4 %shard_map.48 = bf16[512,512]{1,0:T(8,128)(2,1)S(1)} custom-call(f32[1]{0:T(128)} %bitcast.1.count_ref, f32[1280,128]{1,0:T(8,128)S(1)} %bitcast.12, f32[1280,128]{1,0:T(8,128)S(1)} %collective-permute-done.refs_1_), custom_call_target="tpu_custom_call" | custom-call | flops 11274289152 | bytes 1048576 | tf_op jit(solution)/shard_map/pallas_call | solution.py:160
  214.9 0.7 constant_dynamic-slice_fusion
  215.7 3.4 %reduce-scatter.5.cloned.1.call-done = f32[1,1280,128]{2,1,0:T(8,128)} async-done(((f32[8,1280,128]{2,1,0:T(8,128)}), f32[1,1280,128]{2,1,0:T(8,128)}) %reduce-scatter.5.cloned.1.call-update) | async-done | bytes 655376 | tf_op jit(solution)/shard_map/reduce_scatter | solution.py:222
  219.0 1.1 copy-done.9
  220.1 13.4 %shard_map.52.b_ref = bf16[512,512]{1,0:T(8,128)(2,1)S(1)} custom-call(f32[1]{0:T(128)} %bitcast.1.count_ref, f32[1280,128]{1,0:T(8,128)S(1)} %bitcast.13), custom_call_target="tpu_custom_call" | custom-call | flops 11274289152 | bytes 1048576 | tf_op jit(solution)/shard_map/pallas_call | solution.py:160
  233.5 42.5 %all-gather.3.cloned.1.call-done.a_ref = bf16[4096,512]{1,0:T(8,128)(2,1)} async-done(((bf16[256,512]{1,0:T(8,128)(2,1)}), bf16[4096,512]{1,0:T(8,128)(2,1)}) %all-gather.3.cloned.1.call-update) | async-done | bytes 4194320 | tf_op jit(solution)/shard_map/all_gather | solution.py:227
  276.1 2.2 copy-done.2
  278.3 2.2 copy-done.3
  280.4 3.5 %shard_map.49.a_ref = bf16[4096,512]{1,0:T(8,128)(2,1)S(1)} custom-call(bf16[4096,512]{1,0:T(8,128)(2,1)S(1)} %copy-done.3, bf16[4096,512]{1,0:T(8,128)(2,1)S(1)} %bitcast.7), custom_call_target="tpu_custom_call" | custom-call | flops 2147483648 | bytes 12582912 | tf_op jit(solution)/shard_map/pallas_call | solution.py:183
  284.0 5.4 %shard_map.53 = bf16[4096,512]{1,0:T(8,128)(2,1)} custom-call(bf16[4096,512]{1,0:T(8,128)(2,1)S(1)} %shard_map.49.a_ref, bf16[512,512]{1,0:T(8,128)(2,1)S(1)} %shard_map.52.b_ref), custom_call_target="tpu_custom_call" | custom-call | flops 2147483648 | bytes 12582912 | tf_op jit(solution)/shard_map/pallas_call | solution.py:183
  (30 shorter events, 2.8 us)
Async XLA Ops:
  7.3 1.6 copy-start.5
  8.9 0.7 copy-start.6
  9.6 12.2 %copy-start.7 = (s32[256,1]{0,1:T(1,128)S(1)}, s32[256,1]{0,1:T(1,128)}, u32[]{:S(2)}) copy-start(s32[256,1]{0,1:T(1,128)} %param.6) | copy-start | bytes 3076
  13.9 91.8 %all-to-all-start = ((bf16[16,128,512]{2,1,0:T(8,128)(2,1)}), bf16[16,128,512]{2,1,0:T(8,128)(2,1)S(1)}, u32[]{:S(2)}, u32[]{:S(2)}) async-start(bf16[16,128,512]{2,1,0:T(8,128)(2,1)} %shard_map.46), calls=%async_computation | async-start | bytes 4194304 | tf_op jit(solution)/shard_map/all_to_all | solution.py:217
  21.8 163.1 %reduce-scatter.3.cloned.1.call-start = ((), (), s32[]{:S(2)}) async-start(), calls=%async_computation.4 | async-start | bytes 5898240 | tf_op jit(solution)/shard_map/reduce_scatter | solution.py:219
  111.4 2.3 copy-start.1
  113.7 105.3 %reduce-scatter.5.cloned.1.call-start = ((), (), s32[]{:S(2)}) async-start(), calls=%async_computation.6 | async-start | bytes 5898240 | tf_op jit(solution)/shard_map/reduce_scatter | solution.py:222
  113.8 2.2 copy-start.4
  182.5 2.3 copy-start
  184.8 91.2 %all-gather.3.cloned.1.call-start = ((), (), s32[]{:S(2)}) async-start(), calls=%async_computation.5 | async-start | bytes 4456448 | tf_op jit(solution)/shard_map/all_gather | solution.py:227
  184.9 15.5 %collective-permute-start = (f32[1280,128]{1,0:T(8,128)}, f32[1280,128]{1,0:T(8,128)S(1)}, u32[]{:S(2)}, u32[]{:S(2)}) collective-permute-start(f32[1280,128]{1,0:T(8,128)} %bitcast.11), channel_id=1, source_target_pairs={{0,1},{1,0},{2,3},{3,2},{4,5},{5,4},{6,7},{7,6},{8,9},{9,8},{10,11... | collective-permute-start | bytes 1966088 | tf_op jit(solution)/shard_map/ppermute | solution.py:224
  200.4 1.1 copy-start.8
  219.0 1.1 copy-start.9
  276.1 2.2 copy-start.2
  278.2 2.2 copy-start.3
Sparse Core Ops, SparseCore 0:
  113.9 35.6 reduce-scatter.2
  185.0 34.0 reduce-scatter.4
  221.2 54.8 all-gather.2

commit v2 on v1

v2 whole, which is shorter than its diff:
```python
import jax
import jax.numpy as jnp
from jax import lax
from jax.experimental import pallas as pl
from jax.experimental.pallas import tpu as pltpu
from jax.sharding import PartitionSpec as P

D = 4096
FF = 8192
BLK = 512
HALF = 256
TILE = 128
EXPERTS = 8
SLOT_DEV = 256
NS_STEPS = 8
DAMPING = 0.1
VMEM_LIMIT = 20 * 1024 * 1024

TILES = [(i, j) for i in range(4) for j in range(i, 4)]
PACKED = len(TILES) * TILE
NOTE = 16
CAP = 64

BRIEF = pl.CostEstimate(flops=1 << 20, bytes_accessed=1 << 12, transcendentals=0)


def params():
    return pltpu.CompilerParams(vmem_limit_bytes=VMEM_LIMIT)


def route_kernel(noted, col_ref, row_ref, x_ref, o_ref, perm):
    n = SLOT_DEV

    @pl.when(pl.program_id(0) == 0)
    def _():
        sub = lax.broadcasted_iota(jnp.int32, (n, n), 0)
        lane = lax.broadcasted_iota(jnp.int32, (n, n), 1)
        earlier = col_ref[...] * n + sub < row_ref[...] * n + lane
        place = jnp.sum(earlier.astype(jnp.float32), axis=0, keepdims=True)
        place = place.astype(jnp.int32)
        if noted:
            place = (place >> 1) + (place & 1) * (n // 2)
        perm[...] = (sub == place).astype(jnp.float32).astype(jnp.bfloat16)

    moved = jnp.dot(perm[...], x_ref[...], preferred_element_type=jnp.float32)
    moved = moved.astype(jnp.bfloat16)
    if noted:
        lane = lax.broadcasted_iota(jnp.int32, (n, BLK), 1)
        counts = jnp.sum((col_ref[...] == lane).astype(jnp.float32), axis=0, keepdims=True)
        counts = jnp.broadcast_to(counts, (NOTE, BLK)).astype(jnp.bfloat16)
        for half in range(2):
            o_ref[half, : n // 2, :] = moved[half * (n // 2) : (half + 1) * (n // 2)]
            o_ref[half, n // 2 :, :] = counts
    else:
        o_ref[0] = moved


def route(x, ids_col, ids_row, noted):
    blocks = x.shape[1] // BLK
    block = (2, SLOT_DEV // 2 + NOTE, BLK) if noted else (1, SLOT_DEV, BLK)
    return pl.pallas_call(
        lambda *refs: route_kernel(noted, *refs),
        grid=(blocks,),
        in_specs=[
            pl.BlockSpec((SLOT_DEV, 1), lambda b: (0, 0)),
            pl.BlockSpec((1, SLOT_DEV), lambda b: (0, 0)),
            pl.BlockSpec((SLOT_DEV, BLK), lambda b: (0, b)),
        ],
        out_specs=pl.BlockSpec(block, lambda b: (b, 0, 0)),
        out_shape=jax.ShapeDtypeStruct((blocks * block[0],) + block[1:], jnp.bfloat16),
        scratch_shapes=[pltpu.VMEM((SLOT_DEV, SLOT_DEV), jnp.bfloat16)],
        compiler_params=params(),
        cost_estimate=BRIEF,
    )(ids_col, ids_row, x)


def gram_kernel(rows, window, start_ref, end_ref, x_ref, o_ref, picked):
    e = pl.program_id(0)
    place = lax.broadcasted_iota(jnp.int32, (window, BLK), 0)
    total = 0
    for j in range(x_ref.shape[0]):
        start = start_ref[j, e]
        end = end_ref[j, e]
        total = total + (end - start)
        base = pl.multiple_of(jnp.minimum(start // 16 * 16, rows - window), 16)
        part = x_ref[j, pl.ds(base, window), :]
        keep = (place >= start - base) & (place < end - base)
        picked[pl.ds(j * window, window), :] = jnp.where(keep, part, jnp.zeros_like(part))
    left = picked[:, :HALF]
    right = picked[:, HALF:]

    def product(a, b):
        return lax.dot_general(a, b, (((0,), (0,)), ((), ())), preferred_element_type=jnp.float32)

    quarters = {(0, 0): product(left, left), (0, 1): product(left, right), (1, 1): product(right, right)}
    for n, (i, j) in enumerate(TILES):
        block = quarters[(i // 2, j // 2)]
        r, c = i % 2 * TILE, j % 2 * TILE
        o_ref[0, pl.ds(n * TILE, TILE), :] = block[r : r + TILE, c : c + TILE]
    o_ref[0, pl.ds(PACKED, 8), :] = jnp.full((8, TILE), total >> 5, jnp.int32).astype(jnp.float32)
    o_ref[0, pl.ds(PACKED + 8, 8), :] = jnp.full((8, TILE), total & 31, jnp.int32).astype(jnp.float32)


def gram(x, start, end, rows, most):
    sources = x.shape[0]
    height = PACKED + NOTE
    window = most + 16
    return pl.pallas_call(
        lambda *refs: gram_kernel(rows, window, *refs),
        grid_spec=pltpu.PrefetchScalarGridSpec(
            num_scalar_prefetch=2,
            grid=(EXPERTS,),
            in_specs=[pl.BlockSpec(memory_space=pltpu.VMEM)],
            out_specs=pl.BlockSpec((1, height, TILE), lambda e, s, t: (e, 0, 0)),
            scratch_shapes=[pltpu.VMEM((sources * window, BLK), jnp.bfloat16)],
        ),
        out_shape=jax.ShapeDtypeStruct((EXPERTS, height, TILE), jnp.float32),
        compiler_params=params(),
        cost_estimate=BRIEF,
    )(start, end, x)


def newton_kernel(packed, *refs):
    grams, o_ref = refs[:-7], refs[-7]
    e_top, e_low, x_top, x_low, f_ref, g_ref = refs[-6:]

    def diagonal(width):
        shape = (HALF, width)
        return lax.broadcasted_iota(jnp.int32, shape, 0) == lax.broadcasted_iota(jnp.int32, shape, 1)

    wide, square = diagonal(BLK), diagonal(HALF)

    def total(row, height):
        value = grams[0][pl.ds(row, height), :].astype(jnp.float32)
        for more in grams[1:]:
            value = value + more[pl.ds(row, height), :].astype(jnp.float32)
        return value

    note = total(PACKED, NOTE)
    scale = 1.0 / (32.0 * note[0:1, :] + note[8:9, :])
    for n, (i, j) in enumerate(TILES):
        tile = total(n * TILE, TILE) * scale
        if i < 2:
            e_top[pl.ds(i * TILE, TILE), pl.ds(j * TILE, TILE)] = tile
        else:
            e_low[pl.ds((i - 2) * TILE, TILE), pl.ds((j - 2) * TILE, TILE)] = tile
        if (i, j) == (0, 1):
            e_top[pl.ds(TILE, TILE), pl.ds(0, TILE)] = tile.T
        if (i, j) == (2, 3):
            e_low[pl.ds(TILE, TILE), pl.ds(0, TILE)] = tile.T
    top = e_top[...] + jnp.where(wide, DAMPING, 0.0)
    low = e_low[...] + jnp.where(square, DAMPING, 0.0)

    def squares(x):
        return jnp.sum(x * x, keepdims=True)

    norm = jnp.sqrt(squares(top[:, :HALF]) + 2.0 * squares(top[:, HALF:]) + squares(low))
    top, low = top / norm, low / norm
    e_top[...], e_low[...] = top, low
    x_top[...] = (jnp.where(wide, 2.0, 0.0) - top) / norm
    x_low[...] = (jnp.where(square, 2.0, 0.0) - low) / norm

    def center(top_ref, low_ref, whole):
        top, low = top_ref[...], low_ref[...]
        trace = jnp.sum(jnp.where(square, top[:, :HALF], 0.0) + jnp.where(square, low, 0.0), keepdims=True)
        mean = trace * (1.0 / BLK)
        top = top - jnp.where(wide, mean, 0.0)
        low = low - jnp.where(square, mean, 0.0)
        rounded = top.astype(jnp.bfloat16)
        whole[:HALF, :] = rounded
        whole[HALF:, HALF:] = low.astype(jnp.bfloat16)
        whole[HALF:, :HALF] = rounded[:, HALF:].T
        return mean, top, low

    def product(whole):
        return (
            jnp.dot(whole[:HALF, :], f_ref[...], preferred_element_type=jnp.float32),
            jnp.dot(whole[HALF:, :], f_ref[:, HALF:], preferred_element_type=jnp.float32),
        )

    def next_e(s, top, low):
        product_top, product_low = product(f_ref)
        e_top[...] = jnp.where(wide, 2.0 * s - s * s, 0.0) + (2.0 - 2.0 * s) * top - product_top
        e_low[...] = jnp.where(square, 2.0 * s - s * s, 0.0) + (2.0 - 2.0 * s) * low - product_low

    def next_x(s, e_top, e_low, t, top, low):
        product_top, product_low = product(g_ref)
        x_top[...] = jnp.where(wide, 2.0 * t - t * s, 0.0) + (2.0 - s) * top - t * e_top - product_top
        x_low[...] = jnp.where(square, 2.0 * t - t * s, 0.0) + (2.0 - s) * low - t * e_low - product_low

    next_e(*center(e_top, e_low, f_ref))
    for step in range(1, NS_STEPS):
        e = center(e_top, e_low, f_ref)
        x = center(x_top, x_low, g_ref)
        next_x(*e, *x)
        if step < NS_STEPS - 1:
            next_e(*e)
    top = x_top[...].astype(jnp.bfloat16)
    low = x_low[...].astype(jnp.bfloat16)
    if packed:
        for n, (i, j) in enumerate(TILES):
            rows = top if i < 2 else low
            r, c = i % 2 * TILE, (j if i < 2 else j - 2) * TILE
            o_ref[pl.ds(n * TILE, TILE), :] = rows[r : r + TILE, c : c + TILE]
    else:
        o_ref[:HALF, :] = top
        o_ref[HALF:, HALF:] = low
        o_ref[HALF:, :HALF] = top[:, HALF:].T


def newton(packed, *grams):
    return pl.pallas_call(
        lambda *refs: newton_kernel(packed, *refs),
        in_specs=[pl.BlockSpec(memory_space=pltpu.VMEM)] * len(grams),
        out_specs=pl.BlockSpec(memory_space=pltpu.VMEM),
        out_shape=jax.ShapeDtypeStruct((PACKED, TILE) if packed else (BLK, BLK), jnp.bfloat16),
        scratch_shapes=[pltpu.VMEM((HALF, BLK), jnp.float32), pltpu.VMEM((HALF, HALF), jnp.float32)] * 2
        + [pltpu.VMEM((BLK, BLK), jnp.bfloat16)] * 2,
        compiler_params=params(),
        cost_estimate=BRIEF,
    )(*grams)


def left_kernel(index_ref, *refs):
    packed, w_ref, o_ref, block = refs[:-3], refs[-3], refs[-2], refs[-1]
    for k, inverse in enumerate(packed):

        @pl.when(pl.program_id(0) == k)
        def _(inverse=inverse):
            for n, (i, j) in enumerate(TILES):
                tile = inverse[pl.ds(n * TILE, TILE), :]
                block[pl.ds(i * TILE, TILE), pl.ds(j * TILE, TILE)] = tile
                if i != j:
                    block[pl.ds(j * TILE, TILE), pl.ds(i * TILE, TILE)] = tile.T

    o_ref[...] = jnp.dot(
        block[...], w_ref[...], preferred_element_type=jnp.float32
    ).astype(jnp.bfloat16)


def left_product(index, packed, grad):
    blocks = len(packed)
    return pl.pallas_call(
        left_kernel,
        grid_spec=pltpu.PrefetchScalarGridSpec(
            num_scalar_prefetch=1,
            grid=(blocks,),
            in_specs=[pl.BlockSpec((PACKED, TILE), lambda n, s: (0, 0))] * blocks
            + [pl.BlockSpec((BLK, BLK), lambda n, s: (s[n], 0))],
            out_specs=pl.BlockSpec((BLK, BLK), lambda n, s: (s[n], 0)),
            scratch_shapes=[pltpu.VMEM((BLK, BLK), jnp.bfloat16)],
        ),
        out_shape=jax.ShapeDtypeStruct((blocks * BLK, BLK), jnp.bfloat16),
        compiler_params=params(),
        cost_estimate=BRIEF,
    )(index, *packed, grad)


def right_kernel(a_ref, b_ref, o_ref):
    o_ref[...] = jnp.dot(
        a_ref[...], b_ref[...], preferred_element_type=jnp.float32
    ).astype(jnp.bfloat16)


def right_product(a, b):
    blocks = a.shape[0] // BLK
    return pl.pallas_call(
        right_kernel,
        grid=(blocks,),
        in_specs=[
            pl.BlockSpec((BLK, BLK), lambda n: (n, 0)),
            pl.BlockSpec((BLK, BLK), lambda n: (0, 0)),
        ],
        out_specs=pl.BlockSpec((BLK, BLK), lambda n: (n, 0)),
        out_shape=jax.ShapeDtypeStruct((blocks * BLK, BLK), jnp.bfloat16),
        compiler_params=params(),
        cost_estimate=BRIEF,
    )(a, b)


def send(x, axis, target):
    return lax.ppermute(x, axis, [(i, target(i)) for i in range(lax.axis_size(axis))])


def sum_over_group(grams):
    return lax.psum_scatter(grams, "expert", scatter_dimension=0, tiled=True)[0]


def per_device(slot_inputs, slot_grads, slot_expert, weight_grad):
    shard_pos = lax.axis_index("shard")
    odd = shard_pos & 1
    ids_row = slot_expert.reshape(1, SLOT_DEV)
    sent_act = route(slot_inputs, slot_expert, ids_row, True)
    sent_out = route(slot_grads, slot_expert, ids_row, False)

    got_act = lax.all_to_all(sent_act, "shard", 0, 0, tiled=True)
    sent_out, got_act = lax.optimization_barrier((sent_out, got_act))
    got_out = lax.all_to_all(sent_out, "shard", 0, 0, tiled=True)

    counts = got_act[:, SLOT_DEV // 2, :EXPERTS].astype(jnp.int32)
    label = jnp.arange(EXPERTS, dtype=jnp.int32)
    before = (label[:, None] < label[None, :]).astype(jnp.int32)
    start = jnp.sum(counts[:, :, None] * before[None], axis=1)
    end = start + counts

    act = gram(got_act, (start + 1 - odd) >> 1, (end + 1 - odd) >> 1, SLOT_DEV // 2, CAP // 2)
    act = sum_over_group(act)
    out = sum_over_group(gram(got_out, start, end, SLOT_DEV, CAP))
    other = send(act.astype(jnp.bfloat16), "shard", lambda i: i ^ 1)
    act_inverse = newton(True, act, other)
    out_inverse = newton(False, out)

    def up(i):
        return (i + 4) % 16

    def down(i):
        return (i - 4) % 16

    across = send(act_inverse, "shard", lambda i: i // 4 * 4 + 3 - i % 4)
    own_below = send(act_inverse, "shard", up)
    own_above = send(act_inverse, "shard", down)
    across_below = send(across, "shard", up)
    across_above = send(across, "shard", down)
    own_far = send(own_below, "shard", up)
    across_far = send(across_above, "shard", down)
    z, side = shard_pos >> 2, shard_pos >> 1 & 1
    inverses = [act_inverse, across, own_below, across_below, own_above, across_above, own_far, across_far]
    index = []
    for step in (0, -1, 1, 2):
        index += [2 * ((z + step) & 3) + side, 2 * ((z + step) & 3) + 1 - side]
    left = left_product(jnp.stack(index).astype(jnp.int32), inverses, weight_grad[0])
    return right_product(left, out_inverse)[None]


def solution(mesh):
    in_specs = (
        P(("expert", "shard"), None),
        P(("expert", "shard"), None),
        P(("expert", "shard"), None),
        P("expert", None, "shard"),
    )
    out_specs = P("expert", None, "shard")
    return jax.shard_map(
        per_device, mesh=mesh, in_specs=in_specs, out_specs=out_specs, check_vma=False
    )
```

time: 298 us -> 204 us (0.68)
  blocking collectives: 138 us -> 54.1 us
  Pallas kernels: 57.2 us -> 41.5 us
  starting transfers between devices: 8.65 us -> 16.3 us
  waiting for transfers between devices: 59.5 us -> 53.8 us
  local copies, waits for them, and re-layouts: 17.5 us -> 22.2 us
    unnamed x1 -> x0, blocking collectives: 83.2 us -> none
    all_gather x1 -> x0, waiting for transfers between devices: 42.5 us -> none  [per_device(): act_inverse = lax.all_gather(rows, 'shard', axis=0, tiled=True)]
    all_to_all x1, waiting for transfers between devices: 0.01 us -> 26.9 us  [per_device(): got_act = lax.all_to_all(sent_act, 'shard', 0, 0, tiled=True)]
    pallas_call x8, Pallas kernels: 57.2 us -> 41.5 us  [the longest x2 13.2 us: gram(): pl.pallas_call(lambda *refs: gram_kernel(rows, window, *refs), grid_spec=...]
    ppermute x1 -> x8, waiting for transfers between devices: 13.6 us -> 26.9 us  [send(): lax.ppermute(x, axis, [(i, target(i)) for i in range(lax.axis_size(axis))])]
    ppermute x1 -> x8, starting transfers between devices: 0.65 us -> 8.36 us  [send(): lax.ppermute(x, axis, [(i, target(i)) for i in range(lax.axis_size(axis))])]
    unnamed x23 -> x27, local copies, waits for them, and re-layouts: 16.7 us -> 22 us
    reduce_scatter x2, waiting for transfers between devices: 3.37 us -> 0.02 us  [sum_over_group(): return lax.psum_scatter(grams, 'expert', scatter_dimension=0, tiled=True)[0]]
  transfers between devices with their start and end apart: 5 -> 11, of which waited for: 3 -> 6; matrix products, arithmetic and copies ran while one was open for 1% -> 1% of each run, Pallas kernels for 13% -> 11%
where the time goes in v2:
time: 204 us; the launch traced here: 203 us
  blocking collectives  54.1 us (27%)
  waiting for transfers between devices  53.8 us (26%)
  Pallas kernels  41.5 us (20%)
  local copies, waits for them, and re-layouts  22.2 us (11%)
  starting transfers between devices  16.3 us (8%)
  between operations  13.6 us (7%)
    all_to_all x1, blocking collectives, per_device(): got_out = lax.all_to_all(sent_out, 'shard', 0, 0, tiled=True)  54.1 us
    all_to_all x1, waiting for transfers between devices, per_device(): got_act = lax.all_to_all(sent_act, 'shard', 0, 0, tiled=True)  26.9 us
    ppermute x8, waiting for transfers between devices, send(): lax.ppermute(x, axis, [(i, target(i)) for i in range(lax.axis_size(axis))])  26.9 us
    unnamed x27, local copies, waits for them, and re-layouts  22 us
    pallas_call x2, Pallas kernels, gram(): pl.pallas_call(lambda *refs: gram_kernel(rows, window, *refs), grid_spec=...  13.2 us
    pallas_call x2, Pallas kernels, newton(): pl.pallas_call(lambda *refs: newton_kernel(packed, *refs), in_specs=[pl.B...  11.2 us
    ppermute x8, starting transfers between devices, send(): lax.ppermute(x, axis, [(i, target(i)) for i in range(lax.axis_size(axis))])  8.36 us
    all_to_all x1, starting transfers between devices, per_device(): got_act = lax.all_to_all(sent_act, 'shard', 0, 0, tiled=True)  7.87 us
  transfers between devices with their start and end apart: 11, of which 6 were waited for; matrix products, arithmetic and copies ran while one was open for 1% of the time, Pallas kernels for 11%

profile of v2, /device:TPU:24, one launch (start us, length us, event | category | flops | bytes accessed | tf_op | source)
XLA Modules:
  0.0 202.8 jit_solution(73115057169221642)
XLA Ops:
  9.6 2.2 %shard_map.47 = bf16[16,144,512]{2,1,0:T(8,128)(2,1)S(1)} custom-call(s32[256,1]{1,0:T(8,128)S(1)} %copy.17.refs_0_, s32[1,256]{1,0:T(1,128)S(1)} %bitcast.21, bf16[256,4096]{1,0:T(8,128)(2,1)S(1)} %copy-done.9), custom_call_target="tpu_custom_call" | custom-call | flops 1048576 | bytes 4096 | tf_op jit(solution)/shard_map/pallas_call | solution.py:61
  13.3 7.9 %all-to-all-start = ((bf16[16,144,512]{2,1,0:T(8,128)(2,1)}), bf16[16,144,512]{2,1,0:T(8,128)(2,1)S(1)}, u32[]{:S(2)}, u32[]{:S(2)}) async-start(bf16[16,144,512]{2,1,0:T(8,128)(2,1)} %copy-done.5), calls=%async_computation | async-start | bytes 4718592 | tf_op jit(solution)/shard_map/all_to_all | solution.py:296
  21.2 2.2 %copy-done.6 = bf16[256,8192]{1,0:T(8,128)(2,1)S(1)} copy-done((bf16[256,8192]{1,0:T(8,128)(2,1)S(1)}, bf16[256,8192]{1,0:T(8,128)(2,1)}, u32[]{:S(2)}) %copy-start.6) | copy-done | bytes 4194328
  23.4 4.3 %shard_map.46 = bf16[16,256,512]{2,1,0:T(8,128)(2,1)S(1)} custom-call(s32[256,1]{1,0:T(8,128)S(1)} %copy.17.refs_0_, s32[1,256]{1,0:T(1,128)S(1)} %bitcast.22, bf16[256,8192]{1,0:T(8,128)(2,1)S(1)} %copy-done.6), custom_call_target="tpu_custom_call" | custom-call | flops 1048576 | bytes 4096 | tf_op jit(solution)/shard_map/pallas_call | solution.py:61
  27.7 2.0 copy-done.2
  29.8 26.9 %all-to-all-done.refs_2_ = bf16[16,144,512]{2,1,0:T(8,128)(2,1)S(1)} async-done(((bf16[16,144,512]{2,1,0:T(8,128)(2,1)}), bf16[16,144,512]{2,1,0:T(8,128)(2,1)S(1)}, u32[]{:S(2)}, u32[]{:S(2)}) %all-to-all-start) | async-done | bytes 2359328 | tf_op jit(solution)/shard_map/all_to_all | solution.py:296
  56.9 5.8 %shard_map.48 = f32[8,1296,128]{2,1,0:T(8,128)S(1)} custom-call(s32[16,8]{1,0:T(8,128)S(1)} %get-tuple-element.11.refs_0_, s32[16,8]{1,0:T(8,128)S(1)} %get-tuple-element.9.refs_1_, bf16[16,144,512]{2,1,0:T(8,128)(2,1)S(1)} %all-to-all-done.refs_2_), custom_call_target="tpu_custom_call" | custom-call | flops 1048576 | bytes 4096 | tf_op jit(solution)/shard_map/pallas_call | solution.py:108
  62.8 2.4 %copy-done.1 = f32[8,1296,128]{2,1,0:T(8,128)} copy-done((f32[8,1296,128]{2,1,0:T(8,128)}, f32[8,1296,128]{2,1,0:T(8,128)S(1)}, u32[]{:S(2)}) %copy-start.1) | copy-done | bytes 5308440
  65.2 54.1 %all_to_all.10.refs_2_ = bf16[16,256,512]{2,1,0:T(8,128)(2,1)S(1)} all-to-all(bf16[16,256,512]{2,1,0:T(8,128)(2,1)} %copy-done.2), channel_id=1, replica_groups=mesh['expert'=8,'shard'=16] {'shard'}, dimensions={0} | all-to-all | bytes 8388608 | tf_op jit(solution)/shard_map/all_to_all | solution.py:298
  119.3 7.3 %shard_map.51 = f32[8,1296,128]{2,1,0:T(8,128)S(1)} custom-call(s32[16,8]{1,0:T(8,128)S(1)} %copy.20.refs_0_, s32[16,8]{1,0:T(8,128)S(1)} %get-tuple-element.10.refs_1_, bf16[16,256,512]{2,1,0:T(8,128)(2,1)S(1)} %all_to_all.10.refs_2_), custom_call_target="tpu_custom_call" | custom-call | flops 1048576 | bytes 4096 | tf_op jit(solution)/shard_map/pallas_call | solution.py:108
  126.6 2.4 %copy-done = f32[8,1296,128]{2,1,0:T(8,128)} copy-done((f32[8,1296,128]{2,1,0:T(8,128)}, f32[8,1296,128]{2,1,0:T(8,128)S(1)}, u32[]{:S(2)}) %copy-start) | copy-done | bytes 5308440
  130.9 6.8 %collective-permute-done.refs_1_ = bf16[1296,128]{1,0:T(8,128)(2,1)S(1)} collective-permute-done((bf16[1296,128]{1,0:T(8,128)(2,1)S(1)}, bf16[1296,128]{1,0:T(8,128)(2,1)S(1)}, u32[]{:S(2)}, u32[]{:S(2)}) %collective-permute-start) | collective-permute-done | bytes 331808 | tf_op jit(solution)/shard_map/ppermute | solution.py:282
  138.8 5.6 %shard_map.49.refs_0_ = bf16[1280,128]{1,0:T(8,128)(2,1)S(1)} custom-call(f32[1296,128]{1,0:T(8,128)S(1)} %bitcast.19, bf16[1296,128]{1,0:T(8,128)(2,1)S(1)} %collective-permute-done.refs_1_), custom_call_target="tpu_custom_call" | custom-call | flops 1048576 | bytes 4096 | tf_op jit(solution)/shard_map/pallas_call | solution.py:212
  145.6 7.2 %collective-permute-done.1.refs_1_ = bf16[1280,128]{1,0:T(8,128)(2,1)S(1)} collective-permute-done((bf16[1280,128]{1,0:T(8,128)(2,1)S(1)}, bf16[1280,128]{1,0:T(8,128)(2,1)S(1)}, u32[]{:S(2)}, u32[]{:S(2)}) %collective-permute-start.1) | collective-permute-done | bytes 327712 | tf_op jit(solution)/shard_map/ppermute | solution.py:282
  156.9 6.6 %collective-permute-done.5.refs_5_ = bf16[1280,128]{1,0:T(8,128)(2,1)S(1)} collective-permute-done((bf16[1280,128]{1,0:T(8,128)(2,1)S(1)}, bf16[1280,128]{1,0:T(8,128)(2,1)S(1)}, u32[]{:S(2)}, u32[]{:S(2)}) %collective-permute-start.5) | collective-permute-done | bytes 327712 | tf_op jit(solution)/shard_map/ppermute | solution.py:282
  163.4 2.4 %collective-permute-start.7 = (bf16[1280,128]{1,0:T(8,128)(2,1)S(1)}, bf16[1280,128]{1,0:T(8,128)(2,1)S(1)}, u32[]{:S(2)}, u32[]{:S(2)}) collective-permute-start(bf16[1280,128]{1,0:T(8,128)(2,1)S(1)} %collective-permute-done.5.refs_5_), channel_id=1, source_target_pairs={{0,12},{1,13},{2,14},{3,15},{4,0},{5,1},{6,2},{7,3},{8,4},{9,5},{1... | collective-permute-start | bytes 983048 | tf_op jit(solution)/shard_map/ppermute | solution.py:282
  165.9 2.8 %collective-permute-done.4.refs_4_ = bf16[1280,128]{1,0:T(8,128)(2,1)S(1)} collective-permute-done((bf16[1280,128]{1,0:T(8,128)(2,1)S(1)}, bf16[1280,128]{1,0:T(8,128)(2,1)S(1)}, u32[]{:S(2)}, u32[]{:S(2)}) %collective-permute-start.4) | collective-permute-done | bytes 327712 | tf_op jit(solution)/shard_map/ppermute | solution.py:282
  168.7 3.5 %collective-permute-done.7.refs_7_ = bf16[1280,128]{1,0:T(8,128)(2,1)S(1)} collective-permute-done((bf16[1280,128]{1,0:T(8,128)(2,1)S(1)}, bf16[1280,128]{1,0:T(8,128)(2,1)S(1)}, u32[]{:S(2)}, u32[]{:S(2)}) %collective-permute-start.7) | collective-permute-done | bytes 327712 | tf_op jit(solution)/shard_map/ppermute | solution.py:282
  172.2 2.2 %copy-done.7 = bf16[1,4096,512]{2,1,0:T(8,128)(2,1)S(1)} copy-done((bf16[1,4096,512]{2,1,0:T(8,128)(2,1)S(1)}, bf16[1,4096,512]{2,1,0:T(8,128)(2,1)}, u32[]{:S(2)}) %copy-start.7) | copy-done | bytes 4194328
  174.4 5.3 %shard_map.50.a_ref = bf16[4096,512]{1,0:T(8,128)(2,1)S(1)} custom-call(s32[8]{0:T(128)S(1)} %stack.35.index_ref, bf16[1280,128]{1,0:T(8,128)(2,1)S(1)} %shard_map.49.refs_0_, bf16[1280,128]{1,0:T(8,128)(2,1)S(1)} %collective-permute-done.1.refs_1_, bf16[1280,128]{1,0:T(8,128)(2,1)S(1)} %collective-permute-done.2.refs_2_, ...), custom_call_target="tpu_custom_call" | custom-call | flops 1048576 | bytes 4096 | tf_op jit(solution)/shard_map/pallas_call | solution.py:243
  179.7 2.0 copy-done.3
  182.8 5.6 %shard_map.52.b_ref = bf16[512,512]{1,0:T(8,128)(2,1)S(1)} custom-call(f32[1296,128]{1,0:T(8,128)S(1)} %bitcast.20), custom_call_target="tpu_custom_call" | custom-call | flops 1048576 | bytes 4096 | tf_op jit(solution)/shard_map/pallas_call | solution.py:212
  188.4 2.2 %copy-done.4 = bf16[4096,512]{1,0:T(8,128)(2,1)S(1)} copy-done((bf16[4096,512]{1,0:T(8,128)(2,1)S(1)}, bf16[4096,512]{1,0:T(8,128)(2,1)}, u32[]{:S(2)}) %copy-start.4) | copy-done | bytes 4194328
  190.6 5.4 %shard_map.53 = bf16[4096,512]{1,0:T(8,128)(2,1)} custom-call(bf16[4096,512]{1,0:T(8,128)(2,1)S(1)} %copy-done.4, bf16[512,512]{1,0:T(8,128)(2,1)S(1)} %shard_map.52.b_ref), custom_call_target="tpu_custom_call" | custom-call | flops 1048576 | bytes 4096 | tf_op jit(solution)/shard_map/pallas_call | solution.py:267
  (44 shorter events, 14.3 us)
Async XLA Ops:
  7.3 1.6 copy-start.9
  8.9 0.7 copy-start.11
  9.6 11.6 %copy-start.12 = (s32[256,1]{0,1:T(1,128)S(1)}, s32[256,1]{0,1:T(1,128)}, u32[]{:S(2)}) copy-start(s32[256,1]{0,1:T(1,128)} %param.6) | copy-start | bytes 3076
  11.8 1.4 copy-start.5
  13.3 43.4 %all-to-all-start = ((bf16[16,144,512]{2,1,0:T(8,128)(2,1)}), bf16[16,144,512]{2,1,0:T(8,128)(2,1)S(1)}, u32[]{:S(2)}, u32[]{:S(2)}) async-start(bf16[16,144,512]{2,1,0:T(8,128)(2,1)} %copy-done.5), calls=%async_computation | async-start | bytes 4718592 | tf_op jit(solution)/shard_map/all_to_all | solution.py:296
  21.2 107.9 %reduce-scatter.3.cloned.1.call-start = ((), (), s32[]{:S(2)}) async-start(), calls=%async_computation.4 | async-start | bytes 5971968 | tf_op jit(solution)/shard_map/reduce_scatter | solution.py:286
  21.2 2.2 %copy-start.6 = (bf16[256,8192]{1,0:T(8,128)(2,1)S(1)}, bf16[256,8192]{1,0:T(8,128)(2,1)}, u32[]{:S(2)}) copy-start(bf16[256,8192]{1,0:T(8,128)(2,1)} %refs_2_.2) | copy-start | bytes 12582916
  27.7 2.0 copy-start.2
  62.8 2.4 %copy-start.1 = (f32[8,1296,128]{2,1,0:T(8,128)}, f32[8,1296,128]{2,1,0:T(8,128)S(1)}, u32[]{:S(2)}) copy-start(f32[8,1296,128]{2,1,0:T(8,128)S(1)} %shard_map.48) | copy-start | bytes 15925252
  65.2 116.5 %reduce-scatter.5.cloned.1.call-start = ((), (), s32[]{:S(2)}) async-start(), calls=%async_computation.5 | async-start | bytes 5971968 | tf_op jit(solution)/shard_map/reduce_scatter | solution.py:286
  126.6 2.4 %copy-start = (f32[8,1296,128]{2,1,0:T(8,128)}, f32[8,1296,128]{2,1,0:T(8,128)S(1)}, u32[]{:S(2)}) copy-start(f32[8,1296,128]{2,1,0:T(8,128)S(1)} %shard_map.51) | copy-start | bytes 15925252
  130.2 7.5 %collective-permute-start = (bf16[1296,128]{1,0:T(8,128)(2,1)S(1)}, bf16[1296,128]{1,0:T(8,128)(2,1)S(1)}, u32[]{:S(2)}, u32[]{:S(2)}) collective-permute-start(bf16[1296,128]{1,0:T(8,128)(2,1)S(1)} %bitcast_convert_fusion), channel_id=1, source_target_pairs={{0,1},{1,0},{2,3},{3,2},{4,5},{5,4},{6,7},{7,6},{8,9},{9,8},{10,11... | collective-permute-start | bytes 995336 | tf_op jit(solution)/shard_map/ppermute | solution.py:282
  137.7 1.1 copy-start.8
  144.4 8.4 %collective-permute-start.1 = (bf16[1280,128]{1,0:T(8,128)(2,1)S(1)}, bf16[1280,128]{1,0:T(8,128)(2,1)S(1)}, u32[]{:S(2)}, u32[]{:S(2)}) collective-permute-start(bf16[1280,128]{1,0:T(8,128)(2,1)S(1)} %shard_map.49.refs_0_), channel_id=1, source_target_pairs={{0,3},{1,2},{2,1},{3,0},{4,7},{5,6},{6,5},{7,4},{8,11},{9,10},{10,... | collective-permute-start | bytes 983048 | tf_op jit(solution)/shard_map/ppermute | solution.py:282
  145.2 10.8 %collective-permute-start.2 = (bf16[1280,128]{1,0:T(8,128)(2,1)S(1)}, bf16[1280,128]{1,0:T(8,128)(2,1)S(1)}, u32[]{:S(2)}, u32[]{:S(2)}) collective-permute-start(bf16[1280,128]{1,0:T(8,128)(2,1)S(1)} %shard_map.49.refs_0_), channel_id=1, source_target_pairs={{0,4},{1,5},{2,6},{3,7},{4,8},{5,9},{6,10},{7,11},{8,12},{9,13},{1... | collective-permute-start | bytes 983048 | tf_op jit(solution)/shard_map/ppermute | solution.py:282
  152.8 10.7 %collective-permute-start.5 = (bf16[1280,128]{1,0:T(8,128)(2,1)S(1)}, bf16[1280,128]{1,0:T(8,128)(2,1)S(1)}, u32[]{:S(2)}, u32[]{:S(2)}) collective-permute-start(bf16[1280,128]{1,0:T(8,128)(2,1)S(1)} %collective-permute-done.1.refs_1_), channel_id=1, source_target_pairs={{0,12},{1,13},{2,14},{3,15},{4,0},{5,1},{6,2},{7,3},{8,4},{9,5},{1... | collective-permute-start | bytes 983048 | tf_op jit(solution)/shard_map/ppermute | solution.py:282
  154.0 14.7 %collective-permute-start.4 = (bf16[1280,128]{1,0:T(8,128)(2,1)S(1)}, bf16[1280,128]{1,0:T(8,128)(2,1)S(1)}, u32[]{:S(2)}, u32[]{:S(2)}) collective-permute-start(bf16[1280,128]{1,0:T(8,128)(2,1)S(1)} %shard_map.49.refs_0_), channel_id=1, source_target_pairs={{0,12},{1,13},{2,14},{3,15},{4,0},{5,1},{6,2},{7,3},{8,4},{9,5},{1... | collective-permute-start | bytes 983048 | tf_op jit(solution)/shard_map/ppermute | solution.py:282
  154.6 14.1 %collective-permute-start.3 = (bf16[1280,128]{1,0:T(8,128)(2,1)S(1)}, bf16[1280,128]{1,0:T(8,128)(2,1)S(1)}, u32[]{:S(2)}, u32[]{:S(2)}) collective-permute-start(bf16[1280,128]{1,0:T(8,128)(2,1)S(1)} %collective-permute-done.1.refs_1_), channel_id=1, source_target_pairs={{0,4},{1,5},{2,6},{3,7},{4,8},{5,9},{6,10},{7,11},{8,12},{9,13},{1... | collective-permute-start | bytes 983048 | tf_op jit(solution)/shard_map/ppermute | solution.py:282
  156.0 12.7 %collective-permute-start.6 = (bf16[1280,128]{1,0:T(8,128)(2,1)S(1)}, bf16[1280,128]{1,0:T(8,128)(2,1)S(1)}, u32[]{:S(2)}, u32[]{:S(2)}) collective-permute-start(bf16[1280,128]{1,0:T(8,128)(2,1)S(1)} %collective-permute-done.2.refs_2_), channel_id=1, source_target_pairs={{0,4},{1,5},{2,6},{3,7},{4,8},{5,9},{6,10},{7,11},{8,12},{9,13},{1... | collective-permute-start | bytes 983048 | tf_op jit(solution)/shard_map/ppermute | solution.py:282
  163.4 8.8 %collective-permute-start.7 = (bf16[1280,128]{1,0:T(8,128)(2,1)S(1)}, bf16[1280,128]{1,0:T(8,128)(2,1)S(1)}, u32[]{:S(2)}, u32[]{:S(2)}) collective-permute-start(bf16[1280,128]{1,0:T(8,128)(2,1)S(1)} %collective-permute-done.5.refs_5_), channel_id=1, source_target_pairs={{0,12},{1,13},{2,14},{3,15},{4,0},{5,1},{6,2},{7,3},{8,4},{9,5},{1... | collective-permute-start | bytes 983048 | tf_op jit(solution)/shard_map/ppermute | solution.py:282
  172.2 2.2 %copy-start.7 = (bf16[1,4096,512]{2,1,0:T(8,128)(2,1)S(1)}, bf16[1,4096,512]{2,1,0:T(8,128)(2,1)}, u32[]{:S(2)}) copy-start(bf16[1,4096,512]{2,1,0:T(8,128)(2,1)} %param.7) | copy-start | bytes 12582916
  179.7 2.0 copy-start.3
  181.7 1.1 copy-start.10
  188.4 2.2 %copy-start.4 = (bf16[4096,512]{1,0:T(8,128)(2,1)S(1)}, bf16[4096,512]{1,0:T(8,128)(2,1)}, u32[]{:S(2)}) copy-start(bf16[4096,512]{1,0:T(8,128)(2,1)} %copy-done.3) | copy-start | bytes 12582916
Sparse Core Ops, SparseCore 0:
  65.3 34.8 reduce-scatter.2
  129.1 34.0 reduce-scatter.4

commit v3 on v2

--- a/solution.py
+++ b/solution.py
@@ -14,21 +14,22 @@
 SLOT_DEV = 256
 NS_STEPS = 8
 DAMPING = 0.1
-VMEM_LIMIT = 20 * 1024 * 1024
+MIB = 1024 * 1024
 
 TILES = [(i, j) for i in range(4) for j in range(i, 4)]
 PACKED = len(TILES) * TILE
 NOTE = 16
+OUT_ROWS = SLOT_DEV // 2 + NOTE
 CAP = 64
 
 BRIEF = pl.CostEstimate(flops=1 << 20, bytes_accessed=1 << 12, transcendentals=0)
 
 
-def params():
-    return pltpu.CompilerParams(vmem_limit_bytes=VMEM_LIMIT)
-
-
-def route_kernel(noted, col_ref, row_ref, x_ref, o_ref, perm):
+def params(mib):
+    return pltpu.CompilerParams(vmem_limit_bytes=mib * MIB)
+
+
+def route_kernel(col_ref, row_ref, inputs_ref, grads_ref, o_ref, halves, sorts):
     n = SLOT_DEV
 
     @pl.when(pl.program_id(0) == 0)
@@ -38,44 +39,45 @@
         earlier = col_ref[...] * n + sub < row_ref[...] * n + lane
         place = jnp.sum(earlier.astype(jnp.float32), axis=0, keepdims=True)
         place = place.astype(jnp.int32)
-        if noted:
-            place = (place >> 1) + (place & 1) * (n // 2)
-        perm[...] = (sub == place).astype(jnp.float32).astype(jnp.bfloat16)
-
-    moved = jnp.dot(perm[...], x_ref[...], preferred_element_type=jnp.float32)
-    moved = moved.astype(jnp.bfloat16)
-    if noted:
-        lane = lax.broadcasted_iota(jnp.int32, (n, BLK), 1)
-        counts = jnp.sum((col_ref[...] == lane).astype(jnp.float32), axis=0, keepdims=True)
-        counts = jnp.broadcast_to(counts, (NOTE, BLK)).astype(jnp.bfloat16)
-        for half in range(2):
-            o_ref[half, : n // 2, :] = moved[half * (n // 2) : (half + 1) * (n // 2)]
-            o_ref[half, n // 2 :, :] = counts
-    else:
-        o_ref[0] = moved
-
-
-def route(x, ids_col, ids_row, noted):
-    blocks = x.shape[1] // BLK
-    block = (2, SLOT_DEV // 2 + NOTE, BLK) if noted else (1, SLOT_DEV, BLK)
+        sorts[...] = (sub == place).astype(jnp.float32).astype(jnp.bfloat16)
+        place = (place >> 1) + (place & 1) * (n // 2)
+        halves[...] = (sub == place).astype(jnp.float32).astype(jnp.bfloat16)
+
+    def moved(order, x):
+        return jnp.dot(order[...], x, preferred_element_type=jnp.float32).astype(jnp.bfloat16)
+
+    lane = lax.broadcasted_iota(jnp.int32, (n, BLK), 1)
+    counts = jnp.sum((col_ref[...] == lane).astype(jnp.float32), axis=0, keepdims=True)
+    counts = jnp.broadcast_to(counts, (NOTE, BLK)).astype(jnp.bfloat16)
+    rows = moved(halves, inputs_ref[...])
+    for half in range(2):
+        o_ref[half, : n // 2, :] = rows[half * (n // 2) : (half + 1) * (n // 2)]
+        o_ref[half, n // 2 : OUT_ROWS, :] = counts
+        o_ref[half, OUT_ROWS:, :] = moved(sorts, grads_ref[:, half * BLK : (half + 1) * BLK])
+
+
+def route(inputs, grads, ids_col, ids_row):
+    pairs = inputs.shape[1] // BLK
+    rows = OUT_ROWS + SLOT_DEV
     return pl.pallas_call(
-        lambda *refs: route_kernel(noted, *refs),
-        grid=(blocks,),
+        route_kernel,
+        grid=(pairs,),
         in_specs=[
             pl.BlockSpec((SLOT_DEV, 1), lambda b: (0, 0)),
             pl.BlockSpec((1, SLOT_DEV), lambda b: (0, 0)),
             pl.BlockSpec((SLOT_DEV, BLK), lambda b: (0, b)),
+            pl.BlockSpec((SLOT_DEV, 2 * BLK), lambda b: (0, b)),
         ],
-        out_specs=pl.BlockSpec(block, lambda b: (b, 0, 0)),
-        out_shape=jax.ShapeDtypeStruct((blocks * block[0],) + block[1:], jnp.bfloat16),
-        scratch_shapes=[pltpu.VMEM((SLOT_DEV, SLOT_DEV), jnp.bfloat16)],
-        compiler_params=params(),
+        out_specs=pl.BlockSpec((2, rows, BLK), lambda b: (b, 0, 0)),
+        out_shape=jax.ShapeDtypeStruct((2 * pairs, rows, BLK), jnp.bfloat16),
+        scratch_shapes=[pltpu.VMEM((SLOT_DEV, SLOT_DEV), jnp.bfloat16)] * 2,
+        compiler_params=params(20),
         cost_estimate=BRIEF,
-    )(ids_col, ids_row, x)
-
-
-def gram_kernel(rows, window, start_ref, end_ref, x_ref, o_ref, picked):
-    e = pl.program_id(0)
+    )(ids_col, ids_row, inputs, grads)
+
+
+def gram_kernel(first, offset, rows, window, start_ref, end_ref, x_ref, o_ref, picked):
+    e = pl.program_id(0) + first
     place = lax.broadcasted_iota(jnp.int32, (window, BLK), 0)
     total = 0
     for j in range(x_ref.shape[0]):
@@ -83,7 +85,7 @@
         end = end_ref[j, e]
         total = total + (end - start)
         base = pl.multiple_of(jnp.minimum(start // 16 * 16, rows - window), 16)
-        part = x_ref[j, pl.ds(base, window), :]
+        part = x_ref[j, pl.ds(offset + base, window), :]
         keep = (place >= start - base) & (place < end - base)
         picked[pl.ds(j * window, window), :] = jnp.where(keep, part, jnp.zeros_like(part))
     left = picked[:, :HALF]
@@ -101,21 +103,21 @@
     o_ref[0, pl.ds(PACKED + 8, 8), :] = jnp.full((8, TILE), total & 31, jnp.int32).astype(jnp.float32)
 
 
-def gram(x, start, end, rows, most):
+def gram(x, start, end, first, offset, rows, most):
     sources = x.shape[0]
     height = PACKED + NOTE
     window = most + 16
     return pl.pallas_call(
-        lambda *refs: gram_kernel(rows, window, *refs),
+        lambda *refs: gram_kernel(first, offset, rows, window, *refs),
         grid_spec=pltpu.PrefetchScalarGridSpec(
             num_scalar_prefetch=2,
-            grid=(EXPERTS,),
+            grid=(4,),
             in_specs=[pl.BlockSpec(memory_space=pltpu.VMEM)],
             out_specs=pl.BlockSpec((1, height, TILE), lambda e, s, t: (e, 0, 0)),
             scratch_shapes=[pltpu.VMEM((sources * window, BLK), jnp.bfloat16)],
         ),
-        out_shape=jax.ShapeDtypeStruct((EXPERTS, height, TILE), jnp.float32),
-        compiler_params=params(),
+        out_shape=jax.ShapeDtypeStruct((4, height, TILE), jnp.float32),
+        compiler_params=params(20),
         cost_estimate=BRIEF,
     )(start, end, x)
 
@@ -216,99 +218,152 @@
         out_shape=jax.ShapeDtypeStruct((PACKED, TILE) if packed else (BLK, BLK), jnp.bfloat16),
         scratch_shapes=[pltpu.VMEM((HALF, BLK), jnp.float32), pltpu.VMEM((HALF, HALF), jnp.float32)] * 2
         + [pltpu.VMEM((BLK, BLK), jnp.bfloat16)] * 2,
-        compiler_params=params(),
+        compiler_params=params(20),
         cost_estimate=BRIEF,
     )(*grams)
 
 
-def left_kernel(index_ref, *refs):
-    packed, w_ref, o_ref, block = refs[:-3], refs[-3], refs[-2], refs[-1]
-    for k, inverse in enumerate(packed):
-
-        @pl.when(pl.program_id(0) == k)
-        def _(inverse=inverse):
-            for n, (i, j) in enumerate(TILES):
-                tile = inverse[pl.ds(n * TILE, TILE), :]
-                block[pl.ds(i * TILE, TILE), pl.ds(j * TILE, TILE)] = tile
-                if i != j:
-                    block[pl.ds(j * TILE, TILE), pl.ds(i * TILE, TILE)] = tile.T
-
-    o_ref[...] = jnp.dot(
-        block[...], w_ref[...], preferred_element_type=jnp.float32
-    ).astype(jnp.bfloat16)
+def unpack(packed, block):
+    for n, (i, j) in enumerate(TILES):
+        tile = packed[pl.ds(n * TILE, TILE), :]
+        block[pl.ds(i * TILE, TILE), pl.ds(j * TILE, TILE)] = tile
+        if i != j:
+            block[pl.ds(j * TILE, TILE), pl.ds(i * TILE, TILE)] = tile.T
+
+
+def left_kernel(count, index_ref, *refs):
+    packed, w_hbm, o_ref, w_ref, block, w_sem = refs[:count], *refs[count:]
+
+    def fetch(k):
+        rows = pl.ds(pl.multiple_of(index_ref[k] * BLK, BLK), BLK)
+        return pltpu.make_async_copy(w_hbm.at[rows], w_ref.at[k], w_sem.at[k])
+
+    for k in range(count):
+        fetch(k).start()
+    for k in range(count):
+        unpack(packed[k], block.at[k])
+    for k in range(count):
+        fetch(k).wait()
+        left = jnp.dot(block[k], w_ref[k], preferred_element_type=jnp.float32)
+        o_ref[k] = left.astype(jnp.bfloat16)
 
 
 def left_product(index, packed, grad):
-    blocks = len(packed)
+    count = len(packed)
+    vmem = pl.BlockSpec(memory_space=pltpu.VMEM)
     return pl.pallas_call(
-        left_kernel,
-        grid_spec=pltpu.PrefetchScalarGridSpec(
-            num_scalar_prefetch=1,
-            grid=(blocks,),
-            in_specs=[pl.BlockSpec((PACKED, TILE), lambda n, s: (0, 0))] * blocks
-            + [pl.BlockSpec((BLK, BLK), lambda n, s: (s[n], 0))],
-            out_specs=pl.BlockSpec((BLK, BLK), lambda n, s: (s[n], 0)),
-            scratch_shapes=[pltpu.VMEM((BLK, BLK), jnp.bfloat16)],
-        ),
-        out_shape=jax.ShapeDtypeStruct((blocks * BLK, BLK), jnp.bfloat16),
-        compiler_params=params(),
+        lambda *refs: left_kernel(count, *refs),
+        in_specs=[pl.BlockSpec(memory_space=pltpu.SMEM)]
+        + [vmem] * count
+        + [pl.BlockSpec(memory_space=pltpu.HBM)],
+        out_specs=vmem,
+        out_shape=jax.ShapeDtypeStruct((count, BLK, BLK), jnp.bfloat16),
+        scratch_shapes=[pltpu.VMEM((count, BLK, BLK), jnp.bfloat16)] * 2
+        + [pltpu.SemaphoreType.DMA((count,))],
+        compiler_params=params(20),
         cost_estimate=BRIEF,
     )(index, *packed, grad)
 
 
-def right_kernel(a_ref, b_ref, o_ref):
-    o_ref[...] = jnp.dot(
-        a_ref[...], b_ref[...], preferred_element_type=jnp.float32
-    ).astype(jnp.bfloat16)
-
-
-def right_product(a, b):
-    blocks = a.shape[0] // BLK
+def apply_kernel(count, index_ref, *refs):
+    packed, (done_ref, w_hbm, right_ref, o_hbm) = refs[:count], refs[count : count + 4]
+    w_ref, o_ref, block, w_sem, o_sem = refs[count + 4 :]
+    first = done_ref.shape[0]
+
+    def rows(k):
+        return pl.ds(pl.multiple_of(index_ref[k] * BLK, BLK), BLK)
+
+    def fetch(k):
+        return pltpu.make_async_copy(w_hbm.at[rows(first + k)], w_ref.at[k], w_sem.at[k])
+
+    def store(k):
+        return pltpu.make_async_copy(o_ref.at[k], o_hbm.at[rows(k)], o_sem.at[k])
+
+    def finish(k, left):
+        o_ref[k] = jnp.dot(left, right_ref[...], preferred_element_type=jnp.float32).astype(jnp.bfloat16)
+        store(k).start()
+
+    for k in range(count):
+        fetch(k).start()
+    for k in range(first):
+        finish(k, done_ref[k])
+    for k in range(count):
+        unpack(packed[k], block.at[k])
+    for k in range(count):
+        fetch(k).wait()
+        left = jnp.dot(block[k], w_ref[k], preferred_element_type=jnp.float32)
+        finish(first + k, left.astype(jnp.bfloat16))
+    for k in range(first + count):
+        store(k).wait()
+
+
+def apply(index, done, packed, grad, right):
+    count = len(packed)
+    blocks = done.shape[0] + count
+    vmem, hbm = pl.BlockSpec(memory_space=pltpu.VMEM), pl.BlockSpec(memory_space=pltpu.HBM)
     return pl.pallas_call(
-        right_kernel,
-        grid=(blocks,),
-        in_specs=[
-            pl.BlockSpec((BLK, BLK), lambda n: (n, 0)),
-            pl.BlockSpec((BLK, BLK), lambda n: (0, 0)),
+        lambda *refs: apply_kernel(count, *refs),
+        in_specs=[pl.BlockSpec(memory_space=pltpu.SMEM)] + [vmem] * count + [vmem, hbm, vmem],
+        out_specs=hbm,
+        out_shape=jax.ShapeDtypeStruct((blocks * BLK, BLK), jnp.bfloat16),
+        scratch_shapes=[
+            pltpu.VMEM((count, BLK, BLK), jnp.bfloat16),
+            pltpu.VMEM((blocks, BLK, BLK), jnp.bfloat16),
+            pltpu.VMEM((count, BLK, BLK), jnp.bfloat16),
+            pltpu.SemaphoreType.DMA((count,)),
+            pltpu.SemaphoreType.DMA((blocks,)),
         ],
-        out_specs=pl.BlockSpec((BLK, BLK), lambda n: (n, 0)),
-        out_shape=jax.ShapeDtypeStruct((blocks * BLK, BLK), jnp.bfloat16),
-        compiler_params=params(),
+        compiler_params=params(50),
         cost_estimate=BRIEF,
-    )(a, b)
+    )(index, *packed, done, grad, right)
 
 
 def send(x, axis, target):
     return lax.ppermute(x, axis, [(i, target(i)) for i in range(lax.axis_size(axis))])
 
 
-def sum_over_group(grams):
-    return lax.psum_scatter(grams, "expert", scatter_dimension=0, tiled=True)[0]
+def sum_over_group(grams_of):
+    got = send(grams_of(0), "expert", lambda i: i ^ 1)
+    mine = grams_of(4)
+    parts = [mine[0] + got[0]]
+    for k in range(1, 4):
+        part = (mine[k] + got[k]).astype(jnp.bfloat16)
+        parts.append(send(part, "expert", lambda i: (i + 2 * k) % EXPERTS))
+    return parts
 
 
 def per_device(slot_inputs, slot_grads, slot_expert, weight_grad):
     shard_pos = lax.axis_index("shard")
+    group_pos = lax.axis_index("expert")
+    parity, group = group_pos & 1, group_pos >> 1
     odd = shard_pos & 1
     ids_row = slot_expert.reshape(1, SLOT_DEV)
-    sent_act = route(slot_inputs, slot_expert, ids_row, True)
-    sent_out = route(slot_grads, slot_expert, ids_row, False)
-
-    got_act = lax.all_to_all(sent_act, "shard", 0, 0, tiled=True)
-    sent_out, got_act = lax.optimization_barrier((sent_out, got_act))
-    got_out = lax.all_to_all(sent_out, "shard", 0, 0, tiled=True)
-
-    counts = got_act[:, SLOT_DEV // 2, :EXPERTS].astype(jnp.int32)
+    sent = route(slot_inputs, slot_grads, slot_expert, ids_row)
+    sent, odd, parity, group, shard_pos = lax.optimization_barrier(
+        (sent, odd, parity, group, shard_pos)
+    )
+    got = lax.all_to_all(sent, "shard", 0, 0, tiled=True)
+    got, odd, parity, group, shard_pos, weight_grad = lax.optimization_barrier(
+        (got, odd, parity, group, shard_pos, weight_grad)
+    )
+
+    counts = got[:, SLOT_DEV // 2, :EXPERTS].astype(jnp.int32)
     label = jnp.arange(EXPERTS, dtype=jnp.int32)
-    before = (label[:, None] < label[None, :]).astype(jnp.int32)
+    order = 2 * ((group + label) & 3) + jnp.where(label < 4, 1 - parity, parity)
+    before = (label[:, None] < order[None, :]).astype(jnp.int32)
+    same = (label[:, None] == order[None, :]).astype(jnp.int32)
     start = jnp.sum(counts[:, :, None] * before[None], axis=1)
-    end = start + counts
-
-    act = gram(got_act, (start + 1 - odd) >> 1, (end + 1 - odd) >> 1, SLOT_DEV // 2, CAP // 2)
-    act = sum_over_group(act)
-    out = sum_over_group(gram(got_out, start, end, SLOT_DEV, CAP))
+    end = start + jnp.sum(counts[:, :, None] * same[None], axis=1)
+
+    own_start, own_end = (start + 1 - odd) >> 1, (end + 1 - odd) >> 1
+    act_parts = sum_over_group(
+        lambda first: gram(got, own_start, own_end, first, 0, SLOT_DEV // 2, CAP // 2)
+    )
+    act = act_parts[0]
+    for part in act_parts[1:]:
+        act = act + part.astype(jnp.float32)
     other = send(act.astype(jnp.bfloat16), "shard", lambda i: i ^ 1)
     act_inverse = newton(True, act, other)
-    out_inverse = newton(False, out)
 
     def up(i):
         return (i + 4) % 16
@@ -324,12 +379,16 @@
     own_far = send(own_below, "shard", up)
     across_far = send(across_above, "shard", down)
     z, side = shard_pos >> 2, shard_pos >> 1 & 1
-    inverses = [act_inverse, across, own_below, across_below, own_above, across_above, own_far, across_far]
-    index = []
-    for step in (0, -1, 1, 2):
-        index += [2 * ((z + step) & 3) + side, 2 * ((z + step) & 3) + 1 - side]
-    left = left_product(jnp.stack(index).astype(jnp.int32), inverses, weight_grad[0])
-    return right_product(left, out_inverse)[None]
+    early = [act_inverse, across, own_below, own_above]
+    late = [across_below, across_above, own_far, across_far]
+    places = [(0, 0), (0, 1), (-1, 0), (1, 0), (-1, 1), (1, 1), (2, 0), (2, 1)]
+    index = [2 * ((z + step) & 3) + (side ^ other_side) for step, other_side in places]
+    index = jnp.stack(index).astype(jnp.int32)
+
+    out_parts = sum_over_group(lambda first: gram(got, start, end, first, OUT_ROWS, SLOT_DEV, CAP))
+    done = left_product(index, early, weight_grad[0])
+    out_inverse = newton(False, *out_parts)
+    return apply(index, done, late, weight_grad[0], out_inverse)[None]
 
 
 def solution(mesh):

time: 204 us -> 186 us (0.912)
  blocking collectives: 54.1 us -> 83.9 us
  waiting for transfers between devices: 53.8 us -> 33.9 us
  between operations: 13.6 us -> 0.33 us
  local copies, waits for them, and re-layouts: 22.2 us -> 10.6 us
  starting transfers between devices: 16.3 us -> 13.1 us
    all_to_all x1, blocking collectives: 54.1 us -> 83.9 us  [per_device(): got = lax.all_to_all(sent, 'shard', 0, 0, tiled=True)]
    all_to_all x1 -> x0, waiting for transfers between devices: 26.9 us -> none  [per_device(): got_act = lax.all_to_all(sent_act, 'shard', 0, 0, tiled=True)]
    unnamed x27 -> x11, local copies, waits for them, and re-layouts: 22 us -> 10.3 us
    all_to_all x1 -> x0, starting transfers between devices: 7.87 us -> none  [per_device(): got_act = lax.all_to_all(sent_act, 'shard', 0, 0, tiled=True)]
    ppermute x8 -> x16, waiting for transfers between devices: 26.9 us -> 33.9 us  [send(): lax.ppermute(x, axis, [(i, target(i)) for i in range(lax.axis_size(axis))])]
    ppermute x8 -> x16, starting transfers between devices: 8.36 us -> 13.1 us  [send(): lax.ppermute(x, axis, [(i, target(i)) for i in range(lax.axis_size(axis))])]
    pallas_call x6 -> x7, Pallas kernels: 30.3 us -> 28.7 us  [the longest x4 14.8 us: gram(): pl.pallas_call(lambda *refs: gram_kernel(first, offset, rows, window, *re...]
  transfers between devices with their start and end apart: 11 -> 16, of which waited for: 6 -> 8; matrix products, arithmetic and copies ran while one was open for 1% -> 1% of each run, Pallas kernels for 11% -> 14%
where the time goes in v3:
time: 186 us; the launch traced here: 184 us
  blocking collectives  83.9 us (45%)
  Pallas kernels  40.1 us (22%)
  waiting for transfers between devices  33.9 us (18%)
  starting transfers between devices  13.1 us (7%)
  local copies, waits for them, and re-layouts  10.6 us (6%)
  other arithmetic  2.27 us (1%)
    all_to_all x1, blocking collectives, per_device(): got = lax.all_to_all(sent, 'shard', 0, 0, tiled=True)  83.9 us
    ppermute x16, waiting for transfers between devices, send(): lax.ppermute(x, axis, [(i, target(i)) for i in range(lax.axis_size(axis))])  33.9 us
    pallas_call x4, Pallas kernels, gram(): pl.pallas_call(lambda *refs: gram_kernel(first, offset, rows, window, *re...  14.8 us
    ppermute x16, starting transfers between devices, send(): lax.ppermute(x, axis, [(i, target(i)) for i in range(lax.axis_size(axis))])  13.1 us
    pallas_call x2, Pallas kernels, newton(): pl.pallas_call(lambda *refs: newton_kernel(packed, *refs), in_specs=[pl.B...  11.3 us
    unnamed x11, local copies, waits for them, and re-layouts  10.3 us
    pallas_call x1, Pallas kernels, apply(): pl.pallas_call(lambda *refs: apply_kernel(count, *refs), in_specs=[pl.Blo...  6.77 us
  transfers between devices with their start and end apart: 16, of which 8 were waited for; matrix products, arithmetic and copies ran while one was open for 1% of the time, Pallas kernels for 14%

profile of v3, /device:TPU:24, one launch (start us, length us, event | category | flops | bytes accessed | tf_op | source)
XLA Modules:
  0.0 184.2 jit_solution(6846186787210835226)
XLA Ops:
  0.8 2.2 %copy-done.2 = bf16[256,8192]{1,0:T(8,128)(2,1)S(1)} copy-done((bf16[256,8192]{1,0:T(8,128)(2,1)S(1)}, bf16[256,8192]{1,0:T(8,128)(2,1)}, u32[]{:S(2)}) %copy-start.2) | copy-done | bytes 4194328
  3.0 1.6 copy-done.3
  5.3 3.7 %shard_map.46 = bf16[16,400,512]{2,1,0:T(8,128)(2,1)S(1)} custom-call(s32[256,1]{1,0:T(8,128)S(1)} %copy.15.col_ref, s32[1,256]{1,0:T(1,128)S(1)} %bitcast.37, bf16[256,4096]{1,0:T(8,128)(2,1)S(1)} %copy-done.3, bf16[256,8192]{1,0:T(8,128)(2,1)S(1)} %copy-done.2), custom_call_target="tpu_custom_call" | custom-call | flops 1048576 | bytes 4096 | tf_op jit(solution)/shard_map/pallas_call | solution.py:62
  9.0 83.9 %all_to_all.5.refs_2_ = bf16[16,400,512]{2,1,0:T(8,128)(2,1)} all-to-all(bf16[16,400,512]{2,1,0:T(8,128)(2,1)S(1)} %shard_map.46), channel_id=1, replica_groups=mesh['expert'=8,'shard'=16] {'shard'}, dimensions={0} | all-to-all | bytes 13107200 | tf_op jit(solution)/shard_map/all_to_all | solution.py:345
  94.0 2.9 %copy-done = bf16[16,400,512]{2,1,0:T(8,128)(2,1)S(1)} copy-done((bf16[16,400,512]{2,1,0:T(8,128)(2,1)S(1)}, bf16[16,400,512]{2,1,0:T(8,128)(2,1)}, u32[]{:S(2)}) %copy-start) | copy-done | bytes 6553624
  96.9 3.3 %shard_map.48 = f32[4,1296,128]{2,1,0:T(8,128)S(1)} custom-call(s32[16,8]{1,0:T(8,128)S(1)} %get-tuple-element.40.refs_0_, s32[16,8]{1,0:T(8,128)S(1)} %get-tuple-element.31.refs_1_, bf16[16,400,512]{2,1,0:T(8,128)(2,1)S(1)} %copy-done), custom_call_target="tpu_custom_call" | custom-call | flops 1048576 | bytes 4096 | tf_op jit(solution)/shard_map/pallas_call | solution.py:110
  100.3 4.0 %shard_map.52 = f32[4,1296,128]{2,1,0:T(8,128)S(1)} custom-call(s32[16,8]{1,0:T(8,128)S(1)} %copy.17.refs_0_, s32[16,8]{1,0:T(8,128)S(1)} %get-tuple-element.32.refs_1_, bf16[16,400,512]{2,1,0:T(8,128)(2,1)S(1)} %copy-done), custom_call_target="tpu_custom_call" | custom-call | flops 1048576 | bytes 4096 | tf_op jit(solution)/shard_map/pallas_call | solution.py:110
  104.9 3.3 %shard_map.47 = f32[4,1296,128]{2,1,0:T(8,128)S(1)} custom-call(s32[16,8]{1,0:T(8,128)S(1)} %get-tuple-element.40.refs_0_, s32[16,8]{1,0:T(8,128)S(1)} %get-tuple-element.31.refs_1_, bf16[16,400,512]{2,1,0:T(8,128)(2,1)S(1)} %copy-done), custom_call_target="tpu_custom_call" | custom-call | flops 1048576 | bytes 4096 | tf_op jit(solution)/shard_map/pallas_call | solution.py:110
  108.8 2.6 %collective-permute-start.2 = (bf16[1296,128]{1,0:T(8,128)(2,1)S(1)}, bf16[1296,128]{1,0:T(8,128)(2,1)S(1)}, u32[]{:S(2)}, u32[]{:S(2)}) collective-permute-start(bf16[1296,128]{1,0:T(8,128)(2,1)S(1)} %get-tuple-element.39), channel_id=1, source_target_pairs={{0,64},{16,80},{32,96},{48,112},{64,0},{80,16},{96,32},{112,48},{1... | collective-permute-start | bytes 995336 | tf_op jit(solution)/shard_map/ppermute | solution.py:322
  111.4 7.8 %collective-permute-done.1 = bf16[1296,128]{1,0:T(8,128)(2,1)S(1)} collective-permute-done((bf16[1296,128]{1,0:T(8,128)(2,1)S(1)}, bf16[1296,128]{1,0:T(8,128)(2,1)S(1)}, u32[]{:S(2)}, u32[]{:S(2)}) %collective-permute-start.1) | collective-permute-done | bytes 331808 | tf_op jit(solution)/shard_map/ppermute | solution.py:322
  119.2 1.8 collective-permute-done.2
  121.0 6.0 %collective-permute-done.3 = bf16[1296,128]{1,0:T(8,128)(2,1)S(1)} collective-permute-done((bf16[1296,128]{1,0:T(8,128)(2,1)S(1)}, bf16[1296,128]{1,0:T(8,128)(2,1)S(1)}, u32[]{:S(2)}, u32[]{:S(2)}) %collective-permute-start.3) | collective-permute-done | bytes 331808 | tf_op jit(solution)/shard_map/ppermute | solution.py:322
  127.8 4.1 %shard_map.51 = f32[4,1296,128]{2,1,0:T(8,128)S(1)} custom-call(s32[16,8]{1,0:T(8,128)S(1)} %copy.17.refs_0_, s32[16,8]{1,0:T(8,128)S(1)} %get-tuple-element.32.refs_1_, bf16[16,400,512]{2,1,0:T(8,128)(2,1)S(1)} %copy-done), custom_call_target="tpu_custom_call" | custom-call | flops 1048576 | bytes 4096 | tf_op jit(solution)/shard_map/pallas_call | solution.py:110
  131.9 5.1 %collective-permute-done.4.refs_1_ = bf16[1296,128]{1,0:T(8,128)(2,1)S(1)} collective-permute-done((bf16[1296,128]{1,0:T(8,128)(2,1)S(1)}, bf16[1296,128]{1,0:T(8,128)(2,1)S(1)}, u32[]{:S(2)}, u32[]{:S(2)}) %collective-permute-start.4) | collective-permute-done | bytes 331808 | tf_op jit(solution)/shard_map/ppermute | solution.py:322
  137.0 5.6 %shard_map.49.refs_1_ = bf16[1280,128]{1,0:T(8,128)(2,1)S(1)} custom-call(f32[1296,128]{1,0:T(8,128)S(1)} %get-tuple-element.30.refs_0_, bf16[1296,128]{1,0:T(8,128)(2,1)S(1)} %collective-permute-done.4.refs_1_), custom_call_target="tpu_custom_call" | custom-call | flops 1048576 | bytes 4096 | tf_op jit(solution)/shard_map/pallas_call | solution.py:214
  144.7 1.7 collective-permute-start.14
  146.9 5.9 %collective-permute-done.5.refs_2_ = bf16[1280,128]{1,0:T(8,128)(2,1)} collective-permute-done((bf16[1280,128]{1,0:T(8,128)(2,1)S(1)}, bf16[1280,128]{1,0:T(8,128)(2,1)}, u32[]{:S(2)}, u32[]{:S(2)}) %collective-permute-start.5) | collective-permute-done | bytes 327712 | tf_op jit(solution)/shard_map/ppermute | solution.py:322
  153.6 1.5 collective-permute-done.13.refs_1_
  158.2 5.4 %collective-permute-done.7.refs_2_ = bf16[1280,128]{1,0:T(8,128)(2,1)S(1)} collective-permute-done((bf16[1280,128]{1,0:T(8,128)(2,1)}, bf16[1280,128]{1,0:T(8,128)(2,1)S(1)}, u32[]{:S(2)}, u32[]{:S(2)}) %collective-permute-start.7) | collective-permute-done | bytes 327712 | tf_op jit(solution)/shard_map/ppermute | solution.py:322
  163.6 2.1 %collective-permute-start.10 = (bf16[1280,128]{1,0:T(8,128)(2,1)S(1)}, bf16[1280,128]{1,0:T(8,128)(2,1)S(1)}, u32[]{:S(2)}, u32[]{:S(2)}) collective-permute-start(bf16[1280,128]{1,0:T(8,128)(2,1)S(1)} %collective-permute-done.7.refs_2_), channel_id=1, source_target_pairs={{0,12},{1,13},{2,14},{3,15},{4,0},{5,1},{6,2},{7,3},{8,4},{9,5},{1... | collective-permute-start | bytes 983048 | tf_op jit(solution)/shard_map/ppermute | solution.py:322
  165.8 5.7 %shard_map.53.refs_7_ = bf16[512,512]{1,0:T(8,128)(2,1)S(1)} custom-call(f32[1296,128]{1,0:T(8,128)S(1)} %get-tuple-element.36.refs_0_, bf16[1296,128]{1,0:T(8,128)(2,1)S(1)} %collective-permute-done.13.refs_1_, bf16[1296,128]{1,0:T(8,128)(2,1)S(1)} %collective-permute-done.14.refs_2_, bf16[1296,128]{1,0:T(8,128)(2,1)S(1)} %collective-permute-done.15.refs_3_), custom_call_target="tpu_custom_call" | custom-call | flops 1048576 | bytes 4096 | tf_op jit(solution)/shard_map/pallas_call | solution.py:214
  171.5 2.2 %copy-done.1 = bf16[1,4096,512]{2,1,0:T(8,128)(2,1)S(1)} copy-done((bf16[1,4096,512]{2,1,0:T(8,128)(2,1)S(1)}, bf16[1,4096,512]{2,1,0:T(8,128)(2,1)}, u32[]{:S(2)}) %copy-start.1) | copy-done | bytes 4194328
  173.7 3.5 %shard_map.50.refs_5_ = bf16[4,512,512]{2,1,0:T(8,128)(2,1)S(1)} custom-call(s32[8]{0:T(128)S(1)} %stack.35.refs_0_, bf16[1280,128]{1,0:T(8,128)(2,1)S(1)} %shard_map.49.refs_1_, bf16[1280,128]{1,0:T(8,128)(2,1)} %collective-permute-done.5.refs_2_, bf16[1280,128]{1,0:T(8,128)(2,1)} %collective-permute-done.8.refs_3_, ...), custom_call_target="tpu_custom_call" | custom-call | flops 1048576 | bytes 4096 | tf_op jit(solution)/shard_map/pallas_call | solution.py:254
  177.2 6.8 %shard_map.54 = bf16[4096,512]{1,0:T(8,128)(2,1)} custom-call(s32[8]{0:T(128)S(1)} %stack.35.refs_0_, bf16[1280,128]{1,0:T(8,128)(2,1)S(1)} %collective-permute-done.6.refs_1_, bf16[1280,128]{1,0:T(8,128)(2,1)S(1)} %collective-permute-done.7.refs_2_, bf16[1280,128]{1,0:T(8,128)(2,1)S(1)} %collective-permute-done.9.refs_3_, ...), custom_call_target="tpu_custom_call" | custom-call | flops 1048576 | bytes 4096 | tf_op jit(solution)/shard_map/pallas_call | solution.py:304
  (41 shorter events, 11.2 us)
Async XLA Ops:
  0.8 2.2 %copy-start.2 = (bf16[256,8192]{1,0:T(8,128)(2,1)S(1)}, bf16[256,8192]{1,0:T(8,128)(2,1)}, u32[]{:S(2)}) copy-start(bf16[256,8192]{1,0:T(8,128)(2,1)} %grads_ref.1) | copy-start | bytes 12582916
  3.0 1.6 copy-start.3
  4.6 0.7 copy-start.4
  94.0 2.9 %copy-start = (bf16[16,400,512]{2,1,0:T(8,128)(2,1)S(1)}, bf16[16,400,512]{2,1,0:T(8,128)(2,1)}, u32[]{:S(2)}) copy-start(bf16[16,400,512]{2,1,0:T(8,128)(2,1)} %all_to_all.5.refs_2_) | copy-start | bytes 19660804
  100.2 8.1 %collective-permute-start = (f32[4,1296,128]{2,1,0:T(8,128)S(1)}, f32[4,1296,128]{2,1,0:T(8,128)S(1)}, u32[]{:S(2)}, u32[]{:S(2)}) collective-permute-start(f32[4,1296,128]{2,1,0:T(8,128)S(1)} %shard_map.48), channel_id=1, source_target_pairs={{0,16},{16,0},{32,48},{48,32},{64,80},{80,64},{96,112},{112,96},{1... | collective-permute-start | bytes 7962632 | tf_op jit(solution)/shard_map/ppermute | solution.py:322
  104.4 39.1 %collective-permute-start.12 = (f32[4,1296,128]{2,1,0:T(8,128)S(1)}, f32[4,1296,128]{2,1,0:T(8,128)S(1)}, u32[]{:S(2)}, u32[]{:S(2)}) collective-permute-start(f32[4,1296,128]{2,1,0:T(8,128)S(1)} %shard_map.52), channel_id=1, source_target_pairs={{0,16},{16,0},{32,48},{48,32},{64,80},{80,64},{96,112},{112,96},{1... | collective-permute-start | bytes 7962632 | tf_op jit(solution)/shard_map/ppermute | solution.py:322
  108.5 10.7 %collective-permute-start.1 = (bf16[1296,128]{1,0:T(8,128)(2,1)S(1)}, bf16[1296,128]{1,0:T(8,128)(2,1)S(1)}, u32[]{:S(2)}, u32[]{:S(2)}) collective-permute-start(bf16[1296,128]{1,0:T(8,128)(2,1)S(1)} %get-tuple-element.37), channel_id=1, source_target_pairs={{0,32},{16,48},{32,64},{48,80},{64,96},{80,112},{96,0},{112,16},{1... | collective-permute-start | bytes 995336 | tf_op jit(solution)/shard_map/ppermute | solution.py:322
  108.8 12.2 %collective-permute-start.2 = (bf16[1296,128]{1,0:T(8,128)(2,1)S(1)}, bf16[1296,128]{1,0:T(8,128)(2,1)S(1)}, u32[]{:S(2)}, u32[]{:S(2)}) collective-permute-start(bf16[1296,128]{1,0:T(8,128)(2,1)S(1)} %get-tuple-element.39), channel_id=1, source_target_pairs={{0,64},{16,80},{32,96},{48,112},{64,0},{80,16},{96,32},{112,48},{1... | collective-permute-start | bytes 995336 | tf_op jit(solution)/shard_map/ppermute | solution.py:322
  111.4 15.6 %collective-permute-start.3 = (bf16[1296,128]{1,0:T(8,128)(2,1)S(1)}, bf16[1296,128]{1,0:T(8,128)(2,1)S(1)}, u32[]{:S(2)}, u32[]{:S(2)}) collective-permute-start(bf16[1296,128]{1,0:T(8,128)(2,1)S(1)} %get-tuple-element.38), channel_id=1, source_target_pairs={{0,96},{16,112},{32,0},{48,16},{64,32},{80,48},{96,64},{112,80},{1... | collective-permute-start | bytes 995336 | tf_op jit(solution)/shard_map/ppermute | solution.py:322
  127.2 9.8 %collective-permute-start.4 = (bf16[1296,128]{1,0:T(8,128)(2,1)S(1)}, bf16[1296,128]{1,0:T(8,128)(2,1)S(1)}, u32[]{:S(2)}, u32[]{:S(2)}) collective-permute-start(bf16[1296,128]{1,0:T(8,128)(2,1)S(1)} %get-tuple-element.29), channel_id=1, source_target_pairs={{0,1},{1,0},{2,3},{3,2},{4,5},{5,4},{6,7},{7,6},{8,9},{9,8},{10,11... | collective-permute-start | bytes 995336 | tf_op jit(solution)/shard_map/ppermute | solution.py:322
  142.6 10.2 %collective-permute-start.5 = (bf16[1280,128]{1,0:T(8,128)(2,1)S(1)}, bf16[1280,128]{1,0:T(8,128)(2,1)}, u32[]{:S(2)}, u32[]{:S(2)}) collective-permute-start(bf16[1280,128]{1,0:T(8,128)(2,1)S(1)} %shard_map.49.refs_1_), channel_id=1, source_target_pairs={{0,3},{1,2},{2,1},{3,0},{4,7},{5,6},{6,5},{7,4},{8,11},{9,10},{10,... | collective-permute-start | bytes 983048 | tf_op jit(solution)/shard_map/ppermute | solution.py:322
  144.4 10.7 %collective-permute-start.13 = (bf16[1296,128]{1,0:T(8,128)(2,1)S(1)}, bf16[1296,128]{1,0:T(8,128)(2,1)S(1)}, u32[]{:S(2)}, u32[]{:S(2)}) collective-permute-start(bf16[1296,128]{1,0:T(8,128)(2,1)S(1)} %get-tuple-element.35), channel_id=1, source_target_pairs={{0,32},{16,48},{32,64},{48,80},{64,96},{80,112},{96,0},{112,16},{1... | collective-permute-start | bytes 995336 | tf_op jit(solution)/shard_map/ppermute | solution.py:322
  144.7 12.0 %collective-permute-start.14 = (bf16[1296,128]{1,0:T(8,128)(2,1)S(1)}, bf16[1296,128]{1,0:T(8,128)(2,1)S(1)}, u32[]{:S(2)}, u32[]{:S(2)}) collective-permute-start(bf16[1296,128]{1,0:T(8,128)(2,1)S(1)} %get-tuple-element.34), channel_id=1, source_target_pairs={{0,64},{16,80},{32,96},{48,112},{64,0},{80,16},{96,32},{112,48},{1... | collective-permute-start | bytes 995336 | tf_op jit(solution)/shard_map/ppermute | solution.py:322
  146.4 10.8 %collective-permute-start.8 = (bf16[1280,128]{1,0:T(8,128)(2,1)S(1)}, bf16[1280,128]{1,0:T(8,128)(2,1)}, u32[]{:S(2)}, u32[]{:S(2)}) collective-permute-start(bf16[1280,128]{1,0:T(8,128)(2,1)S(1)} %shard_map.49.refs_1_), channel_id=1, source_target_pairs={{0,4},{1,5},{2,6},{3,7},{4,8},{5,9},{6,10},{7,11},{8,12},{9,13},{1... | collective-permute-start | bytes 983048 | tf_op jit(solution)/shard_map/ppermute | solution.py:322
  152.8 10.9 %collective-permute-start.7 = (bf16[1280,128]{1,0:T(8,128)(2,1)}, bf16[1280,128]{1,0:T(8,128)(2,1)S(1)}, u32[]{:S(2)}, u32[]{:S(2)}) collective-permute-start(bf16[1280,128]{1,0:T(8,128)(2,1)} %collective-permute-done.5.refs_2_), channel_id=1, source_target_pairs={{0,12},{1,13},{2,14},{3,15},{4,0},{5,1},{6,2},{7,3},{8,4},{9,5},{1... | collective-permute-start | bytes 983048 | tf_op jit(solution)/shard_map/ppermute | solution.py:322
  153.6 12.2 %collective-permute-start.15 = (bf16[1296,128]{1,0:T(8,128)(2,1)}, bf16[1296,128]{1,0:T(8,128)(2,1)S(1)}, u32[]{:S(2)}, u32[]{:S(2)}) collective-permute-start(bf16[1296,128]{1,0:T(8,128)(2,1)} %get-tuple-element.33), channel_id=1, source_target_pairs={{0,96},{16,112},{32,0},{48,16},{64,32},{80,48},{96,64},{112,80},{1... | collective-permute-start | bytes 995336 | tf_op jit(solution)/shard_map/ppermute | solution.py:322
  155.2 16.3 %collective-permute-start.11 = (bf16[1280,128]{1,0:T(8,128)(2,1)S(1)}, bf16[1280,128]{1,0:T(8,128)(2,1)}, u32[]{:S(2)}, u32[]{:S(2)}) collective-permute-start(bf16[1280,128]{1,0:T(8,128)(2,1)S(1)} %shard_map.49.refs_1_), channel_id=1, source_target_pairs={{0,12},{1,13},{2,14},{3,15},{4,0},{5,1},{6,2},{7,3},{8,4},{9,5},{1... | collective-permute-start | bytes 983048 | tf_op jit(solution)/shard_map/ppermute | solution.py:322
  156.6 20.6 %collective-permute-start.6 = (bf16[1280,128]{1,0:T(8,128)(2,1)}, bf16[1280,128]{1,0:T(8,128)(2,1)S(1)}, u32[]{:S(2)}, u32[]{:S(2)}) collective-permute-start(bf16[1280,128]{1,0:T(8,128)(2,1)} %collective-permute-done.5.refs_2_), channel_id=1, source_target_pairs={{0,4},{1,5},{2,6},{3,7},{4,8},{5,9},{6,10},{7,11},{8,12},{9,13},{1... | collective-permute-start | bytes 983048 | tf_op jit(solution)/shard_map/ppermute | solution.py:322
  157.2 20.0 %collective-permute-start.9 = (bf16[1280,128]{1,0:T(8,128)(2,1)}, bf16[1280,128]{1,0:T(8,128)(2,1)S(1)}, u32[]{:S(2)}, u32[]{:S(2)}) collective-permute-start(bf16[1280,128]{1,0:T(8,128)(2,1)} %collective-permute-done.8.refs_3_), channel_id=1, source_target_pairs={{0,4},{1,5},{2,6},{3,7},{4,8},{5,9},{6,10},{7,11},{8,12},{9,13},{1... | collective-permute-start | bytes 983048 | tf_op jit(solution)/shard_map/ppermute | solution.py:322
  163.6 13.6 %collective-permute-start.10 = (bf16[1280,128]{1,0:T(8,128)(2,1)S(1)}, bf16[1280,128]{1,0:T(8,128)(2,1)S(1)}, u32[]{:S(2)}, u32[]{:S(2)}) collective-permute-start(bf16[1280,128]{1,0:T(8,128)(2,1)S(1)} %collective-permute-done.7.refs_2_), channel_id=1, source_target_pairs={{0,12},{1,13},{2,14},{3,15},{4,0},{5,1},{6,2},{7,3},{8,4},{9,5},{1... | collective-permute-start | bytes 983048 | tf_op jit(solution)/shard_map/ppermute | solution.py:322
  171.5 2.2 %copy-start.1 = (bf16[1,4096,512]{2,1,0:T(8,128)(2,1)S(1)}, bf16[1,4096,512]{2,1,0:T(8,128)(2,1)}, u32[]{:S(2)}) copy-start(bf16[1,4096,512]{2,1,0:T(8,128)(2,1)} %param.7) | copy-start | bytes 12582916

commit v4 on v3

--- a/solution.py
+++ b/solution.py
@@ -322,14 +322,17 @@
     return lax.ppermute(x, axis, [(i, target(i)) for i in range(lax.axis_size(axis))])
 
 
-def sum_over_group(grams_of):
+def sum_over_chip(grams_of):
     got = send(grams_of(0), "expert", lambda i: i ^ 1)
     mine = grams_of(4)
-    parts = [mine[0] + got[0]]
-    for k in range(1, 4):
-        part = (mine[k] + got[k]).astype(jnp.bfloat16)
-        parts.append(send(part, "expert", lambda i: (i + 2 * k) % EXPERTS))
-    return parts
+    return [mine[0] + got[0]] + [(mine[k] + got[k]).astype(jnp.bfloat16) for k in range(1, 4)]
+
+
+def exchange_along_y(parts):
+    return parts[:1] + [
+        send(part, "expert", lambda i, k=k: (i + 2 * k) % EXPERTS)
+        for k, part in enumerate(parts[1:], 1)
+    ]
 
 
 def per_device(slot_inputs, slot_grads, slot_expert, weight_grad):
@@ -356,14 +359,18 @@
     end = start + jnp.sum(counts[:, :, None] * same[None], axis=1)
 
     own_start, own_end = (start + 1 - odd) >> 1, (end + 1 - odd) >> 1
-    act_parts = sum_over_group(
+    act_parts = sum_over_chip(
         lambda first: gram(got, own_start, own_end, first, 0, SLOT_DEV // 2, CAP // 2)
     )
+    act_parts = exchange_along_y(act_parts)
+    out_parts = sum_over_chip(lambda first: gram(got, start, end, first, OUT_ROWS, SLOT_DEV, CAP))
     act = act_parts[0]
     for part in act_parts[1:]:
         act = act + part.astype(jnp.float32)
     other = send(act.astype(jnp.bfloat16), "shard", lambda i: i ^ 1)
+    other, _ = lax.optimization_barrier((other, out_parts))
     act_inverse = newton(True, act, other)
+    out_parts = exchange_along_y(out_parts)
 
     def up(i):
         return (i + 4) % 16
@@ -372,22 +379,23 @@
         return (i - 4) % 16
 
     across = send(act_inverse, "shard", lambda i: i // 4 * 4 + 3 - i % 4)
+    across, out_parts = lax.optimization_barrier((across, out_parts))
     own_below = send(act_inverse, "shard", up)
     own_above = send(act_inverse, "shard", down)
     across_below = send(across, "shard", up)
     across_above = send(across, "shard", down)
     own_far = send(own_below, "shard", up)
+    out_inverse = newton(False, *out_parts)
+    across_above, out_inverse = lax.optimization_barrier((across_above, out_inverse))
     across_far = send(across_above, "shard", down)
     z, side = shard_pos >> 2, shard_pos >> 1 & 1
-    early = [act_inverse, across, own_below, own_above]
-    late = [across_below, across_above, own_far, across_far]
-    places = [(0, 0), (0, 1), (-1, 0), (1, 0), (-1, 1), (1, 1), (2, 0), (2, 1)]
+    places = [(0, 0), (0, 1), (1, 1), (-1, 0), (1, 0), (-1, 1), (2, 0), (2, 1)]
     index = [2 * ((z + step) & 3) + (side ^ other_side) for step, other_side in places]
     index = jnp.stack(index).astype(jnp.int32)
 
-    out_parts = sum_over_group(lambda first: gram(got, start, end, first, OUT_ROWS, SLOT_DEV, CAP))
+    early = [act_inverse, across, across_above]
     done = left_product(index, early, weight_grad[0])
-    out_inverse = newton(False, *out_parts)
+    late = [own_below, own_above, across_below, own_far, across_far]
     return apply(index, done, late, weight_grad[0], out_inverse)[None]
 
 

time: 186 us -> 183 us (0.984)
  waiting for transfers between devices: 33.9 us -> 29.6 us
  starting transfers between devices: 13.1 us -> 16.9 us
    ppermute x16, waiting for transfers between devices: 33.9 us -> 29.6 us  [send(): lax.ppermute(x, axis, [(i, target(i)) for i in range(lax.axis_size(axis))])]
    ppermute x16, starting transfers between devices: 13.1 us -> 16.9 us  [send(): lax.ppermute(x, axis, [(i, target(i)) for i in range(lax.axis_size(axis))])]
  transfers between devices with their start and end apart: 16 -> 16, of which waited for: 8 -> 9; matrix products, arithmetic and copies ran while one was open for 1% -> 0% of each run, Pallas kernels for 14% -> 14%
where the time goes in v4:
time: 183 us; the launch traced here: 182 us
  blocking collectives  83.9 us (46%)
  Pallas kernels  39.3 us (21%)
  waiting for transfers between devices  29.6 us (16%)
  starting transfers between devices  16.9 us (9%)
  local copies, waits for them, and re-layouts  10.6 us (6%)
    all_to_all x1, blocking collectives, per_device(): got = lax.all_to_all(sent, 'shard', 0, 0, tiled=True)  83.9 us
    ppermute x16, waiting for transfers between devices, send(): lax.ppermute(x, axis, [(i, target(i)) for i in range(lax.axis_size(axis))])  29.6 us
    ppermute x16, starting transfers between devices, send(): lax.ppermute(x, axis, [(i, target(i)) for i in range(lax.axis_size(axis))])  16.9 us
    pallas_call x4, Pallas kernels, gram(): pl.pallas_call(lambda *refs: gram_kernel(first, offset, rows, window, *re...  14.8 us
    pallas_call x2, Pallas kernels, newton(): pl.pallas_call(lambda *refs: newton_kernel(packed, *refs), in_specs=[pl.B...  11.3 us
    unnamed x11, local copies, waits for them, and re-layouts  10.3 us
    pallas_call x1, Pallas kernels, apply(): pl.pallas_call(lambda *refs: apply_kernel(count, *refs), in_specs=[pl.Blo...  7.23 us
    pallas_call x1, Pallas kernels, route(): pl.pallas_call(route_kernel, grid=(pairs,), in_specs=[pl.BlockSpec((SLOT_...  3.72 us
  transfers between devices with their start and end apart: 16, of which 9 were waited for; matrix products, arithmetic and copies ran while one was open for 0% of the time, Pallas kernels for 14%

profile of v4, /device:TPU:24, one launch (start us, length us, event | category | flops | bytes accessed | tf_op | source)
XLA Modules:
  0.0 182.2 jit_solution(12325608229436928797)
XLA Ops:
  0.8 2.2 %copy-done.2 = bf16[256,8192]{1,0:T(8,128)(2,1)S(1)} copy-done((bf16[256,8192]{1,0:T(8,128)(2,1)S(1)}, bf16[256,8192]{1,0:T(8,128)(2,1)}, u32[]{:S(2)}) %copy-start.2) | copy-done | bytes 4194328
  5.3 3.7 %shard_map.46 = bf16[16,400,512]{2,1,0:T(8,128)(2,1)S(1)} custom-call(s32[256,1]{1,0:T(8,128)S(1)} %copy.15.col_ref, s32[1,256]{1,0:T(1,128)S(1)} %bitcast.37, bf16[256,4096]{1,0:T(8,128)(2,1)S(1)} %copy-done.3, bf16[256,8192]{1,0:T(8,128)(2,1)S(1)} %copy-done.2), custom_call_target="tpu_custom_call" | custom-call | flops 1048576 | bytes 4096 | tf_op jit(solution)/shard_map/pallas_call | solution.py:62
  9.0 83.9 %all_to_all.5.refs_2_ = bf16[16,400,512]{2,1,0:T(8,128)(2,1)} all-to-all(bf16[16,400,512]{2,1,0:T(8,128)(2,1)S(1)} %shard_map.46), channel_id=1, replica_groups=mesh['expert'=8,'shard'=16] {'shard'}, dimensions={0} | all-to-all | bytes 13107200 | tf_op jit(solution)/shard_map/all_to_all | solution.py:348
  94.0 2.9 %copy-done = bf16[16,400,512]{2,1,0:T(8,128)(2,1)S(1)} copy-done((bf16[16,400,512]{2,1,0:T(8,128)(2,1)S(1)}, bf16[16,400,512]{2,1,0:T(8,128)(2,1)}, u32[]{:S(2)}) %copy-start) | copy-done | bytes 6553624
  96.9 3.3 %shard_map.48 = f32[4,1296,128]{2,1,0:T(8,128)S(1)} custom-call(s32[16,8]{1,0:T(8,128)S(1)} %get-tuple-element.56.refs_0_, s32[16,8]{1,0:T(8,128)S(1)} %get-tuple-element.47.refs_1_, bf16[16,400,512]{2,1,0:T(8,128)(2,1)S(1)} %copy-done), custom_call_target="tpu_custom_call" | custom-call | flops 1048576 | bytes 4096 | tf_op jit(solution)/shard_map/pallas_call | solution.py:110
  100.3 4.0 %shard_map.50 = f32[4,1296,128]{2,1,0:T(8,128)S(1)} custom-call(s32[16,8]{1,0:T(8,128)S(1)} %copy.17.refs_0_, s32[16,8]{1,0:T(8,128)S(1)} %get-tuple-element.48.refs_1_, bf16[16,400,512]{2,1,0:T(8,128)(2,1)S(1)} %copy-done), custom_call_target="tpu_custom_call" | custom-call | flops 1048576 | bytes 4096 | tf_op jit(solution)/shard_map/pallas_call | solution.py:110
  104.9 3.3 %shard_map.47 = f32[4,1296,128]{2,1,0:T(8,128)S(1)} custom-call(s32[16,8]{1,0:T(8,128)S(1)} %get-tuple-element.56.refs_0_, s32[16,8]{1,0:T(8,128)S(1)} %get-tuple-element.47.refs_1_, bf16[16,400,512]{2,1,0:T(8,128)(2,1)S(1)} %copy-done), custom_call_target="tpu_custom_call" | custom-call | flops 1048576 | bytes 4096 | tf_op jit(solution)/shard_map/pallas_call | solution.py:110
  108.8 2.6 %collective-permute-start.2 = (bf16[1296,128]{1,0:T(8,128)(2,1)S(1)}, bf16[1296,128]{1,0:T(8,128)(2,1)S(1)}, u32[]{:S(2)}, u32[]{:S(2)}) collective-permute-start(bf16[1296,128]{1,0:T(8,128)(2,1)S(1)} %get-tuple-element.55), channel_id=1, source_target_pairs={{0,64},{16,80},{32,96},{48,112},{64,0},{80,16},{96,32},{112,48},{1... | collective-permute-start | bytes 995336 | tf_op jit(solution)/shard_map/ppermute | solution.py:322
  111.4 4.1 %shard_map.49 = f32[4,1296,128]{2,1,0:T(8,128)S(1)} custom-call(s32[16,8]{1,0:T(8,128)S(1)} %copy.17.refs_0_, s32[16,8]{1,0:T(8,128)S(1)} %get-tuple-element.48.refs_1_, bf16[16,400,512]{2,1,0:T(8,128)(2,1)S(1)} %copy-done), custom_call_target="tpu_custom_call" | custom-call | flops 1048576 | bytes 4096 | tf_op jit(solution)/shard_map/pallas_call | solution.py:110
  115.4 3.8 %collective-permute-done.1 = bf16[1296,128]{1,0:T(8,128)(2,1)S(1)} collective-permute-done((bf16[1296,128]{1,0:T(8,128)(2,1)S(1)}, bf16[1296,128]{1,0:T(8,128)(2,1)S(1)}, u32[]{:S(2)}, u32[]{:S(2)}) %collective-permute-start.1) | collective-permute-done | bytes 331808 | tf_op jit(solution)/shard_map/ppermute | solution.py:322
  119.2 1.8 collective-permute-done.2
  121.0 6.0 %collective-permute-done.3 = bf16[1296,128]{1,0:T(8,128)(2,1)S(1)} collective-permute-done((bf16[1296,128]{1,0:T(8,128)(2,1)S(1)}, bf16[1296,128]{1,0:T(8,128)(2,1)S(1)}, u32[]{:S(2)}, u32[]{:S(2)}) %collective-permute-start.3) | collective-permute-done | bytes 331808 | tf_op jit(solution)/shard_map/ppermute | solution.py:322
  128.1 1.8 %collective-permute-start.10 = (bf16[1296,128]{1,0:T(8,128)(2,1)S(1)}, bf16[1296,128]{1,0:T(8,128)(2,1)S(1)}, u32[]{:S(2)}, u32[]{:S(2)}) collective-permute-start(bf16[1296,128]{1,0:T(8,128)(2,1)S(1)} %get-tuple-element.50), channel_id=1, source_target_pairs={{0,64},{16,80},{32,96},{48,112},{64,0},{80,16},{96,32},{112,48},{1... | collective-permute-start | bytes 995336 | tf_op jit(solution)/shard_map/ppermute | solution.py:322
  130.1 3.0 %collective-permute-start.9 = (bf16[1296,128]{1,0:T(8,128)(2,1)S(1)}, bf16[1296,128]{1,0:T(8,128)(2,1)S(1)}, u32[]{:S(2)}, u32[]{:S(2)}) collective-permute-start(bf16[1296,128]{1,0:T(8,128)(2,1)S(1)} %get-tuple-element.51), channel_id=1, source_target_pairs={{0,32},{16,48},{32,64},{48,80},{64,96},{80,112},{96,0},{112,16},{1... | collective-permute-start | bytes 995336 | tf_op jit(solution)/shard_map/ppermute | solution.py:322
  133.2 3.8 %collective-permute-done.4.refs_1_ = bf16[1296,128]{1,0:T(8,128)(2,1)S(1)} collective-permute-done((bf16[1296,128]{1,0:T(8,128)(2,1)S(1)}, bf16[1296,128]{1,0:T(8,128)(2,1)S(1)}, u32[]{:S(2)}, u32[]{:S(2)}) %collective-permute-start.4) | collective-permute-done | bytes 331808 | tf_op jit(solution)/shard_map/ppermute | solution.py:322
  137.0 5.6 %shard_map.51.refs_1_ = bf16[1280,128]{1,0:T(8,128)(2,1)S(1)} custom-call(f32[1296,128]{1,0:T(8,128)S(1)} %get-tuple-element.46.refs_0_, bf16[1296,128]{1,0:T(8,128)(2,1)S(1)} %collective-permute-done.4.refs_1_), custom_call_target="tpu_custom_call" | custom-call | flops 1048576 | bytes 4096 | tf_op jit(solution)/shard_map/pallas_call | solution.py:214
  144.1 2.1 %collective-permute-done.11.refs_3_ = bf16[1296,128]{1,0:T(8,128)(2,1)S(1)} collective-permute-done((bf16[1296,128]{1,0:T(8,128)(2,1)S(1)}, bf16[1296,128]{1,0:T(8,128)(2,1)S(1)}, u32[]{:S(2)}, u32[]{:S(2)}) %collective-permute-start.11) | collective-permute-done | bytes 331808 | tf_op jit(solution)/shard_map/ppermute | solution.py:322
  146.2 6.6 %collective-permute-done.8.refs_2_ = bf16[1280,128]{1,0:T(8,128)(2,1)S(1)} collective-permute-done((bf16[1280,128]{1,0:T(8,128)(2,1)S(1)}, bf16[1280,128]{1,0:T(8,128)(2,1)S(1)}, u32[]{:S(2)}, u32[]{:S(2)}) %collective-permute-start.8) | collective-permute-done | bytes 327712 | tf_op jit(solution)/shard_map/ppermute | solution.py:322
  156.9 5.7 %shard_map.52.refs_8_ = bf16[512,512]{1,0:T(8,128)(2,1)S(1)} custom-call(f32[1296,128]{1,0:T(8,128)S(1)} %get-tuple-element.36.refs_0_, bf16[1296,128]{1,0:T(8,128)(2,1)S(1)} %collective-permute-done.9.refs_1_, bf16[1296,128]{1,0:T(8,128)(2,1)S(1)} %collective-permute-done.10.refs_2_, bf16[1296,128]{1,0:T(8,128)(2,1)S(1)} %collective-permute-done.11.refs_3_), custom_call_target="tpu_custom_call" | custom-call | flops 1048576 | bytes 4096 | tf_op jit(solution)/shard_map/pallas_call | solution.py:214
  163.5 2.1 %collective-permute-start.15 = (bf16[1280,128]{1,0:T(8,128)(2,1)S(1)}, bf16[1280,128]{1,0:T(8,128)(2,1)S(1)}, u32[]{:S(2)}, u32[]{:S(2)}) collective-permute-start(bf16[1280,128]{1,0:T(8,128)(2,1)S(1)} %collective-permute-done.14.refs_3_), channel_id=1, source_target_pairs={{0,12},{1,13},{2,14},{3,15},{4,0},{5,1},{6,2},{7,3},{8,4},{9,5},{1... | collective-permute-start | bytes 983048 | tf_op jit(solution)/shard_map/ppermute | solution.py:322
  165.7 2.2 %copy-done.1 = bf16[1,4096,512]{2,1,0:T(8,128)(2,1)S(1)} copy-done((bf16[1,4096,512]{2,1,0:T(8,128)(2,1)S(1)}, bf16[1,4096,512]{2,1,0:T(8,128)(2,1)}, u32[]{:S(2)}) %copy-start.1) | copy-done | bytes 4194328
  167.9 2.3 %shard_map.53.refs_6_ = bf16[3,512,512]{2,1,0:T(8,128)(2,1)S(1)} custom-call(s32[8]{0:T(128)S(1)} %stack.35.refs_0_, bf16[1280,128]{1,0:T(8,128)(2,1)S(1)} %shard_map.51.refs_1_, bf16[1280,128]{1,0:T(8,128)(2,1)S(1)} %collective-permute-done.8.refs_2_, bf16[1280,128]{1,0:T(8,128)(2,1)S(1)} %collective-permute-done.14.refs_3_, bf16[4096,512]{1,0:T(8,128)(2,1)S(1)} %bitcast.36), custom_call_target="tpu_custom_call" | custom-call | flops 1048576 | bytes 4096 | tf_op jit(solution)/shard_map/pallas_call | solution.py:254
  170.5 4.2 %collective-permute-done.15.refs_5_ = bf16[1280,128]{1,0:T(8,128)(2,1)S(1)} collective-permute-done((bf16[1280,128]{1,0:T(8,128)(2,1)S(1)}, bf16[1280,128]{1,0:T(8,128)(2,1)S(1)}, u32[]{:S(2)}, u32[]{:S(2)}) %collective-permute-start.15) | collective-permute-done | bytes 327712 | tf_op jit(solution)/shard_map/ppermute | solution.py:322
  174.8 7.2 %shard_map.54 = bf16[4096,512]{1,0:T(8,128)(2,1)} custom-call(s32[8]{0:T(128)S(1)} %stack.35.refs_0_, bf16[1280,128]{1,0:T(8,128)(2,1)S(1)} %collective-permute-done.6.refs_1_, bf16[1280,128]{1,0:T(8,128)(2,1)S(1)} %collective-permute-done.7.refs_2_, bf16[1280,128]{1,0:T(8,128)(2,1)S(1)} %collective-permute-done.12.refs_3_, ...), custom_call_target="tpu_custom_call" | custom-call | flops 1048576 | bytes 4096 | tf_op jit(solution)/shard_map/pallas_call | solution.py:304
  (41 shorter events, 13.6 us)
Async XLA Ops:
  0.8 2.2 %copy-start.2 = (bf16[256,8192]{1,0:T(8,128)(2,1)S(1)}, bf16[256,8192]{1,0:T(8,128)(2,1)}, u32[]{:S(2)}) copy-start(bf16[256,8192]{1,0:T(8,128)(2,1)} %grads_ref.1) | copy-start | bytes 12582916
  3.0 1.6 copy-start.3
  4.6 0.7 copy-start.4
  94.0 2.9 %copy-start = (bf16[16,400,512]{2,1,0:T(8,128)(2,1)S(1)}, bf16[16,400,512]{2,1,0:T(8,128)(2,1)}, u32[]{:S(2)}) copy-start(bf16[16,400,512]{2,1,0:T(8,128)(2,1)} %all_to_all.5.refs_2_) | copy-start | bytes 19660804
  100.2 8.1 %collective-permute-start = (f32[4,1296,128]{2,1,0:T(8,128)S(1)}, f32[4,1296,128]{2,1,0:T(8,128)S(1)}, u32[]{:S(2)}, u32[]{:S(2)}) collective-permute-start(f32[4,1296,128]{2,1,0:T(8,128)S(1)} %shard_map.48), channel_id=1, source_target_pairs={{0,16},{16,0},{32,48},{48,32},{64,80},{80,64},{96,112},{112,96},{1... | collective-permute-start | bytes 7962632 | tf_op jit(solution)/shard_map/ppermute | solution.py:322
  104.4 23.5 %collective-permute-start.5 = (f32[4,1296,128]{2,1,0:T(8,128)S(1)}, f32[4,1296,128]{2,1,0:T(8,128)S(1)}, u32[]{:S(2)}, u32[]{:S(2)}) collective-permute-start(f32[4,1296,128]{2,1,0:T(8,128)S(1)} %shard_map.50), channel_id=1, source_target_pairs={{0,16},{16,0},{32,48},{48,32},{64,80},{80,64},{96,112},{112,96},{1... | collective-permute-start | bytes 7962632 | tf_op jit(solution)/shard_map/ppermute | solution.py:322
  108.5 10.7 %collective-permute-start.1 = (bf16[1296,128]{1,0:T(8,128)(2,1)S(1)}, bf16[1296,128]{1,0:T(8,128)(2,1)S(1)}, u32[]{:S(2)}, u32[]{:S(2)}) collective-permute-start(bf16[1296,128]{1,0:T(8,128)(2,1)S(1)} %get-tuple-element.53), channel_id=1, source_target_pairs={{0,32},{16,48},{32,64},{48,80},{64,96},{80,112},{96,0},{112,16},{1... | collective-permute-start | bytes 995336 | tf_op jit(solution)/shard_map/ppermute | solution.py:322
  108.8 12.2 %collective-permute-start.2 = (bf16[1296,128]{1,0:T(8,128)(2,1)S(1)}, bf16[1296,128]{1,0:T(8,128)(2,1)S(1)}, u32[]{:S(2)}, u32[]{:S(2)}) collective-permute-start(bf16[1296,128]{1,0:T(8,128)(2,1)S(1)} %get-tuple-element.55), channel_id=1, source_target_pairs={{0,64},{16,80},{32,96},{48,112},{64,0},{80,16},{96,32},{112,48},{1... | collective-permute-start | bytes 995336 | tf_op jit(solution)/shard_map/ppermute | solution.py:322
  111.4 15.6 %collective-permute-start.3 = (bf16[1296,128]{1,0:T(8,128)(2,1)S(1)}, bf16[1296,128]{1,0:T(8,128)(2,1)S(1)}, u32[]{:S(2)}, u32[]{:S(2)}) collective-permute-start(bf16[1296,128]{1,0:T(8,128)(2,1)S(1)} %get-tuple-element.54), channel_id=1, source_target_pairs={{0,96},{16,112},{32,0},{48,16},{64,32},{80,48},{96,64},{112,80},{1... | collective-permute-start | bytes 995336 | tf_op jit(solution)/shard_map/ppermute | solution.py:322
  127.2 9.8 %collective-permute-start.4 = (bf16[1296,128]{1,0:T(8,128)(2,1)S(1)}, bf16[1296,128]{1,0:T(8,128)(2,1)S(1)}, u32[]{:S(2)}, u32[]{:S(2)}) collective-permute-start(bf16[1296,128]{1,0:T(8,128)(2,1)S(1)} %get-tuple-element.45), channel_id=1, source_target_pairs={{0,1},{1,0},{2,3},{3,2},{4,5},{5,4},{6,7},{7,6},{8,9},{9,8},{10,11... | collective-permute-start | bytes 995336 | tf_op jit(solution)/shard_map/ppermute | solution.py:322
  128.1 16.0 %collective-permute-start.10 = (bf16[1296,128]{1,0:T(8,128)(2,1)S(1)}, bf16[1296,128]{1,0:T(8,128)(2,1)S(1)}, u32[]{:S(2)}, u32[]{:S(2)}) collective-permute-start(bf16[1296,128]{1,0:T(8,128)(2,1)S(1)} %get-tuple-element.50), channel_id=1, source_target_pairs={{0,64},{16,80},{32,96},{48,112},{64,0},{80,16},{96,32},{112,48},{1... | collective-permute-start | bytes 995336 | tf_op jit(solution)/shard_map/ppermute | solution.py:322
  129.9 16.3 %collective-permute-start.11 = (bf16[1296,128]{1,0:T(8,128)(2,1)S(1)}, bf16[1296,128]{1,0:T(8,128)(2,1)S(1)}, u32[]{:S(2)}, u32[]{:S(2)}) collective-permute-start(bf16[1296,128]{1,0:T(8,128)(2,1)S(1)} %get-tuple-element.49), channel_id=1, source_target_pairs={{0,96},{16,112},{32,0},{48,16},{64,32},{80,48},{96,64},{112,80},{1... | collective-permute-start | bytes 995336 | tf_op jit(solution)/shard_map/ppermute | solution.py:322
  130.1 16.1 %collective-permute-start.9 = (bf16[1296,128]{1,0:T(8,128)(2,1)S(1)}, bf16[1296,128]{1,0:T(8,128)(2,1)S(1)}, u32[]{:S(2)}, u32[]{:S(2)}) collective-permute-start(bf16[1296,128]{1,0:T(8,128)(2,1)S(1)} %get-tuple-element.51), channel_id=1, source_target_pairs={{0,32},{16,48},{32,64},{48,80},{64,96},{80,112},{96,0},{112,16},{1... | collective-permute-start | bytes 995336 | tf_op jit(solution)/shard_map/ppermute | solution.py:322
  142.6 10.3 %collective-permute-start.8 = (bf16[1280,128]{1,0:T(8,128)(2,1)S(1)}, bf16[1280,128]{1,0:T(8,128)(2,1)S(1)}, u32[]{:S(2)}, u32[]{:S(2)}) collective-permute-start(bf16[1280,128]{1,0:T(8,128)(2,1)S(1)} %shard_map.51.refs_1_), channel_id=1, source_target_pairs={{0,3},{1,2},{2,1},{3,0},{4,7},{5,6},{6,5},{7,4},{8,11},{9,10},{10,... | collective-permute-start | bytes 983048 | tf_op jit(solution)/shard_map/ppermute | solution.py:322
  143.6 12.1 %collective-permute-start.6 = (bf16[1280,128]{1,0:T(8,128)(2,1)S(1)}, bf16[1280,128]{1,0:T(8,128)(2,1)S(1)}, u32[]{:S(2)}, u32[]{:S(2)}) collective-permute-start(bf16[1280,128]{1,0:T(8,128)(2,1)S(1)} %shard_map.51.refs_1_), channel_id=1, source_target_pairs={{0,4},{1,5},{2,6},{3,7},{4,8},{5,9},{6,10},{7,11},{8,12},{9,13},{1... | collective-permute-start | bytes 983048 | tf_op jit(solution)/shard_map/ppermute | solution.py:322
  152.9 10.6 %collective-permute-start.14 = (bf16[1280,128]{1,0:T(8,128)(2,1)S(1)}, bf16[1280,128]{1,0:T(8,128)(2,1)S(1)}, u32[]{:S(2)}, u32[]{:S(2)}) collective-permute-start(bf16[1280,128]{1,0:T(8,128)(2,1)S(1)} %collective-permute-done.8.refs_2_), channel_id=1, source_target_pairs={{0,12},{1,13},{2,14},{3,15},{4,0},{5,1},{6,2},{7,3},{8,4},{9,5},{1... | collective-permute-start | bytes 983048 | tf_op jit(solution)/shard_map/ppermute | solution.py:322
  153.7 16.8 %collective-permute-start.7 = (bf16[1280,128]{1,0:T(8,128)(2,1)S(1)}, bf16[1280,128]{1,0:T(8,128)(2,1)S(1)}, u32[]{:S(2)}, u32[]{:S(2)}) collective-permute-start(bf16[1280,128]{1,0:T(8,128)(2,1)S(1)} %shard_map.51.refs_1_), channel_id=1, source_target_pairs={{0,12},{1,13},{2,14},{3,15},{4,0},{5,1},{6,2},{7,3},{8,4},{9,5},{1... | collective-permute-start | bytes 983048 | tf_op jit(solution)/shard_map/ppermute | solution.py:322
  154.3 16.2 %collective-permute-start.12 = (bf16[1280,128]{1,0:T(8,128)(2,1)S(1)}, bf16[1280,128]{1,0:T(8,128)(2,1)S(1)}, u32[]{:S(2)}, u32[]{:S(2)}) collective-permute-start(bf16[1280,128]{1,0:T(8,128)(2,1)S(1)} %collective-permute-done.8.refs_2_), channel_id=1, source_target_pairs={{0,4},{1,5},{2,6},{3,7},{4,8},{5,9},{6,10},{7,11},{8,12},{9,13},{1... | collective-permute-start | bytes 983048 | tf_op jit(solution)/shard_map/ppermute | solution.py:322
  155.8 14.8 %collective-permute-start.13 = (bf16[1280,128]{1,0:T(8,128)(2,1)S(1)}, bf16[1280,128]{1,0:T(8,128)(2,1)S(1)}, u32[]{:S(2)}, u32[]{:S(2)}) collective-permute-start(bf16[1280,128]{1,0:T(8,128)(2,1)S(1)} %collective-permute-done.6.refs_1_), channel_id=1, source_target_pairs={{0,4},{1,5},{2,6},{3,7},{4,8},{5,9},{6,10},{7,11},{8,12},{9,13},{1... | collective-permute-start | bytes 983048 | tf_op jit(solution)/shard_map/ppermute | solution.py:322
  163.5 11.3 %collective-permute-start.15 = (bf16[1280,128]{1,0:T(8,128)(2,1)S(1)}, bf16[1280,128]{1,0:T(8,128)(2,1)S(1)}, u32[]{:S(2)}, u32[]{:S(2)}) collective-permute-start(bf16[1280,128]{1,0:T(8,128)(2,1)S(1)} %collective-permute-done.14.refs_3_), channel_id=1, source_target_pairs={{0,12},{1,13},{2,14},{3,15},{4,0},{5,1},{6,2},{7,3},{8,4},{9,5},{1... | collective-permute-start | bytes 983048 | tf_op jit(solution)/shard_map/ppermute | solution.py:322
  165.7 2.2 %copy-start.1 = (bf16[1,4096,512]{2,1,0:T(8,128)(2,1)S(1)}, bf16[1,4096,512]{2,1,0:T(8,128)(2,1)}, u32[]{:S(2)}) copy-start(bf16[1,4096,512]{2,1,0:T(8,128)(2,1)} %param.7) | copy-start | bytes 12582916

commit v5 on v4

--- a/solution.py
+++ b/solution.py
@@ -29,51 +29,53 @@
     return pltpu.CompilerParams(vmem_limit_bytes=mib * MIB)
 
 
-def route_kernel(col_ref, row_ref, inputs_ref, grads_ref, o_ref, halves, sorts):
+def route_kernel(row_ref, inputs_ref, grads_ref, o_ref, halves, sorts, counts):
     n = SLOT_DEV
 
     @pl.when(pl.program_id(0) == 0)
     def _():
         sub = lax.broadcasted_iota(jnp.int32, (n, n), 0)
         lane = lax.broadcasted_iota(jnp.int32, (n, n), 1)
-        earlier = col_ref[...] * n + sub < row_ref[...] * n + lane
+        ids = jnp.broadcast_to(row_ref[...].astype(jnp.float32), (n, n))
+        column = ids.T
+        earlier = (column < ids) | ((column == ids) & (sub < lane))
         place = jnp.sum(earlier.astype(jnp.float32), axis=0, keepdims=True)
         place = place.astype(jnp.int32)
         sorts[...] = (sub == place).astype(jnp.float32).astype(jnp.bfloat16)
         place = (place >> 1) + (place & 1) * (n // 2)
         halves[...] = (sub == place).astype(jnp.float32).astype(jnp.bfloat16)
+        named = (column == lane.astype(jnp.float32)).astype(jnp.float32)
+        totals = jnp.broadcast_to(jnp.sum(named, axis=0, keepdims=True), (NOTE, n))
+        counts[...] = jnp.concatenate([totals, totals], axis=1).astype(jnp.bfloat16)
 
     def moved(order, x):
         return jnp.dot(order[...], x, preferred_element_type=jnp.float32).astype(jnp.bfloat16)
 
-    lane = lax.broadcasted_iota(jnp.int32, (n, BLK), 1)
-    counts = jnp.sum((col_ref[...] == lane).astype(jnp.float32), axis=0, keepdims=True)
-    counts = jnp.broadcast_to(counts, (NOTE, BLK)).astype(jnp.bfloat16)
     rows = moved(halves, inputs_ref[...])
     for half in range(2):
         o_ref[half, : n // 2, :] = rows[half * (n // 2) : (half + 1) * (n // 2)]
-        o_ref[half, n // 2 : OUT_ROWS, :] = counts
+        o_ref[half, n // 2 : OUT_ROWS, :] = counts[...]
         o_ref[half, OUT_ROWS:, :] = moved(sorts, grads_ref[:, half * BLK : (half + 1) * BLK])
 
 
-def route(inputs, grads, ids_col, ids_row):
+def route(inputs, grads, ids_row):
     pairs = inputs.shape[1] // BLK
     rows = OUT_ROWS + SLOT_DEV
     return pl.pallas_call(
         route_kernel,
         grid=(pairs,),
         in_specs=[
-            pl.BlockSpec((SLOT_DEV, 1), lambda b: (0, 0)),
             pl.BlockSpec((1, SLOT_DEV), lambda b: (0, 0)),
             pl.BlockSpec((SLOT_DEV, BLK), lambda b: (0, b)),
             pl.BlockSpec((SLOT_DEV, 2 * BLK), lambda b: (0, b)),
         ],
         out_specs=pl.BlockSpec((2, rows, BLK), lambda b: (b, 0, 0)),
         out_shape=jax.ShapeDtypeStruct((2 * pairs, rows, BLK), jnp.bfloat16),
-        scratch_shapes=[pltpu.VMEM((SLOT_DEV, SLOT_DEV), jnp.bfloat16)] * 2,
+        scratch_shapes=[pltpu.VMEM((SLOT_DEV, SLOT_DEV), jnp.bfloat16)] * 2
+        + [pltpu.VMEM((NOTE, BLK), jnp.bfloat16)],
         compiler_params=params(20),
         cost_estimate=BRIEF,
-    )(ids_col, ids_row, inputs, grads)
+    )(ids_row, inputs, grads)
 
 
 def gram_kernel(first, offset, rows, window, start_ref, end_ref, x_ref, o_ref, picked):
@@ -341,7 +343,7 @@
     parity, group = group_pos & 1, group_pos >> 1
     odd = shard_pos & 1
     ids_row = slot_expert.reshape(1, SLOT_DEV)
-    sent = route(slot_inputs, slot_grads, slot_expert, ids_row)
+    sent = route(slot_inputs, slot_grads, ids_row)
     sent, odd, parity, group, shard_pos = lax.optimization_barrier(
         (sent, odd, parity, group, shard_pos)
     )

time: 183 us -> 182 us (level)
    unnamed x11 -> x10, local copies, waits for them, and re-layouts: 10.3 us -> 9.51 us
where the time goes in v5:
time: 182 us; the launch traced here: 181 us
  blocking collectives  83.9 us (46%)
  Pallas kernels  39.3 us (22%)
  waiting for transfers between devices  29.6 us (16%)
  starting transfers between devices  16.9 us (9%)
  local copies, waits for them, and re-layouts  9.81 us (5%)
    all_to_all x1, blocking collectives, per_device(): got = lax.all_to_all(sent, 'shard', 0, 0, tiled=True)  83.9 us
    ppermute x16, waiting for transfers between devices, send(): lax.ppermute(x, axis, [(i, target(i)) for i in range(lax.axis_size(axis))])  29.6 us
    ppermute x16, starting transfers between devices, send(): lax.ppermute(x, axis, [(i, target(i)) for i in range(lax.axis_size(axis))])  16.9 us
    pallas_call x4, Pallas kernels, gram(): pl.pallas_call(lambda *refs: gram_kernel(first, offset, rows, window, *re...  14.8 us
    pallas_call x2, Pallas kernels, newton(): pl.pallas_call(lambda *refs: newton_kernel(packed, *refs), in_specs=[pl.B...  11.3 us
    unnamed x10, local copies, waits for them, and re-layouts  9.51 us
    pallas_call x1, Pallas kernels, apply(): pl.pallas_call(lambda *refs: apply_kernel(count, *refs), in_specs=[pl.Blo...  7.23 us
    pallas_call x1, Pallas kernels, route(): pl.pallas_call(route_kernel, grid=(pairs,), in_specs=[pl.BlockSpec((1, SL...  3.75 us
  transfers between devices with their start and end apart: 16, of which 9 were waited for; matrix products, arithmetic and copies ran while one was open for 0% of the time, Pallas kernels for 14%

profile of v5, /device:TPU:24, one launch (start us, length us, event | category | flops | bytes accessed | tf_op | source)
XLA Modules:
  0.0 181.4 jit_solution(6265104171622844943)
XLA Ops:
  0.0 2.2 %copy-done.2 = bf16[256,8192]{1,0:T(8,128)(2,1)S(1)} copy-done((bf16[256,8192]{1,0:T(8,128)(2,1)S(1)}, bf16[256,8192]{1,0:T(8,128)(2,1)}, u32[]{:S(2)}) %copy-start.2) | copy-done | bytes 4194328
  4.5 3.7 %shard_map.46 = bf16[16,400,512]{2,1,0:T(8,128)(2,1)S(1)} custom-call(s32[1,256]{1,0:T(1,128)S(1)} %bitcast.37, bf16[256,4096]{1,0:T(8,128)(2,1)S(1)} %copy-done.3, bf16[256,8192]{1,0:T(8,128)(2,1)S(1)} %copy-done.2), custom_call_target="tpu_custom_call" | custom-call | flops 1048576 | bytes 4096 | tf_op jit(solution)/shard_map/pallas_call | solution.py:64
  8.2 83.9 %all_to_all.5.refs_2_ = bf16[16,400,512]{2,1,0:T(8,128)(2,1)} all-to-all(bf16[16,400,512]{2,1,0:T(8,128)(2,1)S(1)} %shard_map.46), channel_id=1, replica_groups=mesh['expert'=8,'shard'=16] {'shard'}, dimensions={0} | all-to-all | bytes 13107200 | tf_op jit(solution)/shard_map/all_to_all | solution.py:350
  93.2 2.9 %copy-done = bf16[16,400,512]{2,1,0:T(8,128)(2,1)S(1)} copy-done((bf16[16,400,512]{2,1,0:T(8,128)(2,1)S(1)}, bf16[16,400,512]{2,1,0:T(8,128)(2,1)}, u32[]{:S(2)}) %copy-start) | copy-done | bytes 6553624
  96.1 3.3 %shard_map.48 = f32[4,1296,128]{2,1,0:T(8,128)S(1)} custom-call(s32[16,8]{1,0:T(8,128)S(1)} %get-tuple-element.56.refs_0_, s32[16,8]{1,0:T(8,128)S(1)} %get-tuple-element.47.refs_1_, bf16[16,400,512]{2,1,0:T(8,128)(2,1)S(1)} %copy-done), custom_call_target="tpu_custom_call" | custom-call | flops 1048576 | bytes 4096 | tf_op jit(solution)/shard_map/pallas_call | solution.py:112
  99.5 4.0 %shard_map.50 = f32[4,1296,128]{2,1,0:T(8,128)S(1)} custom-call(s32[16,8]{1,0:T(8,128)S(1)} %copy.14.refs_0_, s32[16,8]{1,0:T(8,128)S(1)} %get-tuple-element.48.refs_1_, bf16[16,400,512]{2,1,0:T(8,128)(2,1)S(1)} %copy-done), custom_call_target="tpu_custom_call" | custom-call | flops 1048576 | bytes 4096 | tf_op jit(solution)/shard_map/pallas_call | solution.py:112
  104.1 3.3 %shard_map.47 = f32[4,1296,128]{2,1,0:T(8,128)S(1)} custom-call(s32[16,8]{1,0:T(8,128)S(1)} %get-tuple-element.56.refs_0_, s32[16,8]{1,0:T(8,128)S(1)} %get-tuple-element.47.refs_1_, bf16[16,400,512]{2,1,0:T(8,128)(2,1)S(1)} %copy-done), custom_call_target="tpu_custom_call" | custom-call | flops 1048576 | bytes 4096 | tf_op jit(solution)/shard_map/pallas_call | solution.py:112
  108.0 2.6 %collective-permute-start.2 = (bf16[1296,128]{1,0:T(8,128)(2,1)S(1)}, bf16[1296,128]{1,0:T(8,128)(2,1)S(1)}, u32[]{:S(2)}, u32[]{:S(2)}) collective-permute-start(bf16[1296,128]{1,0:T(8,128)(2,1)S(1)} %get-tuple-element.55), channel_id=1, source_target_pairs={{0,64},{16,80},{32,96},{48,112},{64,0},{80,16},{96,32},{112,48},{1... | collective-permute-start | bytes 995336 | tf_op jit(solution)/shard_map/ppermute | solution.py:324
  110.6 4.1 %shard_map.49 = f32[4,1296,128]{2,1,0:T(8,128)S(1)} custom-call(s32[16,8]{1,0:T(8,128)S(1)} %copy.14.refs_0_, s32[16,8]{1,0:T(8,128)S(1)} %get-tuple-element.48.refs_1_, bf16[16,400,512]{2,1,0:T(8,128)(2,1)S(1)} %copy-done), custom_call_target="tpu_custom_call" | custom-call | flops 1048576 | bytes 4096 | tf_op jit(solution)/shard_map/pallas_call | solution.py:112
  114.7 3.8 %collective-permute-done.1 = bf16[1296,128]{1,0:T(8,128)(2,1)S(1)} collective-permute-done((bf16[1296,128]{1,0:T(8,128)(2,1)S(1)}, bf16[1296,128]{1,0:T(8,128)(2,1)S(1)}, u32[]{:S(2)}, u32[]{:S(2)}) %collective-permute-start.1) | collective-permute-done | bytes 331808 | tf_op jit(solution)/shard_map/ppermute | solution.py:324
  118.4 1.8 collective-permute-done.2
  120.2 6.0 %collective-permute-done.3 = bf16[1296,128]{1,0:T(8,128)(2,1)S(1)} collective-permute-done((bf16[1296,128]{1,0:T(8,128)(2,1)S(1)}, bf16[1296,128]{1,0:T(8,128)(2,1)S(1)}, u32[]{:S(2)}, u32[]{:S(2)}) %collective-permute-start.3) | collective-permute-done | bytes 331808 | tf_op jit(solution)/shard_map/ppermute | solution.py:324
  127.3 1.8 %collective-permute-start.10 = (bf16[1296,128]{1,0:T(8,128)(2,1)S(1)}, bf16[1296,128]{1,0:T(8,128)(2,1)S(1)}, u32[]{:S(2)}, u32[]{:S(2)}) collective-permute-start(bf16[1296,128]{1,0:T(8,128)(2,1)S(1)} %get-tuple-element.50), channel_id=1, source_target_pairs={{0,64},{16,80},{32,96},{48,112},{64,0},{80,16},{96,32},{112,48},{1... | collective-permute-start | bytes 995336 | tf_op jit(solution)/shard_map/ppermute | solution.py:324
  129.3 3.0 %collective-permute-start.9 = (bf16[1296,128]{1,0:T(8,128)(2,1)S(1)}, bf16[1296,128]{1,0:T(8,128)(2,1)S(1)}, u32[]{:S(2)}, u32[]{:S(2)}) collective-permute-start(bf16[1296,128]{1,0:T(8,128)(2,1)S(1)} %get-tuple-element.51), channel_id=1, source_target_pairs={{0,32},{16,48},{32,64},{48,80},{64,96},{80,112},{96,0},{112,16},{1... | collective-permute-start | bytes 995336 | tf_op jit(solution)/shard_map/ppermute | solution.py:324
  132.4 3.8 %collective-permute-done.4.refs_1_ = bf16[1296,128]{1,0:T(8,128)(2,1)S(1)} collective-permute-done((bf16[1296,128]{1,0:T(8,128)(2,1)S(1)}, bf16[1296,128]{1,0:T(8,128)(2,1)S(1)}, u32[]{:S(2)}, u32[]{:S(2)}) %collective-permute-start.4) | collective-permute-done | bytes 331808 | tf_op jit(solution)/shard_map/ppermute | solution.py:324
  136.2 5.6 %shard_map.51.refs_1_ = bf16[1280,128]{1,0:T(8,128)(2,1)S(1)} custom-call(f32[1296,128]{1,0:T(8,128)S(1)} %get-tuple-element.46.refs_0_, bf16[1296,128]{1,0:T(8,128)(2,1)S(1)} %collective-permute-done.4.refs_1_), custom_call_target="tpu_custom_call" | custom-call | flops 1048576 | bytes 4096 | tf_op jit(solution)/shard_map/pallas_call | solution.py:216
  143.3 2.1 %collective-permute-done.11.refs_3_ = bf16[1296,128]{1,0:T(8,128)(2,1)S(1)} collective-permute-done((bf16[1296,128]{1,0:T(8,128)(2,1)S(1)}, bf16[1296,128]{1,0:T(8,128)(2,1)S(1)}, u32[]{:S(2)}, u32[]{:S(2)}) %collective-permute-start.11) | collective-permute-done | bytes 331808 | tf_op jit(solution)/shard_map/ppermute | solution.py:324
  145.5 6.6 %collective-permute-done.8.refs_2_ = bf16[1280,128]{1,0:T(8,128)(2,1)S(1)} collective-permute-done((bf16[1280,128]{1,0:T(8,128)(2,1)S(1)}, bf16[1280,128]{1,0:T(8,128)(2,1)S(1)}, u32[]{:S(2)}, u32[]{:S(2)}) %collective-permute-start.8) | collective-permute-done | bytes 327712 | tf_op jit(solution)/shard_map/ppermute | solution.py:324
  156.1 5.7 %shard_map.52.refs_8_ = bf16[512,512]{1,0:T(8,128)(2,1)S(1)} custom-call(f32[1296,128]{1,0:T(8,128)S(1)} %get-tuple-element.36.refs_0_, bf16[1296,128]{1,0:T(8,128)(2,1)S(1)} %collective-permute-done.9.refs_1_, bf16[1296,128]{1,0:T(8,128)(2,1)S(1)} %collective-permute-done.10.refs_2_, bf16[1296,128]{1,0:T(8,128)(2,1)S(1)} %collective-permute-done.11.refs_3_), custom_call_target="tpu_custom_call" | custom-call | flops 1048576 | bytes 4096 | tf_op jit(solution)/shard_map/pallas_call | solution.py:216
  162.7 2.1 %collective-permute-start.15 = (bf16[1280,128]{1,0:T(8,128)(2,1)S(1)}, bf16[1280,128]{1,0:T(8,128)(2,1)S(1)}, u32[]{:S(2)}, u32[]{:S(2)}) collective-permute-start(bf16[1280,128]{1,0:T(8,128)(2,1)S(1)} %collective-permute-done.14.refs_3_), channel_id=1, source_target_pairs={{0,12},{1,13},{2,14},{3,15},{4,0},{5,1},{6,2},{7,3},{8,4},{9,5},{1... | collective-permute-start | bytes 983048 | tf_op jit(solution)/shard_map/ppermute | solution.py:324
  164.9 2.2 %copy-done.1 = bf16[1,4096,512]{2,1,0:T(8,128)(2,1)S(1)} copy-done((bf16[1,4096,512]{2,1,0:T(8,128)(2,1)S(1)}, bf16[1,4096,512]{2,1,0:T(8,128)(2,1)}, u32[]{:S(2)}) %copy-start.1) | copy-done | bytes 4194328
  167.1 2.3 %shard_map.53.refs_6_ = bf16[3,512,512]{2,1,0:T(8,128)(2,1)S(1)} custom-call(s32[8]{0:T(128)S(1)} %stack.35.refs_0_, bf16[1280,128]{1,0:T(8,128)(2,1)S(1)} %shard_map.51.refs_1_, bf16[1280,128]{1,0:T(8,128)(2,1)S(1)} %collective-permute-done.8.refs_2_, bf16[1280,128]{1,0:T(8,128)(2,1)S(1)} %collective-permute-done.14.refs_3_, bf16[4096,512]{1,0:T(8,128)(2,1)S(1)} %bitcast.36), custom_call_target="tpu_custom_call" | custom-call | flops 1048576 | bytes 4096 | tf_op jit(solution)/shard_map/pallas_call | solution.py:256
  169.7 4.2 %collective-permute-done.15.refs_5_ = bf16[1280,128]{1,0:T(8,128)(2,1)S(1)} collective-permute-done((bf16[1280,128]{1,0:T(8,128)(2,1)S(1)}, bf16[1280,128]{1,0:T(8,128)(2,1)S(1)}, u32[]{:S(2)}, u32[]{:S(2)}) %collective-permute-start.15) | collective-permute-done | bytes 327712 | tf_op jit(solution)/shard_map/ppermute | solution.py:324
  174.0 7.2 %shard_map.54 = bf16[4096,512]{1,0:T(8,128)(2,1)} custom-call(s32[8]{0:T(128)S(1)} %stack.35.refs_0_, bf16[1280,128]{1,0:T(8,128)(2,1)S(1)} %collective-permute-done.6.refs_1_, bf16[1280,128]{1,0:T(8,128)(2,1)S(1)} %collective-permute-done.7.refs_2_, bf16[1280,128]{1,0:T(8,128)(2,1)S(1)} %collective-permute-done.12.refs_3_, ...), custom_call_target="tpu_custom_call" | custom-call | flops 1048576 | bytes 4096 | tf_op jit(solution)/shard_map/pallas_call | solution.py:306
  (40 shorter events, 12.8 us)
Async XLA Ops:
  0.0 2.2 %copy-start.2 = (bf16[256,8192]{1,0:T(8,128)(2,1)S(1)}, bf16[256,8192]{1,0:T(8,128)(2,1)}, u32[]{:S(2)}) copy-start(bf16[256,8192]{1,0:T(8,128)(2,1)} %grads_ref.1) | copy-start | bytes 12582916
  2.2 1.6 copy-start.3
  3.8 0.7 copy-start.4
  93.2 2.9 %copy-start = (bf16[16,400,512]{2,1,0:T(8,128)(2,1)S(1)}, bf16[16,400,512]{2,1,0:T(8,128)(2,1)}, u32[]{:S(2)}) copy-start(bf16[16,400,512]{2,1,0:T(8,128)(2,1)} %all_to_all.5.refs_2_) | copy-start | bytes 19660804
  99.4 8.1 %collective-permute-start = (f32[4,1296,128]{2,1,0:T(8,128)S(1)}, f32[4,1296,128]{2,1,0:T(8,128)S(1)}, u32[]{:S(2)}, u32[]{:S(2)}) collective-permute-start(f32[4,1296,128]{2,1,0:T(8,128)S(1)} %shard_map.48), channel_id=1, source_target_pairs={{0,16},{16,0},{32,48},{48,32},{64,80},{80,64},{96,112},{112,96},{1... | collective-permute-start | bytes 7962632 | tf_op jit(solution)/shard_map/ppermute | solution.py:324
  103.6 23.5 %collective-permute-start.5 = (f32[4,1296,128]{2,1,0:T(8,128)S(1)}, f32[4,1296,128]{2,1,0:T(8,128)S(1)}, u32[]{:S(2)}, u32[]{:S(2)}) collective-permute-start(f32[4,1296,128]{2,1,0:T(8,128)S(1)} %shard_map.50), channel_id=1, source_target_pairs={{0,16},{16,0},{32,48},{48,32},{64,80},{80,64},{96,112},{112,96},{1... | collective-permute-start | bytes 7962632 | tf_op jit(solution)/shard_map/ppermute | solution.py:324
  107.7 10.7 %collective-permute-start.1 = (bf16[1296,128]{1,0:T(8,128)(2,1)S(1)}, bf16[1296,128]{1,0:T(8,128)(2,1)S(1)}, u32[]{:S(2)}, u32[]{:S(2)}) collective-permute-start(bf16[1296,128]{1,0:T(8,128)(2,1)S(1)} %get-tuple-element.53), channel_id=1, source_target_pairs={{0,32},{16,48},{32,64},{48,80},{64,96},{80,112},{96,0},{112,16},{1... | collective-permute-start | bytes 995336 | tf_op jit(solution)/shard_map/ppermute | solution.py:324
  108.0 12.2 %collective-permute-start.2 = (bf16[1296,128]{1,0:T(8,128)(2,1)S(1)}, bf16[1296,128]{1,0:T(8,128)(2,1)S(1)}, u32[]{:S(2)}, u32[]{:S(2)}) collective-permute-start(bf16[1296,128]{1,0:T(8,128)(2,1)S(1)} %get-tuple-element.55), channel_id=1, source_target_pairs={{0,64},{16,80},{32,96},{48,112},{64,0},{80,16},{96,32},{112,48},{1... | collective-permute-start | bytes 995336 | tf_op jit(solution)/shard_map/ppermute | solution.py:324
  110.6 15.6 %collective-permute-start.3 = (bf16[1296,128]{1,0:T(8,128)(2,1)S(1)}, bf16[1296,128]{1,0:T(8,128)(2,1)S(1)}, u32[]{:S(2)}, u32[]{:S(2)}) collective-permute-start(bf16[1296,128]{1,0:T(8,128)(2,1)S(1)} %get-tuple-element.54), channel_id=1, source_target_pairs={{0,96},{16,112},{32,0},{48,16},{64,32},{80,48},{96,64},{112,80},{1... | collective-permute-start | bytes 995336 | tf_op jit(solution)/shard_map/ppermute | solution.py:324
  126.4 9.8 %collective-permute-start.4 = (bf16[1296,128]{1,0:T(8,128)(2,1)S(1)}, bf16[1296,128]{1,0:T(8,128)(2,1)S(1)}, u32[]{:S(2)}, u32[]{:S(2)}) collective-permute-start(bf16[1296,128]{1,0:T(8,128)(2,1)S(1)} %get-tuple-element.45), channel_id=1, source_target_pairs={{0,1},{1,0},{2,3},{3,2},{4,5},{5,4},{6,7},{7,6},{8,9},{9,8},{10,11... | collective-permute-start | bytes 995336 | tf_op jit(solution)/shard_map/ppermute | solution.py:324
  127.3 16.0 %collective-permute-start.10 = (bf16[1296,128]{1,0:T(8,128)(2,1)S(1)}, bf16[1296,128]{1,0:T(8,128)(2,1)S(1)}, u32[]{:S(2)}, u32[]{:S(2)}) collective-permute-start(bf16[1296,128]{1,0:T(8,128)(2,1)S(1)} %get-tuple-element.50), channel_id=1, source_target_pairs={{0,64},{16,80},{32,96},{48,112},{64,0},{80,16},{96,32},{112,48},{1... | collective-permute-start | bytes 995336 | tf_op jit(solution)/shard_map/ppermute | solution.py:324
  129.1 16.3 %collective-permute-start.11 = (bf16[1296,128]{1,0:T(8,128)(2,1)S(1)}, bf16[1296,128]{1,0:T(8,128)(2,1)S(1)}, u32[]{:S(2)}, u32[]{:S(2)}) collective-permute-start(bf16[1296,128]{1,0:T(8,128)(2,1)S(1)} %get-tuple-element.49), channel_id=1, source_target_pairs={{0,96},{16,112},{32,0},{48,16},{64,32},{80,48},{96,64},{112,80},{1... | collective-permute-start | bytes 995336 | tf_op jit(solution)/shard_map/ppermute | solution.py:324
  129.3 16.1 %collective-permute-start.9 = (bf16[1296,128]{1,0:T(8,128)(2,1)S(1)}, bf16[1296,128]{1,0:T(8,128)(2,1)S(1)}, u32[]{:S(2)}, u32[]{:S(2)}) collective-permute-start(bf16[1296,128]{1,0:T(8,128)(2,1)S(1)} %get-tuple-element.51), channel_id=1, source_target_pairs={{0,32},{16,48},{32,64},{48,80},{64,96},{80,112},{96,0},{112,16},{1... | collective-permute-start | bytes 995336 | tf_op jit(solution)/shard_map/ppermute | solution.py:324
  141.8 10.3 %collective-permute-start.8 = (bf16[1280,128]{1,0:T(8,128)(2,1)S(1)}, bf16[1280,128]{1,0:T(8,128)(2,1)S(1)}, u32[]{:S(2)}, u32[]{:S(2)}) collective-permute-start(bf16[1280,128]{1,0:T(8,128)(2,1)S(1)} %shard_map.51.refs_1_), channel_id=1, source_target_pairs={{0,3},{1,2},{2,1},{3,0},{4,7},{5,6},{6,5},{7,4},{8,11},{9,10},{10,... | collective-permute-start | bytes 983048 | tf_op jit(solution)/shard_map/ppermute | solution.py:324
  142.8 12.1 %collective-permute-start.6 = (bf16[1280,128]{1,0:T(8,128)(2,1)S(1)}, bf16[1280,128]{1,0:T(8,128)(2,1)S(1)}, u32[]{:S(2)}, u32[]{:S(2)}) collective-permute-start(bf16[1280,128]{1,0:T(8,128)(2,1)S(1)} %shard_map.51.refs_1_), channel_id=1, source_target_pairs={{0,4},{1,5},{2,6},{3,7},{4,8},{5,9},{6,10},{7,11},{8,12},{9,13},{1... | collective-permute-start | bytes 983048 | tf_op jit(solution)/shard_map/ppermute | solution.py:324
  152.1 10.6 %collective-permute-start.14 = (bf16[1280,128]{1,0:T(8,128)(2,1)S(1)}, bf16[1280,128]{1,0:T(8,128)(2,1)S(1)}, u32[]{:S(2)}, u32[]{:S(2)}) collective-permute-start(bf16[1280,128]{1,0:T(8,128)(2,1)S(1)} %collective-permute-done.8.refs_2_), channel_id=1, source_target_pairs={{0,12},{1,13},{2,14},{3,15},{4,0},{5,1},{6,2},{7,3},{8,4},{9,5},{1... | collective-permute-start | bytes 983048 | tf_op jit(solution)/shard_map/ppermute | solution.py:324
  152.9 16.8 %collective-permute-start.7 = (bf16[1280,128]{1,0:T(8,128)(2,1)S(1)}, bf16[1280,128]{1,0:T(8,128)(2,1)S(1)}, u32[]{:S(2)}, u32[]{:S(2)}) collective-permute-start(bf16[1280,128]{1,0:T(8,128)(2,1)S(1)} %shard_map.51.refs_1_), channel_id=1, source_target_pairs={{0,12},{1,13},{2,14},{3,15},{4,0},{5,1},{6,2},{7,3},{8,4},{9,5},{1... | collective-permute-start | bytes 983048 | tf_op jit(solution)/shard_map/ppermute | solution.py:324
  153.5 16.3 %collective-permute-start.12 = (bf16[1280,128]{1,0:T(8,128)(2,1)S(1)}, bf16[1280,128]{1,0:T(8,128)(2,1)S(1)}, u32[]{:S(2)}, u32[]{:S(2)}) collective-permute-start(bf16[1280,128]{1,0:T(8,128)(2,1)S(1)} %collective-permute-done.8.refs_2_), channel_id=1, source_target_pairs={{0,4},{1,5},{2,6},{3,7},{4,8},{5,9},{6,10},{7,11},{8,12},{9,13},{1... | collective-permute-start | bytes 983048 | tf_op jit(solution)/shard_map/ppermute | solution.py:324
  155.0 14.8 %collective-permute-start.13 = (bf16[1280,128]{1,0:T(8,128)(2,1)S(1)}, bf16[1280,128]{1,0:T(8,128)(2,1)S(1)}, u32[]{:S(2)}, u32[]{:S(2)}) collective-permute-start(bf16[1280,128]{1,0:T(8,128)(2,1)S(1)} %collective-permute-done.6.refs_1_), channel_id=1, source_target_pairs={{0,4},{1,5},{2,6},{3,7},{4,8},{5,9},{6,10},{7,11},{8,12},{9,13},{1... | collective-permute-start | bytes 983048 | tf_op jit(solution)/shard_map/ppermute | solution.py:324
  162.7 11.3 %collective-permute-start.15 = (bf16[1280,128]{1,0:T(8,128)(2,1)S(1)}, bf16[1280,128]{1,0:T(8,128)(2,1)S(1)}, u32[]{:S(2)}, u32[]{:S(2)}) collective-permute-start(bf16[1280,128]{1,0:T(8,128)(2,1)S(1)} %collective-permute-done.14.refs_3_), channel_id=1, source_target_pairs={{0,12},{1,13},{2,14},{3,15},{4,0},{5,1},{6,2},{7,3},{8,4},{9,5},{1... | collective-permute-start | bytes 983048 | tf_op jit(solution)/shard_map/ppermute | solution.py:324
  164.9 2.2 %copy-start.1 = (bf16[1,4096,512]{2,1,0:T(8,128)(2,1)S(1)}, bf16[1,4096,512]{2,1,0:T(8,128)(2,1)}, u32[]{:S(2)}) copy-start(bf16[1,4096,512]{2,1,0:T(8,128)(2,1)} %param.7) | copy-start | bytes 12582916

commit v6 on v5

--- a/solution.py
+++ b/solution.py
@@ -96,7 +96,8 @@
     def product(a, b):
         return lax.dot_general(a, b, (((0,), (0,)), ((), ())), preferred_element_type=jnp.float32)
 
-    quarters = {(0, 0): product(left, left), (0, 1): product(left, right), (1, 1): product(right, right)}
+    upper = product(left, picked[...])
+    quarters = {(0, 0): upper[:, :HALF], (0, 1): upper[:, HALF:], (1, 1): product(right, right)}
     for n, (i, j) in enumerate(TILES):
         block = quarters[(i // 2, j // 2)]
         r, c = i % 2 * TILE, j % 2 * TILE

time: 182 us -> 182 us (level)
  no operation moved by 1% of the time
where the time goes in v6:
time: 182 us; the launch traced here: 181 us
  blocking collectives  83.9 us (46%)
  Pallas kernels  39.3 us (22%)
  waiting for transfers between devices  29.6 us (16%)
  starting transfers between devices  16.9 us (9%)
  local copies, waits for them, and re-layouts  9.81 us (5%)
    all_to_all x1, blocking collectives, per_device(): got = lax.all_to_all(sent, 'shard', 0, 0, tiled=True)  83.9 us
    ppermute x16, waiting for transfers between devices, send(): lax.ppermute(x, axis, [(i, target(i)) for i in range(lax.axis_size(axis))])  29.6 us
    ppermute x16, starting transfers between devices, send(): lax.ppermute(x, axis, [(i, target(i)) for i in range(lax.axis_size(axis))])  16.9 us
    pallas_call x4, Pallas kernels, gram(): pl.pallas_call(lambda *refs: gram_kernel(first, offset, rows, window, *re...  14.8 us
    pallas_call x2, Pallas kernels, newton(): pl.pallas_call(lambda *refs: newton_kernel(packed, *refs), in_specs=[pl.B...  11.3 us
    unnamed x10, local copies, waits for them, and re-layouts  9.51 us
    pallas_call x1, Pallas kernels, apply(): pl.pallas_call(lambda *refs: apply_kernel(count, *refs), in_specs=[pl.Blo...  7.23 us
    pallas_call x1, Pallas kernels, route(): pl.pallas_call(route_kernel, grid=(pairs,), in_specs=[pl.BlockSpec((1, SL...  3.75 us
  transfers between devices with their start and end apart: 16, of which 9 were waited for; matrix products, arithmetic and copies ran while one was open for 0% of the time, Pallas kernels for 14%

profile of v6, /device:TPU:24, one launch (start us, length us, event | category | flops | bytes accessed | tf_op | source)
XLA Modules:
  0.0 181.4 jit_solution(6265104171622844943)
XLA Ops:
  0.0 2.2 %copy-done.2 = bf16[256,8192]{1,0:T(8,128)(2,1)S(1)} copy-done((bf16[256,8192]{1,0:T(8,128)(2,1)S(1)}, bf16[256,8192]{1,0:T(8,128)(2,1)}, u32[]{:S(2)}) %copy-start.2) | copy-done | bytes 4194328
  4.5 3.7 %shard_map.46 = bf16[16,400,512]{2,1,0:T(8,128)(2,1)S(1)} custom-call(s32[1,256]{1,0:T(1,128)S(1)} %bitcast.37, bf16[256,4096]{1,0:T(8,128)(2,1)S(1)} %copy-done.3, bf16[256,8192]{1,0:T(8,128)(2,1)S(1)} %copy-done.2), custom_call_target="tpu_custom_call" | custom-call | flops 1048576 | bytes 4096 | tf_op jit(solution)/shard_map/pallas_call | solution.py:64
  8.2 83.9 %all_to_all.5.refs_2_ = bf16[16,400,512]{2,1,0:T(8,128)(2,1)} all-to-all(bf16[16,400,512]{2,1,0:T(8,128)(2,1)S(1)} %shard_map.46), channel_id=1, replica_groups=mesh['expert'=8,'shard'=16] {'shard'}, dimensions={0} | all-to-all | bytes 13107200 | tf_op jit(solution)/shard_map/all_to_all | solution.py:351
  93.2 2.9 %copy-done = bf16[16,400,512]{2,1,0:T(8,128)(2,1)S(1)} copy-done((bf16[16,400,512]{2,1,0:T(8,128)(2,1)S(1)}, bf16[16,400,512]{2,1,0:T(8,128)(2,1)}, u32[]{:S(2)}) %copy-start) | copy-done | bytes 6553624
  96.1 3.3 %shard_map.48 = f32[4,1296,128]{2,1,0:T(8,128)S(1)} custom-call(s32[16,8]{1,0:T(8,128)S(1)} %get-tuple-element.56.refs_0_, s32[16,8]{1,0:T(8,128)S(1)} %get-tuple-element.47.refs_1_, bf16[16,400,512]{2,1,0:T(8,128)(2,1)S(1)} %copy-done), custom_call_target="tpu_custom_call" | custom-call | flops 1048576 | bytes 4096 | tf_op jit(solution)/shard_map/pallas_call | solution.py:113
  99.5 4.0 %shard_map.50 = f32[4,1296,128]{2,1,0:T(8,128)S(1)} custom-call(s32[16,8]{1,0:T(8,128)S(1)} %copy.14.refs_0_, s32[16,8]{1,0:T(8,128)S(1)} %get-tuple-element.48.refs_1_, bf16[16,400,512]{2,1,0:T(8,128)(2,1)S(1)} %copy-done), custom_call_target="tpu_custom_call" | custom-call | flops 1048576 | bytes 4096 | tf_op jit(solution)/shard_map/pallas_call | solution.py:113
  104.1 3.3 %shard_map.47 = f32[4,1296,128]{2,1,0:T(8,128)S(1)} custom-call(s32[16,8]{1,0:T(8,128)S(1)} %get-tuple-element.56.refs_0_, s32[16,8]{1,0:T(8,128)S(1)} %get-tuple-element.47.refs_1_, bf16[16,400,512]{2,1,0:T(8,128)(2,1)S(1)} %copy-done), custom_call_target="tpu_custom_call" | custom-call | flops 1048576 | bytes 4096 | tf_op jit(solution)/shard_map/pallas_call | solution.py:113
  108.0 2.6 %collective-permute-start.2 = (bf16[1296,128]{1,0:T(8,128)(2,1)S(1)}, bf16[1296,128]{1,0:T(8,128)(2,1)S(1)}, u32[]{:S(2)}, u32[]{:S(2)}) collective-permute-start(bf16[1296,128]{1,0:T(8,128)(2,1)S(1)} %get-tuple-element.55), channel_id=1, source_target_pairs={{0,64},{16,80},{32,96},{48,112},{64,0},{80,16},{96,32},{112,48},{1... | collective-permute-start | bytes 995336 | tf_op jit(solution)/shard_map/ppermute | solution.py:325
  110.6 4.1 %shard_map.49 = f32[4,1296,128]{2,1,0:T(8,128)S(1)} custom-call(s32[16,8]{1,0:T(8,128)S(1)} %copy.14.refs_0_, s32[16,8]{1,0:T(8,128)S(1)} %get-tuple-element.48.refs_1_, bf16[16,400,512]{2,1,0:T(8,128)(2,1)S(1)} %copy-done), custom_call_target="tpu_custom_call" | custom-call | flops 1048576 | bytes 4096 | tf_op jit(solution)/shard_map/pallas_call | solution.py:113
  114.7 3.8 %collective-permute-done.1 = bf16[1296,128]{1,0:T(8,128)(2,1)S(1)} collective-permute-done((bf16[1296,128]{1,0:T(8,128)(2,1)S(1)}, bf16[1296,128]{1,0:T(8,128)(2,1)S(1)}, u32[]{:S(2)}, u32[]{:S(2)}) %collective-permute-start.1) | collective-permute-done | bytes 331808 | tf_op jit(solution)/shard_map/ppermute | solution.py:325
  118.4 1.8 collective-permute-done.2
  120.2 6.0 %collective-permute-done.3 = bf16[1296,128]{1,0:T(8,128)(2,1)S(1)} collective-permute-done((bf16[1296,128]{1,0:T(8,128)(2,1)S(1)}, bf16[1296,128]{1,0:T(8,128)(2,1)S(1)}, u32[]{:S(2)}, u32[]{:S(2)}) %collective-permute-start.3) | collective-permute-done | bytes 331808 | tf_op jit(solution)/shard_map/ppermute | solution.py:325
  127.3 1.8 %collective-permute-start.10 = (bf16[1296,128]{1,0:T(8,128)(2,1)S(1)}, bf16[1296,128]{1,0:T(8,128)(2,1)S(1)}, u32[]{:S(2)}, u32[]{:S(2)}) collective-permute-start(bf16[1296,128]{1,0:T(8,128)(2,1)S(1)} %get-tuple-element.50), channel_id=1, source_target_pairs={{0,64},{16,80},{32,96},{48,112},{64,0},{80,16},{96,32},{112,48},{1... | collective-permute-start | bytes 995336 | tf_op jit(solution)/shard_map/ppermute | solution.py:325
  129.3 3.0 %collective-permute-start.9 = (bf16[1296,128]{1,0:T(8,128)(2,1)S(1)}, bf16[1296,128]{1,0:T(8,128)(2,1)S(1)}, u32[]{:S(2)}, u32[]{:S(2)}) collective-permute-start(bf16[1296,128]{1,0:T(8,128)(2,1)S(1)} %get-tuple-element.51), channel_id=1, source_target_pairs={{0,32},{16,48},{32,64},{48,80},{64,96},{80,112},{96,0},{112,16},{1... | collective-permute-start | bytes 995336 | tf_op jit(solution)/shard_map/ppermute | solution.py:325
  132.4 3.8 %collective-permute-done.4.refs_1_ = bf16[1296,128]{1,0:T(8,128)(2,1)S(1)} collective-permute-done((bf16[1296,128]{1,0:T(8,128)(2,1)S(1)}, bf16[1296,128]{1,0:T(8,128)(2,1)S(1)}, u32[]{:S(2)}, u32[]{:S(2)}) %collective-permute-start.4) | collective-permute-done | bytes 331808 | tf_op jit(solution)/shard_map/ppermute | solution.py:325
  136.2 5.6 %shard_map.51.refs_1_ = bf16[1280,128]{1,0:T(8,128)(2,1)S(1)} custom-call(f32[1296,128]{1,0:T(8,128)S(1)} %get-tuple-element.46.refs_0_, bf16[1296,128]{1,0:T(8,128)(2,1)S(1)} %collective-permute-done.4.refs_1_), custom_call_target="tpu_custom_call" | custom-call | flops 1048576 | bytes 4096 | tf_op jit(solution)/shard_map/pallas_call | solution.py:217
  143.3 2.1 %collective-permute-done.11.refs_3_ = bf16[1296,128]{1,0:T(8,128)(2,1)S(1)} collective-permute-done((bf16[1296,128]{1,0:T(8,128)(2,1)S(1)}, bf16[1296,128]{1,0:T(8,128)(2,1)S(1)}, u32[]{:S(2)}, u32[]{:S(2)}) %collective-permute-start.11) | collective-permute-done | bytes 331808 | tf_op jit(solution)/shard_map/ppermute | solution.py:325
  145.5 6.6 %collective-permute-done.8.refs_2_ = bf16[1280,128]{1,0:T(8,128)(2,1)S(1)} collective-permute-done((bf16[1280,128]{1,0:T(8,128)(2,1)S(1)}, bf16[1280,128]{1,0:T(8,128)(2,1)S(1)}, u32[]{:S(2)}, u32[]{:S(2)}) %collective-permute-start.8) | collective-permute-done | bytes 327712 | tf_op jit(solution)/shard_map/ppermute | solution.py:325
  156.1 5.7 %shard_map.52.refs_8_ = bf16[512,512]{1,0:T(8,128)(2,1)S(1)} custom-call(f32[1296,128]{1,0:T(8,128)S(1)} %get-tuple-element.36.refs_0_, bf16[1296,128]{1,0:T(8,128)(2,1)S(1)} %collective-permute-done.9.refs_1_, bf16[1296,128]{1,0:T(8,128)(2,1)S(1)} %collective-permute-done.10.refs_2_, bf16[1296,128]{1,0:T(8,128)(2,1)S(1)} %collective-permute-done.11.refs_3_), custom_call_target="tpu_custom_call" | custom-call | flops 1048576 | bytes 4096 | tf_op jit(solution)/shard_map/pallas_call | solution.py:217
  162.7 2.1 %collective-permute-start.15 = (bf16[1280,128]{1,0:T(8,128)(2,1)S(1)}, bf16[1280,128]{1,0:T(8,128)(2,1)S(1)}, u32[]{:S(2)}, u32[]{:S(2)}) collective-permute-start(bf16[1280,128]{1,0:T(8,128)(2,1)S(1)} %collective-permute-done.14.refs_3_), channel_id=1, source_target_pairs={{0,12},{1,13},{2,14},{3,15},{4,0},{5,1},{6,2},{7,3},{8,4},{9,5},{1... | collective-permute-start | bytes 983048 | tf_op jit(solution)/shard_map/ppermute | solution.py:325
  164.9 2.2 %copy-done.1 = bf16[1,4096,512]{2,1,0:T(8,128)(2,1)S(1)} copy-done((bf16[1,4096,512]{2,1,0:T(8,128)(2,1)S(1)}, bf16[1,4096,512]{2,1,0:T(8,128)(2,1)}, u32[]{:S(2)}) %copy-start.1) | copy-done | bytes 4194328
  167.1 2.3 %shard_map.53.refs_6_ = bf16[3,512,512]{2,1,0:T(8,128)(2,1)S(1)} custom-call(s32[8]{0:T(128)S(1)} %stack.35.refs_0_, bf16[1280,128]{1,0:T(8,128)(2,1)S(1)} %shard_map.51.refs_1_, bf16[1280,128]{1,0:T(8,128)(2,1)S(1)} %collective-permute-done.8.refs_2_, bf16[1280,128]{1,0:T(8,128)(2,1)S(1)} %collective-permute-done.14.refs_3_, bf16[4096,512]{1,0:T(8,128)(2,1)S(1)} %bitcast.36), custom_call_target="tpu_custom_call" | custom-call | flops 1048576 | bytes 4096 | tf_op jit(solution)/shard_map/pallas_call | solution.py:257
  169.7 4.2 %collective-permute-done.15.refs_5_ = bf16[1280,128]{1,0:T(8,128)(2,1)S(1)} collective-permute-done((bf16[1280,128]{1,0:T(8,128)(2,1)S(1)}, bf16[1280,128]{1,0:T(8,128)(2,1)S(1)}, u32[]{:S(2)}, u32[]{:S(2)}) %collective-permute-start.15) | collective-permute-done | bytes 327712 | tf_op jit(solution)/shard_map/ppermute | solution.py:325
  174.0 7.2 %shard_map.54 = bf16[4096,512]{1,0:T(8,128)(2,1)} custom-call(s32[8]{0:T(128)S(1)} %stack.35.refs_0_, bf16[1280,128]{1,0:T(8,128)(2,1)S(1)} %collective-permute-done.6.refs_1_, bf16[1280,128]{1,0:T(8,128)(2,1)S(1)} %collective-permute-done.7.refs_2_, bf16[1280,128]{1,0:T(8,128)(2,1)S(1)} %collective-permute-done.12.refs_3_, ...), custom_call_target="tpu_custom_call" | custom-call | flops 1048576 | bytes 4096 | tf_op jit(solution)/shard_map/pallas_call | solution.py:307
  (40 shorter events, 12.8 us)
Async XLA Ops:
  0.0 2.2 %copy-start.2 = (bf16[256,8192]{1,0:T(8,128)(2,1)S(1)}, bf16[256,8192]{1,0:T(8,128)(2,1)}, u32[]{:S(2)}) copy-start(bf16[256,8192]{1,0:T(8,128)(2,1)} %grads_ref.1) | copy-start | bytes 12582916
  2.2 1.6 copy-start.3
  3.8 0.7 copy-start.4
  93.2 2.9 %copy-start = (bf16[16,400,512]{2,1,0:T(8,128)(2,1)S(1)}, bf16[16,400,512]{2,1,0:T(8,128)(2,1)}, u32[]{:S(2)}) copy-start(bf16[16,400,512]{2,1,0:T(8,128)(2,1)} %all_to_all.5.refs_2_) | copy-start | bytes 19660804
  99.4 8.1 %collective-permute-start = (f32[4,1296,128]{2,1,0:T(8,128)S(1)}, f32[4,1296,128]{2,1,0:T(8,128)S(1)}, u32[]{:S(2)}, u32[]{:S(2)}) collective-permute-start(f32[4,1296,128]{2,1,0:T(8,128)S(1)} %shard_map.48), channel_id=1, source_target_pairs={{0,16},{16,0},{32,48},{48,32},{64,80},{80,64},{96,112},{112,96},{1... | collective-permute-start | bytes 7962632 | tf_op jit(solution)/shard_map/ppermute | solution.py:325
  103.6 23.5 %collective-permute-start.5 = (f32[4,1296,128]{2,1,0:T(8,128)S(1)}, f32[4,1296,128]{2,1,0:T(8,128)S(1)}, u32[]{:S(2)}, u32[]{:S(2)}) collective-permute-start(f32[4,1296,128]{2,1,0:T(8,128)S(1)} %shard_map.50), channel_id=1, source_target_pairs={{0,16},{16,0},{32,48},{48,32},{64,80},{80,64},{96,112},{112,96},{1... | collective-permute-start | bytes 7962632 | tf_op jit(solution)/shard_map/ppermute | solution.py:325
  107.7 10.7 %collective-permute-start.1 = (bf16[1296,128]{1,0:T(8,128)(2,1)S(1)}, bf16[1296,128]{1,0:T(8,128)(2,1)S(1)}, u32[]{:S(2)}, u32[]{:S(2)}) collective-permute-start(bf16[1296,128]{1,0:T(8,128)(2,1)S(1)} %get-tuple-element.53), channel_id=1, source_target_pairs={{0,32},{16,48},{32,64},{48,80},{64,96},{80,112},{96,0},{112,16},{1... | collective-permute-start | bytes 995336 | tf_op jit(solution)/shard_map/ppermute | solution.py:325
  108.0 12.2 %collective-permute-start.2 = (bf16[1296,128]{1,0:T(8,128)(2,1)S(1)}, bf16[1296,128]{1,0:T(8,128)(2,1)S(1)}, u32[]{:S(2)}, u32[]{:S(2)}) collective-permute-start(bf16[1296,128]{1,0:T(8,128)(2,1)S(1)} %get-tuple-element.55), channel_id=1, source_target_pairs={{0,64},{16,80},{32,96},{48,112},{64,0},{80,16},{96,32},{112,48},{1... | collective-permute-start | bytes 995336 | tf_op jit(solution)/shard_map/ppermute | solution.py:325
  110.6 15.6 %collective-permute-start.3 = (bf16[1296,128]{1,0:T(8,128)(2,1)S(1)}, bf16[1296,128]{1,0:T(8,128)(2,1)S(1)}, u32[]{:S(2)}, u32[]{:S(2)}) collective-permute-start(bf16[1296,128]{1,0:T(8,128)(2,1)S(1)} %get-tuple-element.54), channel_id=1, source_target_pairs={{0,96},{16,112},{32,0},{48,16},{64,32},{80,48},{96,64},{112,80},{1... | collective-permute-start | bytes 995336 | tf_op jit(solution)/shard_map/ppermute | solution.py:325
  126.4 9.8 %collective-permute-start.4 = (bf16[1296,128]{1,0:T(8,128)(2,1)S(1)}, bf16[1296,128]{1,0:T(8,128)(2,1)S(1)}, u32[]{:S(2)}, u32[]{:S(2)}) collective-permute-start(bf16[1296,128]{1,0:T(8,128)(2,1)S(1)} %get-tuple-element.45), channel_id=1, source_target_pairs={{0,1},{1,0},{2,3},{3,2},{4,5},{5,4},{6,7},{7,6},{8,9},{9,8},{10,11... | collective-permute-start | bytes 995336 | tf_op jit(solution)/shard_map/ppermute | solution.py:325
  127.3 16.0 %collective-permute-start.10 = (bf16[1296,128]{1,0:T(8,128)(2,1)S(1)}, bf16[1296,128]{1,0:T(8,128)(2,1)S(1)}, u32[]{:S(2)}, u32[]{:S(2)}) collective-permute-start(bf16[1296,128]{1,0:T(8,128)(2,1)S(1)} %get-tuple-element.50), channel_id=1, source_target_pairs={{0,64},{16,80},{32,96},{48,112},{64,0},{80,16},{96,32},{112,48},{1... | collective-permute-start | bytes 995336 | tf_op jit(solution)/shard_map/ppermute | solution.py:325
  129.1 16.3 %collective-permute-start.11 = (bf16[1296,128]{1,0:T(8,128)(2,1)S(1)}, bf16[1296,128]{1,0:T(8,128)(2,1)S(1)}, u32[]{:S(2)}, u32[]{:S(2)}) collective-permute-start(bf16[1296,128]{1,0:T(8,128)(2,1)S(1)} %get-tuple-element.49), channel_id=1, source_target_pairs={{0,96},{16,112},{32,0},{48,16},{64,32},{80,48},{96,64},{112,80},{1... | collective-permute-start | bytes 995336 | tf_op jit(solution)/shard_map/ppermute | solution.py:325
  129.3 16.1 %collective-permute-start.9 = (bf16[1296,128]{1,0:T(8,128)(2,1)S(1)}, bf16[1296,128]{1,0:T(8,128)(2,1)S(1)}, u32[]{:S(2)}, u32[]{:S(2)}) collective-permute-start(bf16[1296,128]{1,0:T(8,128)(2,1)S(1)} %get-tuple-element.51), channel_id=1, source_target_pairs={{0,32},{16,48},{32,64},{48,80},{64,96},{80,112},{96,0},{112,16},{1... | collective-permute-start | bytes 995336 | tf_op jit(solution)/shard_map/ppermute | solution.py:325
  141.8 10.3 %collective-permute-start.8 = (bf16[1280,128]{1,0:T(8,128)(2,1)S(1)}, bf16[1280,128]{1,0:T(8,128)(2,1)S(1)}, u32[]{:S(2)}, u32[]{:S(2)}) collective-permute-start(bf16[1280,128]{1,0:T(8,128)(2,1)S(1)} %shard_map.51.refs_1_), channel_id=1, source_target_pairs={{0,3},{1,2},{2,1},{3,0},{4,7},{5,6},{6,5},{7,4},{8,11},{9,10},{10,... | collective-permute-start | bytes 983048 | tf_op jit(solution)/shard_map/ppermute | solution.py:325
  142.8 12.1 %collective-permute-start.6 = (bf16[1280,128]{1,0:T(8,128)(2,1)S(1)}, bf16[1280,128]{1,0:T(8,128)(2,1)S(1)}, u32[]{:S(2)}, u32[]{:S(2)}) collective-permute-start(bf16[1280,128]{1,0:T(8,128)(2,1)S(1)} %shard_map.51.refs_1_), channel_id=1, source_target_pairs={{0,4},{1,5},{2,6},{3,7},{4,8},{5,9},{6,10},{7,11},{8,12},{9,13},{1... | collective-permute-start | bytes 983048 | tf_op jit(solution)/shard_map/ppermute | solution.py:325
  152.1 10.6 %collective-permute-start.14 = (bf16[1280,128]{1,0:T(8,128)(2,1)S(1)}, bf16[1280,128]{1,0:T(8,128)(2,1)S(1)}, u32[]{:S(2)}, u32[]{:S(2)}) collective-permute-start(bf16[1280,128]{1,0:T(8,128)(2,1)S(1)} %collective-permute-done.8.refs_2_), channel_id=1, source_target_pairs={{0,12},{1,13},{2,14},{3,15},{4,0},{5,1},{6,2},{7,3},{8,4},{9,5},{1... | collective-permute-start | bytes 983048 | tf_op jit(solution)/shard_map/ppermute | solution.py:325
  152.9 16.8 %collective-permute-start.7 = (bf16[1280,128]{1,0:T(8,128)(2,1)S(1)}, bf16[1280,128]{1,0:T(8,128)(2,1)S(1)}, u32[]{:S(2)}, u32[]{:S(2)}) collective-permute-start(bf16[1280,128]{1,0:T(8,128)(2,1)S(1)} %shard_map.51.refs_1_), channel_id=1, source_target_pairs={{0,12},{1,13},{2,14},{3,15},{4,0},{5,1},{6,2},{7,3},{8,4},{9,5},{1... | collective-permute-start | bytes 983048 | tf_op jit(solution)/shard_map/ppermute | solution.py:325
  153.5 16.3 %collective-permute-start.12 = (bf16[1280,128]{1,0:T(8,128)(2,1)S(1)}, bf16[1280,128]{1,0:T(8,128)(2,1)S(1)}, u32[]{:S(2)}, u32[]{:S(2)}) collective-permute-start(bf16[1280,128]{1,0:T(8,128)(2,1)S(1)} %collective-permute-done.8.refs_2_), channel_id=1, source_target_pairs={{0,4},{1,5},{2,6},{3,7},{4,8},{5,9},{6,10},{7,11},{8,12},{9,13},{1... | collective-permute-start | bytes 983048 | tf_op jit(solution)/shard_map/ppermute | solution.py:325
  155.0 14.8 %collective-permute-start.13 = (bf16[1280,128]{1,0:T(8,128)(2,1)S(1)}, bf16[1280,128]{1,0:T(8,128)(2,1)S(1)}, u32[]{:S(2)}, u32[]{:S(2)}) collective-permute-start(bf16[1280,128]{1,0:T(8,128)(2,1)S(1)} %collective-permute-done.6.refs_1_), channel_id=1, source_target_pairs={{0,4},{1,5},{2,6},{3,7},{4,8},{5,9},{6,10},{7,11},{8,12},{9,13},{1... | collective-permute-start | bytes 983048 | tf_op jit(solution)/shard_map/ppermute | solution.py:325
  162.7 11.3 %collective-permute-start.15 = (bf16[1280,128]{1,0:T(8,128)(2,1)S(1)}, bf16[1280,128]{1,0:T(8,128)(2,1)S(1)}, u32[]{:S(2)}, u32[]{:S(2)}) collective-permute-start(bf16[1280,128]{1,0:T(8,128)(2,1)S(1)} %collective-permute-done.14.refs_3_), channel_id=1, source_target_pairs={{0,12},{1,13},{2,14},{3,15},{4,0},{5,1},{6,2},{7,3},{8,4},{9,5},{1... | collective-permute-start | bytes 983048 | tf_op jit(solution)/shard_map/ppermute | solution.py:325
  164.9 2.2 %copy-start.1 = (bf16[1,4096,512]{2,1,0:T(8,128)(2,1)S(1)}, bf16[1,4096,512]{2,1,0:T(8,128)(2,1)}, u32[]{:S(2)}) copy-start(bf16[1,4096,512]{2,1,0:T(8,128)(2,1)} %param.7) | copy-start | bytes 12582916
